TPU v7x, 32 devices: a whole 2x2x4 slice. The times are simulated.
32 devices in a mesh: dp: 2 (over core), modes: 16 (over z, y, x).
Axes of the slice: x: 2, y: 2, z: 4, core: 2. Of those that a mesh axis runs over, the one named last changes fastest.
Arguments:
- x_in: bfloat16 [32768, 512], P(('dp', 'modes')), may hold values from -6 to 6
- cotangent: bfloat16 [32768, 512], P(('dp', 'modes')), may hold values from -6 to 6
- block_grid: int32 [512], P(('dp', 'modes')), may hold values from 8 to 32, as said below
- keep_modes: int32 [3], replicated, may hold values from 6 to 32, as said below
- norm1_gain: float32 [2, 512], replicated, may hold values from 0.5 to 1.5
- norm1_bias: float32 [2, 512], replicated, may hold values from -1.8 to 1.8
- mix_w1: bfloat16 [2, 2, 8, 64, 64], replicated, may hold values from -0.5 to 0.5
- mix_b1: float32 [2, 2, 512], replicated, may hold values from -3 to 3
- mix_w2: bfloat16 [2, 2, 8, 64, 64], replicated, may hold values from -0.5 to 0.5
- mix_b2: float32 [2, 2, 512], replicated, may hold values from -1.8 to 1.8
- norm2_gain: float32 [2, 512], replicated, may hold values from 0.5 to 1.5
- norm2_bias: float32 [2, 512], replicated, may hold values from -1.8 to 1.8
- fc1: bfloat16 [2, 512, 512], replicated, may hold values from -0.25 to 0.25
- fc1_bias: float32 [2, 512], replicated, may hold values from -1.8 to 1.8
- fc2: bfloat16 [2, 512, 512], replicated, may hold values from -0.375 to 0.375
- fc2_bias: float32 [2, 512], replicated, may hold values from -1.8 to 1.8
Outputs:
- out: bfloat16 [32768, 512], P(('dp', 'modes'))
- x_grad: bfloat16 [32768, 512], P(('dp', 'modes'))
- norm1_gain_grad: float32 [2, 512], replicated
- norm1_bias_grad: float32 [2, 512], replicated
- mix_w1_grad: float32 [2, 2, 8, 64, 64], replicated
- mix_b1_grad: float32 [2, 2, 512], replicated
- mix_w2_grad: float32 [2, 2, 8, 64, 64], replicated
- mix_b2_grad: float32 [2, 2, 512], replicated
- norm2_gain_grad: float32 [2, 512], replicated
- norm2_bias_grad: float32 [2, 512], replicated
- fc1_grad: float32 [2, 512, 512], replicated
- fc1_bias_grad: float32 [2, 512], replicated
- fc2_grad: float32 [2, 512, 512], replicated
- fc2_bias_grad: float32 [2, 512], replicated
Inputs may be any that keep to these rules, and one draw needn't show every extreme that they name: `block_grid`: each slab's 16 entries are all 32, or four quarters of 4 entries, each quarter all 16 or all 8; some slab is all 32 and some quarter is all 8. `keep_modes`: entry 0 is 8 minus a quarter of it (rounded down), entry 2 is 32, entry 1 lies between 16 minus a quarter of it (rounded down) and 16.
All inputs are finite; a program needn't handle non-finite values.
Results may differ from a plain program's by a relative error of at most 0.019.
Values may be sent and summed in bfloat16 or wider, within the bound.
No kernel may reach another device: no remote copies, remote signals or barrier semaphores. Data moves between devices by JAX's collectives and lax.ppermute only.
A program may use at most 192 MiB of HBM per device.

v0:
```python
import math
from functools import partial

import jax
import jax.numpy as jnp
from jax import lax
from jax.experimental import pallas as pl
from jax.experimental.pallas import tpu as pltpu
from jax.sharding import PartitionSpec as P

LAYERS = 2
NBLK = 16
F32 = jnp.float32
BF = jnp.bfloat16
C0 = math.sqrt(2.0 / math.pi)
C1 = 0.044715 * C0
PER = 1344
RT = 256
ST = 256
NH = 512
CH = 64
CE = 32
CF = 16


def nn(a, b):
    return jnp.dot(a, b, preferred_element_type=F32)


def nt(a, b):
    return lax.dot_general(a, b, (((1,), (1,)), ((), ())), preferred_element_type=F32)


def tn(a, b):
    return lax.dot_general(a, b, (((0,), (0,)), ((), ())), preferred_element_type=F32)


def gelu_pair(x):
    x2 = x * x
    p = 0.5 + 0.5 * jnp.tanh(x * (C0 + C1 * x2))
    y = x * p
    return y, p + y * (1.0 - p) * (2.0 * C0 + (6.0 * C1) * x2)


def gelu_split(x):
    p = 0.5 + 0.5 * jnp.tanh(x * (C0 + C1 * (x * x)))
    y = (x * p).astype(BF)
    xb, pb, qb = x.astype(BF), p.astype(BF), (1.0 - p).astype(BF)
    return y, pb + y * qb * (2.0 * C0 + (6.0 * C1) * (xb * xb))


def cos_of(t):
    x = t - 0.5
    w = (2.0 * math.pi * x) ** 2
    c = jnp.full_like(w, 1.0 / math.factorial(16))
    for k in range(7, -1, -1):
        c = c * w + (-1.0) ** k / math.factorial(2 * k)
    return -c


def cos_sin(t):
    x = t - 0.5
    w = (2.0 * math.pi * x) ** 2
    c = jnp.full_like(w, 1.0 / math.factorial(16))
    s = jnp.full_like(w, -1.0 / math.factorial(15))
    for k in range(7, -1, -1):
        c = c * w + (-1.0) ** k / math.factorial(2 * k)
        if k < 7:
            s = s * w + (-1.0) ** k / math.factorial(2 * k + 1)
    return -c, -s * (2.0 * math.pi * x)


def pick(values, block):
    out = jnp.zeros(block.shape, jnp.int32)
    for j in range(NBLK):
        out = jnp.where(block == j, values[j], out)
    return out


def log_of(grid):
    return jnp.where(grid == 8, 3, jnp.where(grid == 16, 4, 5))


def slot_of(slot, grid):
    half = grid * grid // 2
    local = slot & (half - 1)
    pp = lax.shift_right_logical(local, log_of(grid))
    qq = local & (grid - 1)
    mid = lax.shift_right_logical(grid, 1)
    first = pp == 0
    special = first & ((qq == 0) | (qq == mid))
    p = jnp.where(first & (qq >= mid), mid, pp)
    q = jnp.where(first & (qq == mid), 0, qq)
    pm = jnp.where(special, p, (grid - p) & (grid - 1))
    qm = jnp.where(special, mid, (grid - q) & (grid - 1))
    return 2 * (slot - local), p, q, special, pm, qm


def build_tables(grid_ref, keep_ref, at, k1, k2, k3, nm, nb):
    rows = at.shape[1]
    slots = rows // 2
    unit = slots // NBLK
    vals = [grid_ref[j] for j in range(NBLK)]
    lane = lax.broadcasted_iota(jnp.int32, (8, rows), 1)
    sub = lax.broadcasted_iota(jnp.int32, (8, rows), 0)
    gc = pick(vals, lane // (2 * unit))
    span = gc * gc
    start_c = lane & ~(span - 1)
    local = lane & (span - 1)
    p_c = lax.shift_right_logical(local, log_of(gc))
    q_c = local & (gc - 1)
    ginv = 1.0 / gc.astype(F32)
    bcs = []
    for j in range(4):
        q_r = (sub + 8 * j) & (gc - 1)
        bcs.append(cos_sin(((q_r * q_c) & (gc - 1)).astype(F32) * ginv))

    def two(x):
        return jnp.concatenate([x, x], 0)

    gc2, start2, p2, q2, ginv2, sub2 = two(gc), two(start_c), two(p_c), two(q_c), two(ginv), lax.broadcasted_iota(jnp.int32, (16, rows), 0)

    def step(i, carry):
        slot = (sub + 8 * i) * 8
        gb = jnp.where(sub < 4, grid_ref[2 * i], grid_ref[2 * i + 1])
        half = gb * gb // 2
        loc = slot & (half - 1)
        p_b = lax.shift_right_logical(loc, log_of(gb))
        ac, as_ = cos_sin(((p_b * p_c) & (gc - 1)).astype(F32) * ginv)
        same = jnp.where(2 * (slot - loc) == start_c, ginv, 0.0)
        ac = ac * same
        as_ = as_ * same
        for j in range(0, 8, 2):
            re, im = [], []
            for d in range(2):
                bc, bs = bcs[(j + d) % 4]
                a1 = ac[j + d : j + d + 1, :]
                a2 = as_[j + d : j + d + 1, :]
                re.append(a1 * bc - a2 * bs)
                im.append(-(a2 * bc + a1 * bs))
            s0 = pl.multiple_of(i * 64 + j * 8, 16)
            at[pl.ds(s0, 16), :] = jnp.concatenate(re, 0).astype(BF)
            at[pl.ds(slots + s0, 16), :] = jnp.concatenate(im, 0).astype(BF)
            g = grid_ref[2 * i + j // 4]
            first = (s0 & (g * g // 2 - 1)) < g

            @pl.when(first)
            def _():
                gv = jnp.full((16, rows), 0, jnp.int32) + g
                start, p, q, special, pm, qm = slot_of(sub2 + s0, gv)
                live = jnp.where(start == start2, ginv2, 0.0)
                t = ((p * p2 + q * q2) & (gc2 - 1)).astype(F32) * ginv2
                tm = ((pm * p2 + qm * q2) & (gc2 - 1)).astype(F32) * ginv2
                quarter = jnp.where(t >= 0.75, t - 0.75, t + 0.25)
                at[pl.ds(s0, 16), :] = (cos_of(t) * live).astype(BF)
                at[pl.ds(slots + s0, 16), :] = (cos_of(jnp.where(special, tm, quarter)) * live).astype(BF)

        return carry

    lax.fori_loop(0, slots // 64, step, 0)

    def mask(i, carry):
        slot = lax.broadcasted_iota(jnp.int32, (unit, 128), 0) + unit * i
        g = jnp.full((unit, 128), 0, jnp.int32) + grid_ref[i]
        _, p, q, special, pm, qm = slot_of(slot, g)
        k = jnp.where(g == 8, keep_ref[0], jnp.where(g == 16, keep_ref[1], keep_ref[2]))
        plus = jnp.where((p < k) & (q < k), 1.0, 0.0)
        minus = jnp.where((pm < k) & (qm < k), 1.0, 0.0)
        n = jnp.where(special, 0.0, 1.0)
        dst = pl.ds(pl.multiple_of(i * unit, unit), unit)
        nm[dst, :] = n.astype(BF)
        nb[dst, :] = (1.0 - n).astype(BF)
        for sign, (m, im) in enumerate(((plus, plus * n), (minus, -minus * n))):
            for ref, f in ((k1, 1.0), (k2, 0.05), (k3, 0.05 * 0.0025)):
                ref[sign, dst, 0:128] = (m * f).astype(BF)
                ref[sign, dst, 128:256] = (im * f).astype(BF)
        return carry

    lax.fori_loop(0, NBLK, mask, 0)


def build_mix(w_ref, out_ref):
    i = lax.broadcasted_iota(jnp.int32, (64, 128), 0)
    j = lax.broadcasted_iota(jnp.int32, (64, 128), 1)
    dup = jnp.where((j & 63) == i, 1.0, 0.0).astype(BF)
    r = lax.broadcasted_iota(jnp.int32, (512, 128), 0)
    c = lax.broadcasted_iota(jnp.int32, (512, 128), 1)
    diag = ((r // 64) & 1) == (c // 64)
    for layer in range(LAYERS):
        re = jnp.where(diag, nn(w_ref[layer, 0], dup), 0.0)
        im = jnp.where(diag, nn(w_ref[layer, 1], dup), 0.0)
        for g in range(4):
            a = re[g * 128 : (g + 1) * 128].astype(BF)
            b = im[g * 128 : (g + 1) * 128]
            out_ref[layer, g, 0:128, 0:128] = a
            out_ref[layer, g, 128:256, 128:256] = a
            out_ref[layer, g, 0:128, 128:256] = b.astype(BF)
            out_ref[layer, g, 128:256, 0:128] = (-b).astype(BF)


def min_layer(layer):
    return layer if isinstance(layer, int) else jnp.minimum(layer, LAYERS - 1)


def fold(x):
    return jnp.sum(x.reshape(x.shape[0] // 8, 8, x.shape[1]), 0)


def kernel(
    grid_ref, keep_ref, core_ref, x_hbm, cot_hbm,
    n1g, n1b, w1_hbm, b1, w2_hbm, b2, n2g, n2b, fc1_hbm, fb1, fc2_hbm, fb2,
    out_hbm, xg_hbm, mine_hbm, other_hbm,
    x_ref, cot_ref, w1, w2, fc1, fc2, out_ref, xg_ref, grads_ref, sems,
    at, st, k1, k2, k3, nm, nb, w1g, w2g,
    xh1, rs1, hu, ul, z, o, da, ds, pq, xh2, rs2, v, act, dp,
    gm, gmid, acc,
):
    g_s, gy = hu, ul

    def copy(k, src, dst):
        return pltpu.make_async_copy(src, dst, sems.at[k])

    loads = [
        copy(k, src, dst)
        for k, (src, dst) in enumerate(
            ((x_hbm, x_ref), (w1_hbm, w1), (w2_hbm, w2), (fc1_hbm, fc1), (fc2_hbm, fc2), (cot_hbm, cot_ref))
        )
    ]
    for c in loads:
        c.start()
    rows = x_ref.shape[0]
    slots = rows // 2
    tiles = rows // RT
    stiles = slots // ST
    build_tables(grid_ref, keep_ref, at, k1, k2, k3, nm, nb)
    for i in range(4):
        st[:, i * 256 : (i + 1) * 256] = at[i * 256 : (i + 1) * 256, :].T
    loads[1].wait()
    loads[2].wait()
    build_mix(w1, w1g)
    build_mix(w2, w2g)
    acc[...] = jnp.zeros_like(acc)

    def tile(i):
        return slice(i * RT, (i + 1) * RT)

    def chunk(i, j):
        return slice(i * RT + j * CH, i * RT + (j + 1) * CH)

    def add_to(layer, k, x):
        acc[layer, k] = acc[layer, k] + fold(x)

    def norm1(layer, dst, h):
        mean = jnp.mean(h, -1, keepdims=True)
        cent = h - mean
        rstd = lax.rsqrt(jnp.mean(cent * cent, -1, keepdims=True) + 1e-05)
        xh = cent * rstd
        u = xh * n1g[pl.ds(min_layer(layer), 1), :] + n1b[pl.ds(min_layer(layer), 1), :]
        xh1[layer, dst, :] = xh.astype(BF)
        rs1[layer, dst, :] = jnp.broadcast_to(rstd, (CH, 128))
        ul[dst, :] = u.astype(BF)
        hu[dst, :] = h + u

    def enter():
        for i in range(tiles):
            for j in range(RT // CH):
                dst = chunk(i, j)
                norm1(0, dst, x_ref[dst, :].astype(F32))

    def block(f):
        pl.when(grid_ref[0] > 0)(f)

    loads[0].wait()
    enter()
    loads[3].wait()
    loads[4].wait()
    loads[5].wait()

    def lanes(x, times):
        return jnp.concatenate([x] * times, 1)

    def analyse(layer, t, p):
        sl = slice(t * ST, (t + 1) * ST)
        h = p % 2
        hs = slice(h * 256, (h + 1) * 256)
        if p < 2:
            zr = nn(at[sl, :], ul[:, hs]).astype(BF)
            for e in range(2):
                c0 = (2 * h + e) * 256
                z[layer, 0, sl, c0 : c0 + 128] = zr[:, e * 128 : e * 128 + 128]
        else:
            n, nbar = nm[sl, :], nb[sl, :]
            zi = nn(at[slots + t * ST : slots + (t + 1) * ST, :], ul[:, hs]).astype(BF)
            for e in range(2):
                c0 = (2 * h + e) * 256
                zie = zi[:, e * 128 : e * 128 + 128]
                zin = zie * n
                z[layer, 0, sl, c0 + 128 : c0 + 256] = zin
                z[layer, 1, sl, c0 + 128 : c0 + 256] = -zin
                z[layer, 1, sl, c0 : c0 + 128] = z[layer, 0, sl, c0 : c0 + 128] * n + zie * nbar

    def both(ref, layer, sl, gl):
        return ref[layer, :, sl, gl].reshape(2 * ST, 256)

    def put(ref, layer, sl, gl, x, c=None):
        if c is None:
            ref[layer, :, sl, gl] = x.reshape(2, ST, 256)
        else:
            r0 = sl.start + c % ST
            ref[layer, c // ST, r0 : r0 + CE, gl] = x

    def combine(dst, sl, cs, x, signed):
        n, nbar = nm[sl, :], nb[sl, :]
        rp, ip = x[0:ST, 0:128], x[0:ST, 128:256]
        rm, im = x[ST : 2 * ST, 0:128], x[ST : 2 * ST, 128:256]
        dst[sl, cs] = rp + rm * n
        q = ip + im if signed else (ip - im) * n
        dst[slots + sl.start : slots + sl.stop, cs] = q + rm * nbar

    def mix_forward(layer):
        def cut(k):
            t, g = k // 4, k % 4
            return slice(t * ST, (t + 1) * ST), slice(g * 128, (g + 1) * 128), slice(g * 256, (g + 1) * 256), g

        def dot_a(k):
            sl, cs, gl, g = cut(k)
            return nn(both(z, layer, sl, gl), w1g[layer, g])

        def gelu_a(k, a):
            sl, cs, gl, g = cut(k)
            bias = lanes2(b1[layer, 0:1, cs], b1[layer, 1:2, cs])
            ys = []
            for c in range(0, 2 * ST, CE):
                og, dag = gelu_split(a[c : c + CE] + bias)
                ys.append(og)
                put(o, layer, sl, gl, og, c)
                put(da, layer, sl, gl, dag, c)
            return nn(jnp.concatenate(ys, 0), w2g[layer, g])

        def shrink_e(k, ew):
            sl, cs, gl, g = cut(k)
            bias = lanes2(b2[layer, 0:1, cs], b2[layer, 1:2, cs])
            for c in range(0, ST, CE):
                rs = slice(sl.start + c, sl.start + c + CE)
                ss = []
                for sign in range(2):
                    e = ew[sign * ST + c : sign * ST + c + CE] + bias
                    r = lax.rsqrt(e * e + 0.0025)
                    c1 = k1[sign, rs, :]
                    ss.append((e - 0.05 * (e * r)).astype(BF) * c1)
                    r = r.astype(BF)
                    ds[layer, sign, rs, gl] = c1 - k3[sign, rs, :] * (r * r * r)
                n, nbar = nm[rs, :], nb[rs, :]
                rm = ss[1][:, 0:128]
                pq[rs, cs] = ss[0][:, 0:128] + rm * n
                pq[slots + rs.start : slots + rs.stop, cs] = ss[0][:, 128:256] + ss[1][:, 128:256] + rm * nbar

        steps = stiles * 4
        for p in range(4):
            analyse(layer, 0, p)
        a = dot_a(0)
        e_prev = None
        for k in range(steps):
            t, g = k // 4, k % 4
            if t + 1 < stiles:
                analyse(layer, t + 1, g)
            nxt = dot_a(k + 1) if k + 1 < steps else None
            e = gelu_a(k, a)
            if e_prev is not None:
                shrink_e(k - 1, e_prev)
            a, e_prev = nxt, e
        shrink_e(steps - 1, e_prev)

    def ff_forward(layer):
        def norm2(i, y):
            for j in range(RT // CH):
                cd = chunk(i, j)
                mid = y[j * CH : (j + 1) * CH] + hu[cd, :]
                mean = jnp.mean(mid, -1, keepdims=True)
                cent = mid - mean
                rstd = lax.rsqrt(jnp.mean(cent * cent, -1, keepdims=True) + 1e-05)
                xh = cent * rstd
                xh2[layer, cd, :] = xh.astype(BF)
                rs2[layer, cd, :] = jnp.broadcast_to(rstd, (CH, 128))
                v[layer, cd, :] = (xh * n2g[pl.ds(layer, 1), :] + n2b[pl.ds(layer, 1), :]).astype(BF)
                hu[cd, :] = mid
            return nn(v[layer, tile(i), :], fc1[layer])

        def gelu_f(i, pre):
            for j in range(0, RT, CF):
                cd = slice(i * RT + j, i * RT + j + CF)
                act[layer, cd, :], dp[layer, cd, :] = gelu_split(pre[j : j + CF] + fb1[pl.ds(layer, 1), :])
            return nn(act[layer, tile(i), :], fc2[layer])

        def leave(i, br):
            for j in range(RT // CH):
                cd = chunk(i, j)
                h = hu[cd, :] + (br[j * CH : (j + 1) * CH] + fb2[pl.ds(layer, 1), :])
                out_ref[cd, :] = h.astype(BF)
                norm1(layer + 1, cd, h)

        def dot_y(i):
            return nn(st[tile(i), :], pq[...])

        y = dot_y(0)
        pre = None
        for i in range(tiles + 1):
            nxt = dot_y(i + 1) if i + 1 < tiles else None
            br = gelu_f(i - 1, pre) if i >= 1 else None
            pre = norm2(i, y) if i < tiles else None
            if i >= 1:
                leave(i - 1, br)
            y = nxt

    @partial(lax.fori_loop, 0, LAYERS, init_val=0)
    def _(layer, carry):
        block(lambda: mix_forward(layer))
        block(lambda: ff_forward(layer))
        return carry

    out_copy = copy(6, out_ref, out_hbm)
    out_copy.start()
    for i in range(tiles):
        g_s[tile(i), :] = cot_ref[tile(i), :].astype(F32)

    def norm_back(gv, xh, rstd, gain):
        t = gv * gain
        mt = jnp.mean(t, -1, keepdims=True)
        mx = jnp.mean(t * xh, -1, keepdims=True)
        return rstd * (t - mt - xh * mx)

    def with_sums(left, right):
        ones = jnp.ones((16, left.shape[0]), BF)
        return nn(jnp.concatenate([left.T, ones], 0), right)

    def ff_backward(layer):
        def load_g(rs):
            return g_s[rs, :]

        def dot_a(i):
            dst = tile(i)
            gmt = g_s[dst, :].astype(BF)
            gm[dst, :] = gmt
            return nt(gmt, fc2[layer])

        def mul(i, ga_):
            dst = tile(i)
            dp[layer, dst, :] = ga_.astype(BF) * dp[layer, dst, :]
            return nt(dp[layer, dst, :], fc1[layer])

        def leave(i, gv):
            for j in range(RT // CH):
                cd = chunk(i, j)
                gvc = gv[j * CH : (j + 1) * CH]
                xh = xh2[layer, cd, :].astype(F32)
                add_to(layer, 6, gvc * xh)
                add_to(layer, 7, gvc)
                rstd = lanes(rs2[layer, cd, :], 4)
                gmc = load_g(cd) + norm_back(gvc, xh, rstd, n2g[pl.ds(layer, 1), :])
                gmid[cd, :] = gmc
                gy[cd, :] = gmc.astype(BF)

        cur = dot_a(0)
        prev = None
        for i in range(tiles + 1):
            nxt = dot_a(i + 1) if i + 1 < tiles else None
            gv = mul(i, cur) if i < tiles else None
            if i >= 1:
                leave(i - 1, prev)
            cur, prev = nxt, gv
        base = pl.multiple_of((layer ^ core_ref[0]) * PER, PER)
        for left, right, off, vec in ((v, dp[layer], 0, 8), (act, gm[...], 512, 9)):
            for h in range(2):
                hs = slice(h * 256, (h + 1) * 256)
                r = base + off + h * 256
                if h == 0:
                    p = with_sums(left[layer, :, hs], right)
                    acc[layer, vec, 0:1, :] = p[256:257]
                else:
                    p = tn(left[layer, :, hs], right)
                grads_ref[pl.ds(r, 256), :] = p[0:256].astype(BF)

    def mix_backward(layer):
        def cut(k):
            t, g = k // 4, k % 4
            return slice(t * ST, (t + 1) * ST), slice(g * 128, (g + 1) * 128), slice(g * 256, (g + 1) * 256), g

        def spectrum(t, h):
            hs = slice(h * 256, (h + 1) * 256)
            gr = nn(at[t * ST : (t + 1) * ST, :], gy[:, hs]).astype(BF)
            gi = nn(at[slots + t * ST : slots + (t + 1) * ST, :], gy[:, hs]).astype(BF)
            return gr, gi

        def dot_o(k, gr, gi):
            sl, cs, gl, g = cut(k)
            n, nbar = nm[sl, :], nb[sl, :]
            hs = slice(g % 2 * 128, g % 2 * 128 + 128)
            grc, gic = gr[:, hs], gi[:, hs]
            ds[layer, 0, sl, gl] = lanes2(grc, gic) * ds[layer, 0, sl, gl]
            ds[layer, 1, sl, gl] = lanes2(grc * n + gic * nbar, gic) * ds[layer, 1, sl, gl]
            return nt(both(ds, layer, sl, gl), w2g[layer, g])

        def dot_z(k, go):
            sl, cs, gl, g = cut(k)
            put(da, layer, sl, gl, go.astype(BF) * both(da, layer, sl, gl))
            return nt(both(da, layer, sl, gl), w1g[layer, g])

        def leave(k, gz):
            sl, cs, gl, g = cut(k)
            combine(pq, sl, cs, gz.astype(BF), False)

        steps = stiles * 4
        sp = {0: spectrum(0, 0)}
        go = dot_o(0, *sp[0])
        prev = None
        for k in range(steps + 1):
            if k % 2 == 0 and k + 2 < steps:
                sp[k // 2 + 1] = spectrum((k + 2) // 4, (k + 2) // 2 % 2)
            nxt = dot_o(k + 1, *sp[(k + 1) // 2]) if k + 1 < steps else None
            gz = dot_z(k, go) if k < steps else None
            if k >= 1:
                leave(k - 1, prev)
            go, prev = nxt, gz
        base = pl.multiple_of((layer ^ core_ref[0]) * PER, PER) + 1024
        low = lax.broadcasted_iota(jnp.int32, (64, 128), 1) < 64
        for left, right, off, vec in ((o, ds, base + 128, 4), (z, da, base, 2)):
            for g in range(4):
                cs = slice(g * 128, (g + 1) * 128)
                gl = slice(g * 256, (g + 1) * 256)
                lf = left[layer, :, :, gl].reshape(rows, 256)
                rt = right[layer, :, :, gl].reshape(rows, 256)
                p = with_sums(lf, rt)
                acc[layer, vec, 0:1, cs] = p[256:257, 0:128]
                acc[layer, vec + 1, 0:1, cs] = p[256:257, 128:256]
                re = p[0:128, 0:128] + p[128:256, 128:256]
                im = p[0:128, 128:256] - p[128:256, 0:128]
                grads_ref[pl.ds(off, 64), cs] = jnp.where(low, re[0:64], re[64:128]).astype(BF)
                grads_ref[pl.ds(off + 64, 64), cs] = jnp.where(low, im[0:64], im[64:128]).astype(BF)

    def in_backward(layer):
        def leave(i, y):
            for j in range(RT // CH):
                cd = chunk(i, j)
                gmc = gmid[cd, :]
                gu = y[j * CH : (j + 1) * CH] + gmc
                xh = xh1[layer, cd, :].astype(F32)
                add_to(layer, 0, gu * xh)
                add_to(layer, 1, gu)
                rstd = lanes(rs1[layer, cd, :], 4)
                gh = gmc + norm_back(gu, xh, rstd, n1g[pl.ds(min_layer(layer), 1), :])
                xg_ref[cd, :] = gh.astype(BF)
                g_s[cd, :] = gh

        y = nn(st[tile(0), :], pq[...])
        for i in range(tiles):
            nxt = nn(st[tile(i + 1), :], pq[...]) if i + 1 < tiles else None
            leave(i, y)
            y = nxt

    @partial(lax.fori_loop, 0, LAYERS, init_val=0)
    def _(step, carry):
        layer = LAYERS - 1 - step
        block(lambda: ff_backward(layer))
        block(lambda: mix_backward(layer))
        block(lambda: in_backward(layer))
        return carry

    for layer in range(LAYERS):
        t = jnp.sum(acc[layer], 1)
        t = jnp.concatenate([t, jnp.zeros((PER - 1290, 512), F32)], 0)
        grads_ref[pl.ds(pl.multiple_of((layer ^ core_ref[0]) * PER, PER) + 1280, PER - 1280), :] = t.astype(BF)
    stores = [copy(7, xg_ref, xg_hbm), copy(8, grads_ref.at[pl.ds(PER, PER)], other_hbm), copy(9, grads_ref.at[pl.ds(0, PER)], mine_hbm)]
    for c in stores:
        c.start()
    out_copy.wait()
    for c in stores:
        c.wait()


def lanes2(a, b):
    return jnp.concatenate([a, b], 1)


def local_step(core, x_in, cotangent, block_grid, keep_modes, n1g, n1b, w1, b1, w2, b2, n2g, n2b, fc1, fb1, fc2, fb2):
    rows, d = x_in.shape
    slots = rows // 2
    vm = pl.BlockSpec(memory_space=pltpu.VMEM)
    sm = pl.BlockSpec(memory_space=pltpu.SMEM)
    hbm = pl.BlockSpec(memory_space=pl.ANY)
    w1r = w1.reshape(LAYERS, 2, 512, 64)
    w2r = w2.reshape(LAYERS, 2, 512, 64)
    scratch = [
        pltpu.VMEM((rows, d), BF), pltpu.VMEM((rows, d), BF),
        pltpu.VMEM(w1r.shape, BF), pltpu.VMEM(w2r.shape, BF), pltpu.VMEM(fc1.shape, BF), pltpu.VMEM(fc2.shape, BF),
        pltpu.VMEM((rows, d), BF), pltpu.VMEM((rows, d), BF), pltpu.VMEM((LAYERS * PER, d), BF),
        pltpu.SemaphoreType.DMA((10,)),
        pltpu.VMEM((rows, rows), BF), pltpu.VMEM((rows, rows), BF),
        pltpu.VMEM((2, slots, 256), BF), pltpu.VMEM((2, slots, 256), BF), pltpu.VMEM((2, slots, 256), BF),
        pltpu.VMEM((slots, 128), BF), pltpu.VMEM((slots, 128), BF),
        pltpu.VMEM((LAYERS, 4, 256, 256), BF), pltpu.VMEM((LAYERS, 4, 256, 256), BF),
        pltpu.VMEM((LAYERS + 1, rows, d), BF), pltpu.VMEM((LAYERS + 1, rows, 128), F32),
        pltpu.VMEM((rows, d), F32), pltpu.VMEM((rows, d), BF),
        pltpu.VMEM((LAYERS, 2, slots, 2 * d), BF), pltpu.VMEM((LAYERS, 2, slots, 2 * d), BF),
        pltpu.VMEM((LAYERS, 2, slots, 2 * d), BF), pltpu.VMEM((LAYERS, 2, slots, 2 * d), BF),
        pltpu.VMEM((rows, d), BF),
        pltpu.VMEM((LAYERS, rows, d), BF), pltpu.VMEM((LAYERS, rows, 128), F32),
        pltpu.VMEM((LAYERS, rows, d), BF), pltpu.VMEM((LAYERS, rows, d), BF), pltpu.VMEM((LAYERS, rows, d), BF),
        pltpu.VMEM((rows, d), BF), pltpu.VMEM((rows, d), F32),
        pltpu.VMEM((LAYERS, 10, 8, d), F32),
    ]
    return pl.pallas_call(
        kernel,
        out_shape=(
            jax.ShapeDtypeStruct((rows, d), BF),
            jax.ShapeDtypeStruct((rows, d), BF),
            jax.ShapeDtypeStruct((PER, d), BF),
            jax.ShapeDtypeStruct((PER, d), BF),
        ),
        in_specs=[sm, sm, sm, hbm, hbm, vm, vm, hbm, vm, hbm, vm, vm, vm, hbm, vm, hbm, vm],
        out_specs=(hbm,) * 4,
        scratch_shapes=scratch,
        compiler_params=pltpu.CompilerParams(vmem_limit_bytes=64 * 1024 * 1024 - 65536),
        name="slab_step",
    )(block_grid, keep_modes, core, x_in, cotangent, n1g, n1b, w1r, b1, w2r, b2, n2g, n2b, fc1, fb1, fc2, fb2)


AXES = ("dp", "modes")


def spread(core_ref, mine, other, n1g, n1b, w1, b1, w2, b2, n2g, n2b, fc1, fb1, fc2, fb2):
    def write(layer, src):
        fc1[layer] = src[0:512, :].astype(F32)
        fc2[layer] = src[512:1024, :].astype(F32)
        for ref, base in ((w1, 1024), (w2, 1152)):
            for part in range(2):
                block = src[base + part * 64 : base + part * 64 + 64, :].astype(F32)
                for k in range(8):
                    ref[layer, part, k] = block[:, k * 64 : k * 64 + 64]
        vec = src[1280:1296, :].astype(F32)
        for row, ref in ((0, n1g), (1, n1b), (6, n2g), (7, n2b), (8, fb1), (9, fb2)):
            ref[layer : layer + 1, :] = vec[row : row + 1]
        b1[layer] = vec[2:4]
        b2[layer] = vec[4:6]

    @pl.when(core_ref[0] == 0)
    def _():
        write(0, mine)
        write(1, other)

    @pl.when(core_ref[0] != 0)
    def _():
        write(1, mine)
        write(0, other)


def unpack(core, mine, other, d):
    vm = pl.BlockSpec(memory_space=pltpu.VMEM)
    vec = jax.ShapeDtypeStruct((LAYERS, d), F32)
    pair = jax.ShapeDtypeStruct((LAYERS, 2, d), F32)
    mix = jax.ShapeDtypeStruct((LAYERS, 2, 8, 64, 64), F32)
    full = jax.ShapeDtypeStruct((LAYERS, d, d), F32)
    return pl.pallas_call(
        spread,
        out_shape=(vec, vec, mix, pair, mix, pair, vec, vec, full, vec, full, vec),
        in_specs=[pl.BlockSpec(memory_space=pltpu.SMEM), vm, vm],
        out_specs=(vm,) * 12,
        compiler_params=pltpu.CompilerParams(vmem_limit_bytes=32 * 1024 * 1024),
        name="spread",
    )(core, mine, other)


def exchange(a, bit, count):
    return lax.ppermute(a, AXES, [(i, i ^ bit) for i in range(count)])


def add(a, b):
    return (a.astype(F32) + b.astype(F32)).astype(BF)


def all_sum(mine, other, count):
    me = lax.axis_index(AXES)
    top = count // 2
    mine = add(mine, exchange(other, top, count))
    bits = [1 << k for k in range(top.bit_length() - 1)]
    orders = [[bits[(c + k) % 3] for k in range(3)] for c in range(3)]
    third = PER // 3
    parts = [mine[c * third : (c + 1) * third] for c in range(3)]
    for k in range(3):
        moved = []
        for c in range(3):
            n = parts[c].shape[0] // 2
            high = (me & orders[c][k]) != 0
            keep = jnp.where(high, parts[c][n:], parts[c][:n])
            send = jnp.where(high, parts[c][:n], parts[c][n:])
            moved.append((keep, exchange(send, orders[c][k], count)))
        parts = [add(keep, got) for keep, got in moved]
    n = parts[0].shape[0]
    last = jnp.concatenate(parts)
    for bit in bits[3:]:
        last = add(last, exchange(last, bit, count))
    parts = [last[c * n : (c + 1) * n] for c in range(3)]
    for k in reversed(range(3)):
        gots = [exchange(parts[c], orders[c][k], count) for c in range(3)]
        for c in range(3):
            high = (me & orders[c][k]) != 0
            low_part = jnp.where(high, gots[c], parts[c])
            high_part = jnp.where(high, parts[c], gots[c])
            parts[c] = jnp.concatenate([low_part, high_part])
    mine = jnp.concatenate(parts)
    return mine, exchange(mine, top, count)


def solution(mesh):
    count = mesh.shape["dp"] * mesh.shape["modes"]

    def on_device(*args):
        core = lax.axis_index("dp").astype(jnp.int32).reshape(1)
        out, x_grad, mine, other = local_step(core, *args)
        mine, other = all_sum(mine, other, count)
        return (out, x_grad) + tuple(unpack(core, mine, other, mine.shape[1]))

    rows = P(AXES, None)
    return jax.shard_map(
        on_device,
        mesh=mesh,
        in_specs=(rows, rows, P(AXES)) + (P(),) * 13,
        out_specs=(rows, rows) + (P(),) * 12,
        check_vma=False,
    )
```

profile of v0, /device:TPU:0, one launch (start us, length us, event | category | flops | bytes accessed | tf_op | source)
XLA Modules:
  0.0 111.3 jit_solution(10798332216218540934)
XLA Ops:
  0.7 44.2 %slab_step.1 = (bf16[1024,512]{1,0:T(8,128)(2,1)}, bf16[1024,512]{1,0:T(8,128)(2,1)}, bf16[1344,512]{1,0:T(8,128)(2,1)}, bf16[1344,512]{1,0:T(8,128)(2,1)}) custom-call(s32[16]{0:T(128)} %grid_ref.1, s32[3]{0:T(128)} %keep_ref.1, s32[1]{0:T(128)} %bitcast.core_ref, bf16[1024,512]{1,0:T(8,128)(2,1)} %x_hbm.1, bf16[1024,512]{1,0:T(8,128)(2,1)} %cot_hbm.1, ...), custom_call_target="tpu_custom_call" | custom-call | tf_op jit(solution)/shard_map/slab_step/pallas_call | solution.py:611
  44.8 0.5 collective-permute-start
  45.4 3.0 %collective-permute-done = bf16[1344,512]{1,0:T(8,128)(2,1)S(1)} collective-permute-done((bf16[1344,512]{1,0:T(8,128)(2,1)}, bf16[1344,512]{1,0:T(8,128)(2,1)S(1)}, u32[]{:S(2)}, u32[]{:S(2)}) %collective-permute-start) | collective-permute-done | bytes 1376288 | tf_op jit(solution)/shard_map/ppermute | solution.py:673
  48.3 1.7 %add_convert_fusion = bf16[1344,512]{1,0:T(8,128)(2,1)S(1)} fusion(bf16[1344,512]{1,0:T(8,128)(2,1)S(1)} %collective-permute-done, bf16[1344,512]{1,0:T(8,128)(2,1)} %get-tuple-element.32), kind=kLoop, calls=%fused_computation | loop fusion | flops 2752512 | bytes 4128768 | tf_op jit(solution)/shard_map/convert_element_type | solution.py:677
  50.0 0.1 broadcast_select_fusion.2
  50.1 2.9 %collective-permute-start.1 = (bf16[224,512]{1,0:T(8,128)(2,1)S(1)}, bf16[224,512]{1,0:T(8,128)(2,1)S(1)}, u32[]{:S(2)}, u32[]{:S(2)}) collective-permute-start(bf16[224,512]{1,0:T(8,128)(2,1)S(1)} %get-tuple-element.49), channel_id=1, source_target_pairs={{0,1},{1,0},{2,3},{3,2},{4,5},{5,4},{6,7},{7,6},{8,9},{9,8},{10,11... | collective-permute-start | bytes 688136 | tf_op jit(solution)/shard_map/ppermute | solution.py:673
  53.0 2.5 %collective-permute-start.7 = (bf16[224,512]{1,0:T(8,128)(2,1)S(1)}, bf16[224,512]{1,0:T(8,128)(2,1)S(1)}, u32[]{:S(2)}, u32[]{:S(2)}) collective-permute-start(bf16[224,512]{1,0:T(8,128)(2,1)S(1)} %get-tuple-element.50), channel_id=1, source_target_pairs={{0,4},{1,5},{2,6},{3,7},{4,0},{5,1},{6,2},{7,3},{8,12},{9,13},{10,... | collective-permute-start | bytes 688136 | tf_op jit(solution)/shard_map/ppermute | solution.py:673
  55.6 0.0 collective-permute-start.4
  55.6 3.5 %collective-permute-done.1 = bf16[224,512]{1,0:T(8,128)(2,1)S(1)} collective-permute-done((bf16[224,512]{1,0:T(8,128)(2,1)S(1)}, bf16[224,512]{1,0:T(8,128)(2,1)S(1)}, u32[]{:S(2)}, u32[]{:S(2)}) %collective-permute-start.1) | collective-permute-done | bytes 229408 | tf_op jit(solution)/shard_map/ppermute | solution.py:673
  59.1 2.1 %collective-permute-done.7 = bf16[224,512]{1,0:T(8,128)(2,1)S(1)} collective-permute-done((bf16[224,512]{1,0:T(8,128)(2,1)S(1)}, bf16[224,512]{1,0:T(8,128)(2,1)S(1)}, u32[]{:S(2)}, u32[]{:S(2)}) %collective-permute-start.7) | collective-permute-done | bytes 229408 | tf_op jit(solution)/shard_map/ppermute | solution.py:673
  61.2 1.5 %collective-permute-done.4 = bf16[224,512]{1,0:T(8,128)(2,1)S(1)} collective-permute-done((bf16[224,512]{1,0:T(8,128)(2,1)S(1)}, bf16[224,512]{1,0:T(8,128)(2,1)S(1)}, u32[]{:S(2)}, u32[]{:S(2)}) %collective-permute-start.4) | collective-permute-done | bytes 229408 | tf_op jit(solution)/shard_map/ppermute | solution.py:673
  62.7 0.3 add_convert_fusion.3
  63.0 0.3 collective-permute-start.5
  63.4 0.5 collective-permute-start.8
  63.9 1.3 %collective-permute-start.2 = (bf16[112,512]{1,0:T(8,128)(2,1)S(1)}, bf16[112,512]{1,0:T(8,128)(2,1)S(1)}, u32[]{:S(2)}, u32[]{:S(2)}) collective-permute-start(bf16[112,512]{1,0:T(8,128)(2,1)S(1)} %broadcast_select_fusion.11), channel_id=1, source_target_pairs={{0,2},{1,3},{2,0},{3,1},{4,6},{5,7},{6,4},{7,5},{8,10},{9,11},{10,... | collective-permute-start | bytes 344072 | tf_op jit(solution)/shard_map/ppermute | solution.py:673
  65.2 2.7 %collective-permute-done.5 = bf16[112,512]{1,0:T(8,128)(2,1)S(1)} collective-permute-done((bf16[112,512]{1,0:T(8,128)(2,1)S(1)}, bf16[112,512]{1,0:T(8,128)(2,1)S(1)}, u32[]{:S(2)}, u32[]{:S(2)}) %collective-permute-start.5) | collective-permute-done | bytes 114720 | tf_op jit(solution)/shard_map/ppermute | solution.py:673
  67.9 0.4 collective-permute-start.6
  68.4 1.7 %collective-permute-start.9 = (bf16[56,512]{1,0:T(8,128)(2,1)S(1)}, bf16[56,512]{1,0:T(8,128)(2,1)S(1)}, u32[]{:S(2)}, u32[]{:S(2)}) collective-permute-start(bf16[56,512]{1,0:T(8,128)(2,1)S(1)} %broadcast_select_fusion.14), channel_id=1, source_target_pairs={{0,2},{1,3},{2,0},{3,1},{4,6},{5,7},{6,4},{7,5},{8,10},{9,11},{10,... | collective-permute-start | bytes 172040 | tf_op jit(solution)/shard_map/ppermute | solution.py:673
  70.2 0.9 collective-permute-start.3
  71.1 1.0 collective-permute-done.6
  72.2 0.5 collective-permute-done.9
  72.7 3.2 %collective-permute-done.3 = bf16[56,512]{1,0:T(8,128)(2,1)S(1)} collective-permute-done((bf16[56,512]{1,0:T(8,128)(2,1)S(1)}, bf16[56,512]{1,0:T(8,128)(2,1)S(1)}, u32[]{:S(2)}, u32[]{:S(2)}) %collective-permute-start.3) | collective-permute-done | bytes 57376 | tf_op jit(solution)/shard_map/ppermute | solution.py:673
  75.9 1.8 %collective-permute-start.10 = (bf16[168,512]{1,0:T(8,128)(2,1)S(1)}, bf16[168,512]{1,0:T(8,128)(2,1)S(1)}, u32[]{:S(2)}, u32[]{:S(2)}) collective-permute-start(bf16[168,512]{1,0:T(8,128)(2,1)S(1)} %pad_maximum_fusion.3), channel_id=1, source_target_pairs={{0,8},{1,9},{2,10},{3,11},{4,12},{5,13},{6,14},{7,15},{8,0},{9,1},... | collective-permute-start | bytes 516104 | tf_op jit(solution)/shard_map/ppermute | solution.py:673
  77.7 6.3 %collective-permute-done.10 = bf16[168,512]{1,0:T(8,128)(2,1)S(1)} collective-permute-done((bf16[168,512]{1,0:T(8,128)(2,1)S(1)}, bf16[168,512]{1,0:T(8,128)(2,1)S(1)}, u32[]{:S(2)}, u32[]{:S(2)}) %collective-permute-start.10) | collective-permute-done | bytes 172064 | tf_op jit(solution)/shard_map/ppermute | solution.py:673
  84.1 0.3 collective-permute-start.17
  84.4 1.6 %collective-permute-start.14 = (bf16[56,512]{1,0:T(8,128)(2,1)S(1)}, bf16[56,512]{1,0:T(8,128)(2,1)S(1)}, u32[]{:S(2)}, u32[]{:S(2)}) collective-permute-start(bf16[56,512]{1,0:T(8,128)(2,1)S(1)} %get-tuple-element.69), channel_id=1, source_target_pairs={{0,1},{1,0},{2,3},{3,2},{4,5},{5,4},{6,7},{7,6},{8,9},{9,8},{10,11... | collective-permute-start | bytes 172040 | tf_op jit(solution)/shard_map/ppermute | solution.py:673
  86.0 0.0 collective-permute-start.11
  86.0 2.7 %collective-permute-done.17 = bf16[56,512]{1,0:T(8,128)(2,1)S(1)} collective-permute-done((bf16[56,512]{1,0:T(8,128)(2,1)S(1)}, bf16[56,512]{1,0:T(8,128)(2,1)S(1)}, u32[]{:S(2)}, u32[]{:S(2)}) %collective-permute-start.17) | collective-permute-done | bytes 57376 | tf_op jit(solution)/shard_map/ppermute | solution.py:673
  88.7 0.1 collective-permute-done.14
  88.8 1.3 %collective-permute-done.11 = bf16[56,512]{1,0:T(8,128)(2,1)S(1)} collective-permute-done((bf16[56,512]{1,0:T(8,128)(2,1)S(1)}, bf16[56,512]{1,0:T(8,128)(2,1)S(1)}, u32[]{:S(2)}, u32[]{:S(2)}) %collective-permute-start.11) | collective-permute-done | bytes 57376 | tf_op jit(solution)/shard_map/ppermute | solution.py:673
  90.2 0.1 collective-permute-start.15
  90.3 0.9 collective-permute-start.12
  91.3 1.4 %collective-permute-start.18 = (bf16[112,512]{1,0:T(8,128)(2,1)S(1)}, bf16[112,512]{1,0:T(8,128)(2,1)S(1)}, u32[]{:S(2)}, u32[]{:S(2)}) collective-permute-start(bf16[112,512]{1,0:T(8,128)(2,1)S(1)} %pad_maximum_fusion.6), channel_id=1, source_target_pairs={{0,1},{1,0},{2,3},{3,2},{4,5},{5,4},{6,7},{7,6},{8,9},{9,8},{10,11... | collective-permute-start | bytes 344072 | tf_op jit(solution)/shard_map/ppermute | solution.py:673
  92.7 2.7 %collective-permute-done.15 = bf16[112,512]{1,0:T(8,128)(2,1)S(1)} collective-permute-done((bf16[112,512]{1,0:T(8,128)(2,1)S(1)}, bf16[112,512]{1,0:T(8,128)(2,1)S(1)}, u32[]{:S(2)}, u32[]{:S(2)}) %collective-permute-start.15) | collective-permute-done | bytes 114720 | tf_op jit(solution)/shard_map/ppermute | solution.py:673
  95.5 1.4 %collective-permute-start.16 = (bf16[224,512]{1,0:T(8,128)(2,1)S(1)}, bf16[224,512]{1,0:T(8,128)(2,1)S(1)}, u32[]{:S(2)}, u32[]{:S(2)}) collective-permute-start(bf16[224,512]{1,0:T(8,128)(2,1)S(1)} %pad_maximum_fusion.1), channel_id=1, source_target_pairs={{0,2},{1,3},{2,0},{3,1},{4,6},{5,7},{6,4},{7,5},{8,10},{9,11},{10,... | collective-permute-start | bytes 688136 | tf_op jit(solution)/shard_map/ppermute | solution.py:673
  97.0 1.6 %collective-permute-start.13 = (bf16[224,512]{1,0:T(8,128)(2,1)S(1)}, bf16[224,512]{1,0:T(8,128)(2,1)S(1)}, u32[]{:S(2)}, u32[]{:S(2)}) collective-permute-start(bf16[224,512]{1,0:T(8,128)(2,1)S(1)} %pad_maximum_fusion), channel_id=1, source_target_pairs={{0,1},{1,0},{2,3},{3,2},{4,5},{5,4},{6,7},{7,6},{8,9},{9,8},{10,11... | collective-permute-start | bytes 688136 | tf_op jit(solution)/shard_map/ppermute | solution.py:673
  98.7 0.2 collective-permute-start.19
  98.9 4.1 %collective-permute-done.13 = bf16[224,512]{1,0:T(8,128)(2,1)S(1)} collective-permute-done((bf16[224,512]{1,0:T(8,128)(2,1)S(1)}, bf16[224,512]{1,0:T(8,128)(2,1)S(1)}, u32[]{:S(2)}, u32[]{:S(2)}) %collective-permute-start.13) | collective-permute-done | bytes 229408 | tf_op jit(solution)/shard_map/ppermute | solution.py:673
  103.1 0.1 select_dynamic-update-slice_fusion.5
  103.1 0.1 select_dynamic-update-slice_fusion.4
  103.2 0.1 select_dynamic-update-slice_fusion.3
  103.3 0.1 select_dynamic-update-slice_fusion.2
  103.4 1.4 %collective-permute-done.19 = bf16[224,512]{1,0:T(8,128)(2,1)S(1)} collective-permute-done((bf16[224,512]{1,0:T(8,128)(2,1)S(1)}, bf16[224,512]{1,0:T(8,128)(2,1)S(1)}, u32[]{:S(2)}, u32[]{:S(2)}) %collective-permute-start.19) | collective-permute-done | bytes 229408 | tf_op jit(solution)/shard_map/ppermute | solution.py:673
  104.8 0.1 select_dynamic-update-slice_fusion.1
  104.8 0.1 select_dynamic-update-slice_fusion.mine
  104.9 0.1 collective-permute-start.20
  105.0 3.1 %collective-permute-done.20.other = bf16[1344,512]{1,0:T(8,128)(2,1)S(1)} collective-permute-done((bf16[1344,512]{1,0:T(8,128)(2,1)S(1)}, bf16[1344,512]{1,0:T(8,128)(2,1)S(1)}, u32[]{:S(2)}, u32[]{:S(2)}) %collective-permute-start.20) | collective-permute-done | bytes 1376288 | tf_op jit(solution)/shard_map/ppermute | solution.py:673
  108.1 3.2 %spread.1 = (f32[2,512]{1,0:T(2,128)}, f32[2,512]{1,0:T(2,128)}, f32[2,2,8,64,64]{4,3,2,1,0:T(8,128)}, f32[2,2,512]{2,1,0:T(2,128)}, f32[2,2,8,64,64]{4,3,2,1,0:...) custom-call(s32[1]{0:T(128)} %bitcast.core_ref, ...), custom_call_target="tpu_custom_call" | custom-call | tf_op jit(solution)/shard_map/spread/pallas_call | solution.py:662
  (30 shorter events, 0.6 us)
Async XLA Ops:
  44.8 3.5 %collective-permute-start = (bf16[1344,512]{1,0:T(8,128)(2,1)}, bf16[1344,512]{1,0:T(8,128)(2,1)S(1)}, u32[]{:S(2)}, u32[]{:S(2)}) collective-permute-start(bf16[1344,512]{1,0:T(8,128)(2,1)} %get-tuple-element.33), channel_id=1, source_target_pairs={{0,16},{1,17},{2,18},{3,19},{4,20},{5,21},{6,22},{7,23},{8,24},{9,... | collective-permute-start | bytes 4128776 | tf_op jit(solution)/shard_map/ppermute | solution.py:673
  50.1 9.0 %collective-permute-start.1 = (bf16[224,512]{1,0:T(8,128)(2,1)S(1)}, bf16[224,512]{1,0:T(8,128)(2,1)S(1)}, u32[]{:S(2)}, u32[]{:S(2)}) collective-permute-start(bf16[224,512]{1,0:T(8,128)(2,1)S(1)} %get-tuple-element.49), channel_id=1, source_target_pairs={{0,1},{1,0},{2,3},{3,2},{4,5},{5,4},{6,7},{7,6},{8,9},{9,8},{10,11... | collective-permute-start | bytes 688136 | tf_op jit(solution)/shard_map/ppermute | solution.py:673
  53.0 8.2 %collective-permute-start.7 = (bf16[224,512]{1,0:T(8,128)(2,1)S(1)}, bf16[224,512]{1,0:T(8,128)(2,1)S(1)}, u32[]{:S(2)}, u32[]{:S(2)}) collective-permute-start(bf16[224,512]{1,0:T(8,128)(2,1)S(1)} %get-tuple-element.50), channel_id=1, source_target_pairs={{0,4},{1,5},{2,6},{3,7},{4,0},{5,1},{6,2},{7,3},{8,12},{9,13},{10,... | collective-permute-start | bytes 688136 | tf_op jit(solution)/shard_map/ppermute | solution.py:673
  55.6 7.1 %collective-permute-start.4 = (bf16[224,512]{1,0:T(8,128)(2,1)S(1)}, bf16[224,512]{1,0:T(8,128)(2,1)S(1)}, u32[]{:S(2)}, u32[]{:S(2)}) collective-permute-start(bf16[224,512]{1,0:T(8,128)(2,1)S(1)} %get-tuple-element.51), channel_id=1, source_target_pairs={{0,2},{1,3},{2,0},{3,1},{4,6},{5,7},{6,4},{7,5},{8,10},{9,11},{10,... | collective-permute-start | bytes 688136 | tf_op jit(solution)/shard_map/ppermute | solution.py:673
  63.0 4.9 %collective-permute-start.5 = (bf16[112,512]{1,0:T(8,128)(2,1)S(1)}, bf16[112,512]{1,0:T(8,128)(2,1)S(1)}, u32[]{:S(2)}, u32[]{:S(2)}) collective-permute-start(bf16[112,512]{1,0:T(8,128)(2,1)S(1)} %broadcast_select_fusion.8), channel_id=1, source_target_pairs={{0,4},{1,5},{2,6},{3,7},{4,0},{5,1},{6,2},{7,3},{8,12},{9,13},{10,... | collective-permute-start | bytes 344072 | tf_op jit(solution)/shard_map/ppermute | solution.py:673
  63.4 5.0 %collective-permute-start.8 = (bf16[112,512]{1,0:T(8,128)(2,1)S(1)}, bf16[112,512]{1,0:T(8,128)(2,1)S(1)}, u32[]{:S(2)}, u32[]{:S(2)}) collective-permute-start(bf16[112,512]{1,0:T(8,128)(2,1)S(1)} %broadcast_select_fusion.5), channel_id=1, source_target_pairs={{0,1},{1,0},{2,3},{3,2},{4,5},{5,4},{6,7},{7,6},{8,9},{9,8},{10,11... | collective-permute-start | bytes 344072 | tf_op jit(solution)/shard_map/ppermute | solution.py:673
  63.9 6.3 %collective-permute-start.2 = (bf16[112,512]{1,0:T(8,128)(2,1)S(1)}, bf16[112,512]{1,0:T(8,128)(2,1)S(1)}, u32[]{:S(2)}, u32[]{:S(2)}) collective-permute-start(bf16[112,512]{1,0:T(8,128)(2,1)S(1)} %broadcast_select_fusion.11), channel_id=1, source_target_pairs={{0,2},{1,3},{2,0},{3,1},{4,6},{5,7},{6,4},{7,5},{8,10},{9,11},{10,... | collective-permute-start | bytes 344072 | tf_op jit(solution)/shard_map/ppermute | solution.py:673
  67.9 4.2 %collective-permute-start.6 = (bf16[56,512]{1,0:T(8,128)(2,1)S(1)}, bf16[56,512]{1,0:T(8,128)(2,1)S(1)}, u32[]{:S(2)}, u32[]{:S(2)}) collective-permute-start(bf16[56,512]{1,0:T(8,128)(2,1)S(1)} %broadcast_select_fusion.17), channel_id=1, source_target_pairs={{0,1},{1,0},{2,3},{3,2},{4,5},{5,4},{6,7},{7,6},{8,9},{9,8},{10,11... | collective-permute-start | bytes 172040 | tf_op jit(solution)/shard_map/ppermute | solution.py:673
  68.4 4.2 %collective-permute-start.9 = (bf16[56,512]{1,0:T(8,128)(2,1)S(1)}, bf16[56,512]{1,0:T(8,128)(2,1)S(1)}, u32[]{:S(2)}, u32[]{:S(2)}) collective-permute-start(bf16[56,512]{1,0:T(8,128)(2,1)S(1)} %broadcast_select_fusion.14), channel_id=1, source_target_pairs={{0,2},{1,3},{2,0},{3,1},{4,6},{5,7},{6,4},{7,5},{8,10},{9,11},{10,... | collective-permute-start | bytes 172040 | tf_op jit(solution)/shard_map/ppermute | solution.py:673
  70.2 5.6 %collective-permute-start.3 = (bf16[56,512]{1,0:T(8,128)(2,1)S(1)}, bf16[56,512]{1,0:T(8,128)(2,1)S(1)}, u32[]{:S(2)}, u32[]{:S(2)}) collective-permute-start(bf16[56,512]{1,0:T(8,128)(2,1)S(1)} %broadcast_select_fusion.20), channel_id=1, source_target_pairs={{0,4},{1,5},{2,6},{3,7},{4,0},{5,1},{6,2},{7,3},{8,12},{9,13},{10,... | collective-permute-start | bytes 172040 | tf_op jit(solution)/shard_map/ppermute | solution.py:673
  75.9 8.1 %collective-permute-start.10 = (bf16[168,512]{1,0:T(8,128)(2,1)S(1)}, bf16[168,512]{1,0:T(8,128)(2,1)S(1)}, u32[]{:S(2)}, u32[]{:S(2)}) collective-permute-start(bf16[168,512]{1,0:T(8,128)(2,1)S(1)} %pad_maximum_fusion.3), channel_id=1, source_target_pairs={{0,8},{1,9},{2,10},{3,11},{4,12},{5,13},{6,14},{7,15},{8,0},{9,1},... | collective-permute-start | bytes 516104 | tf_op jit(solution)/shard_map/ppermute | solution.py:673
  84.1 4.6 %collective-permute-start.17 = (bf16[56,512]{1,0:T(8,128)(2,1)S(1)}, bf16[56,512]{1,0:T(8,128)(2,1)S(1)}, u32[]{:S(2)}, u32[]{:S(2)}) collective-permute-start(bf16[56,512]{1,0:T(8,128)(2,1)S(1)} %get-tuple-element.68), channel_id=1, source_target_pairs={{0,2},{1,3},{2,0},{3,1},{4,6},{5,7},{6,4},{7,5},{8,10},{9,11},{10,... | collective-permute-start | bytes 172040 | tf_op jit(solution)/shard_map/ppermute | solution.py:673
  84.4 4.5 %collective-permute-start.14 = (bf16[56,512]{1,0:T(8,128)(2,1)S(1)}, bf16[56,512]{1,0:T(8,128)(2,1)S(1)}, u32[]{:S(2)}, u32[]{:S(2)}) collective-permute-start(bf16[56,512]{1,0:T(8,128)(2,1)S(1)} %get-tuple-element.69), channel_id=1, source_target_pairs={{0,1},{1,0},{2,3},{3,2},{4,5},{5,4},{6,7},{7,6},{8,9},{9,8},{10,11... | collective-permute-start | bytes 172040 | tf_op jit(solution)/shard_map/ppermute | solution.py:673
  86.0 4.2 %collective-permute-start.11 = (bf16[56,512]{1,0:T(8,128)(2,1)S(1)}, bf16[56,512]{1,0:T(8,128)(2,1)S(1)}, u32[]{:S(2)}, u32[]{:S(2)}) collective-permute-start(bf16[56,512]{1,0:T(8,128)(2,1)S(1)} %get-tuple-element.70), channel_id=1, source_target_pairs={{0,4},{1,5},{2,6},{3,7},{4,0},{5,1},{6,2},{7,3},{8,12},{9,13},{10,... | collective-permute-start | bytes 172040 | tf_op jit(solution)/shard_map/ppermute | solution.py:673
  90.2 5.2 %collective-permute-start.15 = (bf16[112,512]{1,0:T(8,128)(2,1)S(1)}, bf16[112,512]{1,0:T(8,128)(2,1)S(1)}, u32[]{:S(2)}, u32[]{:S(2)}) collective-permute-start(bf16[112,512]{1,0:T(8,128)(2,1)S(1)} %pad_maximum_fusion.5), channel_id=1, source_target_pairs={{0,4},{1,5},{2,6},{3,7},{4,0},{5,1},{6,2},{7,3},{8,12},{9,13},{10,... | collective-permute-start | bytes 344072 | tf_op jit(solution)/shard_map/ppermute | solution.py:673
  90.3 6.6 %collective-permute-start.12 = (bf16[112,512]{1,0:T(8,128)(2,1)S(1)}, bf16[112,512]{1,0:T(8,128)(2,1)S(1)}, u32[]{:S(2)}, u32[]{:S(2)}) collective-permute-start(bf16[112,512]{1,0:T(8,128)(2,1)S(1)} %pad_maximum_fusion.4), channel_id=1, source_target_pairs={{0,2},{1,3},{2,0},{3,1},{4,6},{5,7},{6,4},{7,5},{8,10},{9,11},{10,... | collective-permute-start | bytes 344072 | tf_op jit(solution)/shard_map/ppermute | solution.py:673
  91.3 7.3 %collective-permute-start.18 = (bf16[112,512]{1,0:T(8,128)(2,1)S(1)}, bf16[112,512]{1,0:T(8,128)(2,1)S(1)}, u32[]{:S(2)}, u32[]{:S(2)}) collective-permute-start(bf16[112,512]{1,0:T(8,128)(2,1)S(1)} %pad_maximum_fusion.6), channel_id=1, source_target_pairs={{0,1},{1,0},{2,3},{3,2},{4,5},{5,4},{6,7},{7,6},{8,9},{9,8},{10,11... | collective-permute-start | bytes 344072 | tf_op jit(solution)/shard_map/ppermute | solution.py:673
  95.5 7.7 %collective-permute-start.16 = (bf16[224,512]{1,0:T(8,128)(2,1)S(1)}, bf16[224,512]{1,0:T(8,128)(2,1)S(1)}, u32[]{:S(2)}, u32[]{:S(2)}) collective-permute-start(bf16[224,512]{1,0:T(8,128)(2,1)S(1)} %pad_maximum_fusion.1), channel_id=1, source_target_pairs={{0,2},{1,3},{2,0},{3,1},{4,6},{5,7},{6,4},{7,5},{8,10},{9,11},{10,... | collective-permute-start | bytes 688136 | tf_op jit(solution)/shard_map/ppermute | solution.py:673
  97.0 6.1 %collective-permute-start.13 = (bf16[224,512]{1,0:T(8,128)(2,1)S(1)}, bf16[224,512]{1,0:T(8,128)(2,1)S(1)}, u32[]{:S(2)}, u32[]{:S(2)}) collective-permute-start(bf16[224,512]{1,0:T(8,128)(2,1)S(1)} %pad_maximum_fusion), channel_id=1, source_target_pairs={{0,1},{1,0},{2,3},{3,2},{4,5},{5,4},{6,7},{7,6},{8,9},{9,8},{10,11... | collective-permute-start | bytes 688136 | tf_op jit(solution)/shard_map/ppermute | solution.py:673
  98.7 6.1 %collective-permute-start.19 = (bf16[224,512]{1,0:T(8,128)(2,1)S(1)}, bf16[224,512]{1,0:T(8,128)(2,1)S(1)}, u32[]{:S(2)}, u32[]{:S(2)}) collective-permute-start(bf16[224,512]{1,0:T(8,128)(2,1)S(1)} %pad_maximum_fusion.2), channel_id=1, source_target_pairs={{0,4},{1,5},{2,6},{3,7},{4,0},{5,1},{6,2},{7,3},{8,12},{9,13},{10,... | collective-permute-start | bytes 688136 | tf_op jit(solution)/shard_map/ppermute | solution.py:673
  104.9 3.2 %collective-permute-start.20 = (bf16[1344,512]{1,0:T(8,128)(2,1)S(1)}, bf16[1344,512]{1,0:T(8,128)(2,1)S(1)}, u32[]{:S(2)}, u32[]{:S(2)}) collective-permute-start(bf16[1344,512]{1,0:T(8,128)(2,1)S(1)} %select_dynamic-update-slice_fusion.mine), channel_id=1, source_target_pairs={{0,16},{1,17},{2,18},{3,19},{4,20},{5,21},{6,22},{7,23},{8,24},{9,... | collective-permute-start | bytes 4128776 | tf_op jit(solution)/shard_map/ppermute | solution.py:673
where the time goes:
time: 111 us
  Pallas kernels  47.4 us (43%)
  waiting for transfers between devices  39.2 us (35%)
  starting transfers between devices  20.8 us (19%)
  other arithmetic  3.02 us (3%)
    pallas_call x1, Pallas kernels, local_step(): pl.pallas_call(kernel, out_shape=(jax.ShapeDtypeStruct((rows, d), BF), ja...  44.2 us
    ppermute x21, waiting for transfers between devices, exchange(): return lax.ppermute(a, AXES, [(i, i ^ bit) for i in range(count)])  39.2 us
    ppermute x21, starting transfers between devices, exchange(): return lax.ppermute(a, AXES, [(i, i ^ bit) for i in range(count)])  20.8 us
    pallas_call x1, Pallas kernels, unpack(): pl.pallas_call(spread, out_shape=(vec, vec, mix, pair, mix, pair, vec, ve...  3.19 us
    convert_element_type x9, other arithmetic, add(): return (a.astype(F32) + b.astype(F32)).astype(BF)  2.24 us
  transfers between devices with their start and end apart: 21, of which 16 were waited for; matrix products, arithmetic and copies ran while one was open for 1% of the time, Pallas kernels for 0%

commit v1 on v0

--- a/solution.py
+++ b/solution.py
@@ -96,7 +96,7 @@
     return 2 * (slot - local), p, q, special, pm, qm
 
 
-def build_tables(grid_ref, keep_ref, at, k1, k2, k3, nm, nb):
+def build_tables(grid_ref, keep_ref, at, k1, k3, nm, nb):
     rows = at.shape[1]
     slots = rows // 2
     unit = slots // NBLK
@@ -171,7 +171,7 @@
         nm[dst, :] = n.astype(BF)
         nb[dst, :] = (1.0 - n).astype(BF)
         for sign, (m, im) in enumerate(((plus, plus * n), (minus, -minus * n))):
-            for ref, f in ((k1, 1.0), (k2, 0.05), (k3, 0.05 * 0.0025)):
+            for ref, f in ((k1, 1.0), (k3, 0.05 * 0.0025)):
                 ref[sign, dst, 0:128] = (m * f).astype(BF)
                 ref[sign, dst, 128:256] = (im * f).astype(BF)
         return carry
@@ -210,12 +210,12 @@
     grid_ref, keep_ref, core_ref, x_hbm, cot_hbm,
     n1g, n1b, w1_hbm, b1, w2_hbm, b2, n2g, n2b, fc1_hbm, fb1, fc2_hbm, fb2,
     out_hbm, xg_hbm, mine_hbm, other_hbm,
-    x_ref, cot_ref, w1, w2, fc1, fc2, out_ref, xg_ref, grads_ref, sems,
-    at, st, k1, k2, k3, nm, nb, w1g, w2g,
+    x_ref, cot_ref, w1, w2, fc1, fc2, out_ref, grads_ref, sems,
+    at, st, k1, k3, nm, nb, w1g, w2g,
     xh1, rs1, hu, ul, z, o, da, ds, pq, xh2, rs2, v, act, dp,
-    gm, gmid, acc,
+    gmid, acc,
 ):
-    g_s, gy = hu, ul
+    g_s, gy, gm, xg_ref = hu, ul, x_ref, cot_ref
 
     def copy(k, src, dst):
         return pltpu.make_async_copy(src, dst, sems.at[k])
@@ -232,7 +232,7 @@
     slots = rows // 2
     tiles = rows // RT
     stiles = slots // ST
-    build_tables(grid_ref, keep_ref, at, k1, k2, k3, nm, nb)
+    build_tables(grid_ref, keep_ref, at, k1, k3, nm, nb)
     for i in range(4):
         st[:, i * 256 : (i + 1) * 256] = at[i * 256 : (i + 1) * 256, :].T
     loads[1].wait()
@@ -268,7 +268,7 @@
                 norm1(0, dst, x_ref[dst, :].astype(F32))
 
     def block(f):
-        pl.when(grid_ref[0] > 0)(f)
+        f()
 
     loads[0].wait()
     enter()
@@ -565,16 +565,23 @@
         block(lambda: in_backward(layer))
         return carry
 
-    for layer in range(LAYERS):
+    def vectors(layer):
         t = jnp.sum(acc[layer], 1)
         t = jnp.concatenate([t, jnp.zeros((PER - 1290, 512), F32)], 0)
         grads_ref[pl.ds(pl.multiple_of((layer ^ core_ref[0]) * PER, PER) + 1280, PER - 1280), :] = t.astype(BF)
-    stores = [copy(7, xg_ref, xg_hbm), copy(8, grads_ref.at[pl.ds(PER, PER)], other_hbm), copy(9, grads_ref.at[pl.ds(0, PER)], mine_hbm)]
-    for c in stores:
-        c.start()
+
+    vectors(1)
+    mine_copy = copy(8, grads_ref.at[pl.ds(0, PER)], mine_hbm)
+    other_copy = copy(9, grads_ref.at[pl.ds(PER, PER)], other_hbm)
+    xg_copy = copy(7, xg_ref, xg_hbm)
+    vectors(0)
+    other_copy.start()
+    mine_copy.start()
+    xg_copy.start()
     out_copy.wait()
-    for c in stores:
-        c.wait()
+    other_copy.wait()
+    mine_copy.wait()
+    xg_copy.wait()
 
 
 def lanes2(a, b):
@@ -592,10 +599,10 @@
     scratch = [
         pltpu.VMEM((rows, d), BF), pltpu.VMEM((rows, d), BF),
         pltpu.VMEM(w1r.shape, BF), pltpu.VMEM(w2r.shape, BF), pltpu.VMEM(fc1.shape, BF), pltpu.VMEM(fc2.shape, BF),
-        pltpu.VMEM((rows, d), BF), pltpu.VMEM((rows, d), BF), pltpu.VMEM((LAYERS * PER, d), BF),
+        pltpu.VMEM((rows, d), BF), pltpu.VMEM((LAYERS * PER, d), BF),
         pltpu.SemaphoreType.DMA((10,)),
         pltpu.VMEM((rows, rows), BF), pltpu.VMEM((rows, rows), BF),
-        pltpu.VMEM((2, slots, 256), BF), pltpu.VMEM((2, slots, 256), BF), pltpu.VMEM((2, slots, 256), BF),
+        pltpu.VMEM((2, slots, 256), BF), pltpu.VMEM((2, slots, 256), BF),
         pltpu.VMEM((slots, 128), BF), pltpu.VMEM((slots, 128), BF),
         pltpu.VMEM((LAYERS, 4, 256, 256), BF), pltpu.VMEM((LAYERS, 4, 256, 256), BF),
         pltpu.VMEM((LAYERS + 1, rows, d), BF), pltpu.VMEM((LAYERS + 1, rows, 128), F32),
@@ -605,7 +612,7 @@
         pltpu.VMEM((rows, d), BF),
         pltpu.VMEM((LAYERS, rows, d), BF), pltpu.VMEM((LAYERS, rows, 128), F32),
         pltpu.VMEM((LAYERS, rows, d), BF), pltpu.VMEM((LAYERS, rows, d), BF), pltpu.VMEM((LAYERS, rows, d), BF),
-        pltpu.VMEM((rows, d), BF), pltpu.VMEM((rows, d), F32),
+        pltpu.VMEM((rows, d), F32),
         pltpu.VMEM((LAYERS, 10, 8, d), F32),
     ]
     return pl.pallas_call(
@@ -619,7 +626,7 @@
         in_specs=[sm, sm, sm, hbm, hbm, vm, vm, hbm, vm, hbm, vm, vm, vm, hbm, vm, hbm, vm],
         out_specs=(hbm,) * 4,
         scratch_shapes=scratch,
-        compiler_params=pltpu.CompilerParams(vmem_limit_bytes=64 * 1024 * 1024 - 65536),
+        compiler_params=pltpu.CompilerParams(vmem_limit_bytes=58 * 1024 * 1024),
         name="slab_step",
     )(block_grid, keep_modes, core, x_in, cotangent, n1g, n1b, w1r, b1, w2r, b2, n2g, n2b, fc1, fb1, fc2, fb2)
 
@@ -627,46 +634,87 @@
 AXES = ("dp", "modes")
 
 
-def spread(core_ref, mine, other, n1g, n1b, w1, b1, w2, b2, n2g, n2b, fc1, fb1, fc2, fb2):
-    def write(layer, src):
-        fc1[layer] = src[0:512, :].astype(F32)
-        fc2[layer] = src[512:1024, :].astype(F32)
-        for ref, base in ((w1, 1024), (w2, 1152)):
-            for part in range(2):
-                block = src[base + part * 64 : base + part * 64 + 64, :].astype(F32)
-                for k in range(8):
-                    ref[layer, part, k] = block[:, k * 64 : k * 64 + 64]
-        vec = src[1280:1296, :].astype(F32)
+def spread_layer(layer, src, outs, bufs, sems):
+    fc1, fc2, w1, w2 = bufs
+    fc1[...] = src[0:512, :].astype(F32)
+    copies = [pltpu.make_async_copy(buf, out.at[layer], sems.at[k]) for k, (buf, out) in enumerate(zip(bufs, outs))]
+    copies[0].start()
+    fc2[...] = src[512:1024, :].astype(F32)
+    copies[1].start()
+    for k, (ref, base) in enumerate(((w1, 1024), (w2, 1152))):
+        for part in range(2):
+            block = src[base + part * 64 : base + part * 64 + 64, :].astype(F32)
+            for j in range(8):
+                ref[part, j] = block[:, j * 64 : j * 64 + 64]
+        copies[2 + k].start()
+    return copies
+
+
+def spread_mine(core_ref, mine, fc1_out, fc2_out, w1_out, w2_out, fc1, fc2, w1, w2, sems):
+    for c in spread_layer(core_ref[0], mine, (fc1_out, fc2_out, w1_out, w2_out), (fc1, fc2, w1, w2), sems):
+        c.wait()
+
+
+def spread_other(
+    core_ref, mine, other, fc1_in, fc2_in, w1_in, w2_in,
+    fc1_out, fc2_out, w1_out, w2_out, n1g, n1b, b1, b2, n2g, n2b, fb1, fb2, fc1, fc2, w1, w2, sems,
+):
+    copies = spread_layer(1 - core_ref[0], other, (fc1_out, fc2_out, w1_out, w2_out), (fc1, fc2, w1, w2), sems)
+    here = mine[1280:1296, :].astype(F32)
+    there = other[1280:1296, :].astype(F32)
+    for layer in range(LAYERS):
+        vec = jnp.where(core_ref[0] == layer, here, there)
         for row, ref in ((0, n1g), (1, n1b), (6, n2g), (7, n2b), (8, fb1), (9, fb2)):
             ref[layer : layer + 1, :] = vec[row : row + 1]
         b1[layer] = vec[2:4]
         b2[layer] = vec[4:6]
-
-    @pl.when(core_ref[0] == 0)
-    def _():
-        write(0, mine)
-        write(1, other)
-
-    @pl.when(core_ref[0] != 0)
-    def _():
-        write(1, mine)
-        write(0, other)
-
-
-def unpack(core, mine, other, d):
+    for c in copies:
+        c.wait()
+
+
+def unpack_shapes(d):
+    mix = jax.ShapeDtypeStruct((LAYERS, 2, 8, 64, 64), F32)
+    full = jax.ShapeDtypeStruct((LAYERS, d, d), F32)
+    big = (full, full, mix, mix)
+    scratch = [pltpu.VMEM(s.shape[1:], F32) for s in big] + [pltpu.SemaphoreType.DMA((4,))]
+    return big, scratch
+
+
+def unpack_mine(core, mine, d):
     vm = pl.BlockSpec(memory_space=pltpu.VMEM)
+    hbm = pl.BlockSpec(memory_space=pl.ANY)
+    big, scratch = unpack_shapes(d)
+    return pl.pallas_call(
+        spread_mine,
+        out_shape=big,
+        in_specs=[pl.BlockSpec(memory_space=pltpu.SMEM), vm],
+        out_specs=(hbm,) * 4,
+        scratch_shapes=scratch,
+        compiler_params=pltpu.CompilerParams(vmem_limit_bytes=16 * 1024 * 1024),
+        cost_estimate=pl.CostEstimate(flops=1 << 20, bytes_accessed=4 << 20, transcendentals=0),
+        name="spread_mine",
+    )(core, mine)
+
+
+def unpack(core, mine, other, d, big_in=None):
+    vm = pl.BlockSpec(memory_space=pltpu.VMEM)
+    hbm = pl.BlockSpec(memory_space=pl.ANY)
+    big, scratch = unpack_shapes(d)
     vec = jax.ShapeDtypeStruct((LAYERS, d), F32)
     pair = jax.ShapeDtypeStruct((LAYERS, 2, d), F32)
-    mix = jax.ShapeDtypeStruct((LAYERS, 2, 8, 64, 64), F32)
-    full = jax.ShapeDtypeStruct((LAYERS, d, d), F32)
-    return pl.pallas_call(
-        spread,
-        out_shape=(vec, vec, mix, pair, mix, pair, vec, vec, full, vec, full, vec),
-        in_specs=[pl.BlockSpec(memory_space=pltpu.SMEM), vm, vm],
-        out_specs=(vm,) * 12,
-        compiler_params=pltpu.CompilerParams(vmem_limit_bytes=32 * 1024 * 1024),
-        name="spread",
-    )(core, mine, other)
+    if big_in is None:
+        big_in = unpack_mine(core, mine, d)
+    fc1, fc2, w1, w2, n1g, n1b, b1, b2, n2g, n2b, fb1, fb2 = pl.pallas_call(
+        spread_other,
+        out_shape=big + (vec, vec, pair, pair, vec, vec, vec, vec),
+        in_specs=[pl.BlockSpec(memory_space=pltpu.SMEM), vm, vm] + [hbm] * 4,
+        out_specs=(hbm,) * 4 + (vm,) * 8,
+        scratch_shapes=scratch,
+        input_output_aliases={3: 0, 4: 1, 5: 2, 6: 3},
+        compiler_params=pltpu.CompilerParams(vmem_limit_bytes=16 * 1024 * 1024),
+        name="spread_other",
+    )(core, mine, other, *big_in)
+    return n1g, n1b, w1, b1, w2, b2, n2g, n2b, fc1, fb1, fc2, fb2
 
 
 def exchange(a, bit, count):

time: 111 us -> 109 us (0.982)
  waiting for transfers between devices: 39.2 us -> 30.6 us
  starting transfers between devices: 20.8 us -> 27.6 us
    ppermute x21, waiting for transfers between devices: 39.2 us -> 30.6 us  [exchange(): return lax.ppermute(a, AXES, [(i, i ^ bit) for i in range(count)])]
    ppermute x21, starting transfers between devices: 20.8 us -> 27.6 us  [exchange(): return lax.ppermute(a, AXES, [(i, i ^ bit) for i in range(count)])]
    pallas_call x1, Pallas kernels: 44.2 us -> 42.2 us  [local_step(): pl.pallas_call(kernel, out_shape=(jax.ShapeDtypeStruct((rows, d), BF), ja...]
    pallas_call x1 -> x2, Pallas kernels: 3.19 us -> 4.3 us  [the longest x1 2.46 us: unpack(): pl.pallas_call(spread_other, out_shape=big + (vec, vec, pair, pair, vec,...]
  transfers between devices with their start and end apart: 21 -> 21, of which waited for: 16 -> 15; matrix products, arithmetic and copies ran while one was open for 1% -> 1% of each run, Pallas kernels for 0% -> 2%
where the time goes in v1:
time: 109 us
  Pallas kernels  46.5 us (43%)
  waiting for transfers between devices  30.6 us (28%)
  starting transfers between devices  27.6 us (25%)
  other arithmetic  3.03 us (3%)
    pallas_call x1, Pallas kernels, local_step(): pl.pallas_call(kernel, out_shape=(jax.ShapeDtypeStruct((rows, d), BF), ja...  42.2 us
    ppermute x21, waiting for transfers between devices, exchange(): return lax.ppermute(a, AXES, [(i, i ^ bit) for i in range(count)])  30.6 us
    ppermute x21, starting transfers between devices, exchange(): return lax.ppermute(a, AXES, [(i, i ^ bit) for i in range(count)])  27.6 us
    pallas_call x1, Pallas kernels, unpack(): pl.pallas_call(spread_other, out_shape=big + (vec, vec, pair, pair, vec,...  2.46 us
    convert_element_type x9, other arithmetic, add(): return (a.astype(F32) + b.astype(F32)).astype(BF)  2.25 us
  transfers between devices with their start and end apart: 21, of which 15 were waited for; matrix products, arithmetic and copies ran while one was open for 1% of the time, Pallas kernels for 2%

profile of v1, /device:TPU:0, one launch (start us, length us, event | category | flops | bytes accessed | tf_op | source)
XLA Modules:
  0.0 108.8 jit_solution(16013622401857107631)
XLA Ops:
  0.7 42.2 %slab_step.1 = (bf16[1024,512]{1,0:T(8,128)(2,1)}, bf16[1024,512]{1,0:T(8,128)(2,1)}, bf16[1344,512]{1,0:T(8,128)(2,1)}, bf16[1344,512]{1,0:T(8,128)(2,1)}) custom-call(s32[16]{0:T(128)} %grid_ref.1, s32[3]{0:T(128)} %keep_ref.1, s32[1]{0:T(128)} %bitcast.core_ref, bf16[1024,512]{1,0:T(8,128)(2,1)} %x_hbm.1, bf16[1024,512]{1,0:T(8,128)(2,1)} %cot_hbm.1, ...), custom_call_target="tpu_custom_call" | custom-call | tf_op jit(solution)/shard_map/slab_step/pallas_call | solution.py:618
  42.8 0.5 collective-permute-start
  43.4 3.0 %collective-permute-done = bf16[1344,512]{1,0:T(8,128)(2,1)S(1)} collective-permute-done((bf16[1344,512]{1,0:T(8,128)(2,1)}, bf16[1344,512]{1,0:T(8,128)(2,1)S(1)}, u32[]{:S(2)}, u32[]{:S(2)}) %collective-permute-start) | collective-permute-done | bytes 1376288 | tf_op jit(solution)/shard_map/ppermute | solution.py:721
  46.3 1.7 %add_convert_fusion = bf16[1344,512]{1,0:T(8,128)(2,1)S(1)} fusion(bf16[1344,512]{1,0:T(8,128)(2,1)S(1)} %collective-permute-done, bf16[1344,512]{1,0:T(8,128)(2,1)} %get-tuple-element.36), kind=kLoop, calls=%fused_computation | loop fusion | flops 2752512 | bytes 4128768 | tf_op jit(solution)/shard_map/convert_element_type | solution.py:725
  48.0 0.1 broadcast_select_fusion.2
  48.1 4.2 %collective-permute-start.1 = (bf16[224,512]{1,0:T(8,128)(2,1)S(1)}, bf16[224,512]{1,0:T(8,128)(2,1)S(1)}, u32[]{:S(2)}, u32[]{:S(2)}) collective-permute-start(bf16[224,512]{1,0:T(8,128)(2,1)S(1)} %get-tuple-element.57), channel_id=1, source_target_pairs={{0,1},{1,0},{2,3},{3,2},{4,5},{5,4},{6,7},{7,6},{8,9},{9,8},{10,11... | collective-permute-start | bytes 688136 | tf_op jit(solution)/shard_map/ppermute | solution.py:721
  52.3 1.6 %collective-permute-start.7 = (bf16[224,512]{1,0:T(8,128)(2,1)S(1)}, bf16[224,512]{1,0:T(8,128)(2,1)S(1)}, u32[]{:S(2)}, u32[]{:S(2)}) collective-permute-start(bf16[224,512]{1,0:T(8,128)(2,1)S(1)} %get-tuple-element.58), channel_id=1, source_target_pairs={{0,4},{1,5},{2,6},{3,7},{4,0},{5,1},{6,2},{7,3},{8,12},{9,13},{10,... | collective-permute-start | bytes 688136 | tf_op jit(solution)/shard_map/ppermute | solution.py:721
  53.9 1.9 %collective-permute-start.4 = (bf16[224,512]{1,0:T(8,128)(2,1)S(1)}, bf16[224,512]{1,0:T(8,128)(2,1)S(1)}, u32[]{:S(2)}, u32[]{:S(2)}) collective-permute-start(bf16[224,512]{1,0:T(8,128)(2,1)S(1)} %get-tuple-element.59), channel_id=1, source_target_pairs={{0,2},{1,3},{2,0},{3,1},{4,6},{5,7},{6,4},{7,5},{8,10},{9,11},{10,... | collective-permute-start | bytes 688136 | tf_op jit(solution)/shard_map/ppermute | solution.py:721
  55.8 2.4 %collective-permute-done.1 = bf16[224,512]{1,0:T(8,128)(2,1)S(1)} collective-permute-done((bf16[224,512]{1,0:T(8,128)(2,1)S(1)}, bf16[224,512]{1,0:T(8,128)(2,1)S(1)}, u32[]{:S(2)}, u32[]{:S(2)}) %collective-permute-start.1) | collective-permute-done | bytes 229408 | tf_op jit(solution)/shard_map/ppermute | solution.py:721
  58.2 1.5 %collective-permute-done.7 = bf16[224,512]{1,0:T(8,128)(2,1)S(1)} collective-permute-done((bf16[224,512]{1,0:T(8,128)(2,1)S(1)}, bf16[224,512]{1,0:T(8,128)(2,1)S(1)}, u32[]{:S(2)}, u32[]{:S(2)}) %collective-permute-start.7) | collective-permute-done | bytes 229408 | tf_op jit(solution)/shard_map/ppermute | solution.py:721
  59.7 1.7 %collective-permute-done.4 = bf16[224,512]{1,0:T(8,128)(2,1)S(1)} collective-permute-done((bf16[224,512]{1,0:T(8,128)(2,1)S(1)}, bf16[224,512]{1,0:T(8,128)(2,1)S(1)}, u32[]{:S(2)}, u32[]{:S(2)}) %collective-permute-start.4) | collective-permute-done | bytes 229408 | tf_op jit(solution)/shard_map/ppermute | solution.py:721
  61.4 0.3 add_convert_fusion.3
  61.7 0.5 collective-permute-start.5
  62.3 0.4 collective-permute-start.8
  62.7 1.7 %collective-permute-start.2 = (bf16[112,512]{1,0:T(8,128)(2,1)S(1)}, bf16[112,512]{1,0:T(8,128)(2,1)S(1)}, u32[]{:S(2)}, u32[]{:S(2)}) collective-permute-start(bf16[112,512]{1,0:T(8,128)(2,1)S(1)} %broadcast_select_fusion.11), channel_id=1, source_target_pairs={{0,2},{1,3},{2,0},{3,1},{4,6},{5,7},{6,4},{7,5},{8,10},{9,11},{10,... | collective-permute-start | bytes 344072 | tf_op jit(solution)/shard_map/ppermute | solution.py:721
  64.4 2.1 %collective-permute-done.5 = bf16[112,512]{1,0:T(8,128)(2,1)S(1)} collective-permute-done((bf16[112,512]{1,0:T(8,128)(2,1)S(1)}, bf16[112,512]{1,0:T(8,128)(2,1)S(1)}, u32[]{:S(2)}, u32[]{:S(2)}) %collective-permute-start.5) | collective-permute-done | bytes 114720 | tf_op jit(solution)/shard_map/ppermute | solution.py:721
  66.6 0.4 collective-permute-start.6
  67.2 1.8 %collective-permute-start.9 = (bf16[56,512]{1,0:T(8,128)(2,1)S(1)}, bf16[56,512]{1,0:T(8,128)(2,1)S(1)}, u32[]{:S(2)}, u32[]{:S(2)}) collective-permute-start(bf16[56,512]{1,0:T(8,128)(2,1)S(1)} %broadcast_select_fusion.14), channel_id=1, source_target_pairs={{0,2},{1,3},{2,0},{3,1},{4,6},{5,7},{6,4},{7,5},{8,10},{9,11},{10,... | collective-permute-start | bytes 172040 | tf_op jit(solution)/shard_map/ppermute | solution.py:721
  69.1 2.2 %collective-permute-start.3 = (bf16[56,512]{1,0:T(8,128)(2,1)S(1)}, bf16[56,512]{1,0:T(8,128)(2,1)S(1)}, u32[]{:S(2)}, u32[]{:S(2)}) collective-permute-start(bf16[56,512]{1,0:T(8,128)(2,1)S(1)} %broadcast_select_fusion.20), channel_id=1, source_target_pairs={{0,4},{1,5},{2,6},{3,7},{4,0},{5,1},{6,2},{7,3},{8,12},{9,13},{10,... | collective-permute-start | bytes 172040 | tf_op jit(solution)/shard_map/ppermute | solution.py:721
  71.3 0.1 collective-permute-done.9
  71.5 2.0 %collective-permute-done.3 = bf16[56,512]{1,0:T(8,128)(2,1)S(1)} collective-permute-done((bf16[56,512]{1,0:T(8,128)(2,1)S(1)}, bf16[56,512]{1,0:T(8,128)(2,1)S(1)}, u32[]{:S(2)}, u32[]{:S(2)}) %collective-permute-start.3) | collective-permute-done | bytes 57376 | tf_op jit(solution)/shard_map/ppermute | solution.py:721
  73.5 4.0 %collective-permute-start.10 = (bf16[168,512]{1,0:T(8,128)(2,1)S(1)}, bf16[168,512]{1,0:T(8,128)(2,1)S(1)}, u32[]{:S(2)}, u32[]{:S(2)}) collective-permute-start(bf16[168,512]{1,0:T(8,128)(2,1)S(1)} %pad_maximum_fusion.3), channel_id=1, source_target_pairs={{0,8},{1,9},{2,10},{3,11},{4,12},{5,13},{6,14},{7,15},{8,0},{9,1},... | collective-permute-start | bytes 516104 | tf_op jit(solution)/shard_map/ppermute | solution.py:721
  77.5 5.2 %collective-permute-done.10 = bf16[168,512]{1,0:T(8,128)(2,1)S(1)} collective-permute-done((bf16[168,512]{1,0:T(8,128)(2,1)S(1)}, bf16[168,512]{1,0:T(8,128)(2,1)S(1)}, u32[]{:S(2)}, u32[]{:S(2)}) %collective-permute-start.10) | collective-permute-done | bytes 172064 | tf_op jit(solution)/shard_map/ppermute | solution.py:721
  82.8 0.4 collective-permute-start.17
  83.3 1.7 %collective-permute-start.14 = (bf16[56,512]{1,0:T(8,128)(2,1)S(1)}, bf16[56,512]{1,0:T(8,128)(2,1)S(1)}, u32[]{:S(2)}, u32[]{:S(2)}) collective-permute-start(bf16[56,512]{1,0:T(8,128)(2,1)S(1)} %get-tuple-element.77), channel_id=1, source_target_pairs={{0,1},{1,0},{2,3},{3,2},{4,5},{5,4},{6,7},{7,6},{8,9},{9,8},{10,11... | collective-permute-start | bytes 172040 | tf_op jit(solution)/shard_map/ppermute | solution.py:721
  84.9 0.5 collective-permute-start.11
  85.4 1.7 %collective-permute-done.17 = bf16[56,512]{1,0:T(8,128)(2,1)S(1)} collective-permute-done((bf16[56,512]{1,0:T(8,128)(2,1)S(1)}, bf16[56,512]{1,0:T(8,128)(2,1)S(1)}, u32[]{:S(2)}, u32[]{:S(2)}) %collective-permute-start.17) | collective-permute-done | bytes 57376 | tf_op jit(solution)/shard_map/ppermute | solution.py:721
  87.1 0.9 collective-permute-done.14
  88.0 1.1 %collective-permute-done.11 = bf16[56,512]{1,0:T(8,128)(2,1)S(1)} collective-permute-done((bf16[56,512]{1,0:T(8,128)(2,1)S(1)}, bf16[56,512]{1,0:T(8,128)(2,1)S(1)}, u32[]{:S(2)}, u32[]{:S(2)}) %collective-permute-start.11) | collective-permute-done | bytes 57376 | tf_op jit(solution)/shard_map/ppermute | solution.py:721
  89.1 0.5 collective-permute-start.15
  89.7 0.6 collective-permute-start.12
  90.3 1.6 %collective-permute-start.18 = (bf16[112,512]{1,0:T(8,128)(2,1)S(1)}, bf16[112,512]{1,0:T(8,128)(2,1)S(1)}, u32[]{:S(2)}, u32[]{:S(2)}) collective-permute-start(bf16[112,512]{1,0:T(8,128)(2,1)S(1)} %pad_maximum_fusion.6), channel_id=1, source_target_pairs={{0,1},{1,0},{2,3},{3,2},{4,5},{5,4},{6,7},{7,6},{8,9},{9,8},{10,11... | collective-permute-start | bytes 344072 | tf_op jit(solution)/shard_map/ppermute | solution.py:721
  91.9 3.1 %collective-permute-done.15 = bf16[112,512]{1,0:T(8,128)(2,1)S(1)} collective-permute-done((bf16[112,512]{1,0:T(8,128)(2,1)S(1)}, bf16[112,512]{1,0:T(8,128)(2,1)S(1)}, u32[]{:S(2)}, u32[]{:S(2)}) %collective-permute-start.15) | collective-permute-done | bytes 114720 | tf_op jit(solution)/shard_map/ppermute | solution.py:721
  95.1 0.7 collective-permute-start.16
  95.9 0.8 collective-permute-start.13
  96.8 1.4 %collective-permute-start.19 = (bf16[224,512]{1,0:T(8,128)(2,1)S(1)}, bf16[224,512]{1,0:T(8,128)(2,1)S(1)}, u32[]{:S(2)}, u32[]{:S(2)}) collective-permute-start(bf16[224,512]{1,0:T(8,128)(2,1)S(1)} %pad_maximum_fusion.2), channel_id=1, source_target_pairs={{0,4},{1,5},{2,6},{3,7},{4,0},{5,1},{6,2},{7,3},{8,12},{9,13},{10,... | collective-permute-start | bytes 688136 | tf_op jit(solution)/shard_map/ppermute | solution.py:721
  98.1 3.9 %collective-permute-done.13 = bf16[224,512]{1,0:T(8,128)(2,1)S(1)} collective-permute-done((bf16[224,512]{1,0:T(8,128)(2,1)S(1)}, bf16[224,512]{1,0:T(8,128)(2,1)S(1)}, u32[]{:S(2)}, u32[]{:S(2)}) %collective-permute-start.13) | collective-permute-done | bytes 229408 | tf_op jit(solution)/shard_map/ppermute | solution.py:721
  102.0 0.1 select_dynamic-update-slice_fusion.5
  102.0 0.1 select_dynamic-update-slice_fusion.4
  102.1 0.1 select_dynamic-update-slice_fusion.3
  102.2 0.1 select_dynamic-update-slice_fusion.2
  102.2 0.6 collective-permute-done.19
  102.8 0.1 select_dynamic-update-slice_fusion.1
  102.9 0.1 select_dynamic-update-slice_fusion.mine
  103.0 0.1 collective-permute-start.20
  103.0 1.8 %spread_mine.1 = (f32[2,512,512]{2,1,0:T(8,128)}, f32[2,512,512]{2,1,0:T(8,128)}, f32[2,2,8,64,64]{4,3,2,1,0:T(8,128)}, f32[2,2,8,64,64]{4,3,2,1,0:T(8,128)}) custom-call(s32[1]{0:T(128)} %bitcast.core_ref, bf16[1344,512]{1,0:T(8,128)(2,1)S(1)} %select_dynamic-update-slice_fusion.mine), custom_call_target="tpu_custom_call" | custom-call | flops 1048576 | bytes 4194304 | tf_op jit(solution)/shard_map/spread_mine/pallas_call | solution.py:687
  104.9 1.3 %collective-permute-done.20.other = bf16[1344,512]{1,0:T(8,128)(2,1)S(1)} collective-permute-done((bf16[1344,512]{1,0:T(8,128)(2,1)S(1)}, bf16[1344,512]{1,0:T(8,128)(2,1)S(1)}, u32[]{:S(2)}, u32[]{:S(2)}) %collective-permute-start.20) | collective-permute-done | bytes 1376288 | tf_op jit(solution)/shard_map/ppermute | solution.py:721
  106.2 2.5 %spread_other.1 = (f32[2,512,512]{2,1,0:T(8,128)}, f32[2,512,512]{2,1,0:T(8,128)}, f32[2,2,8,64,64]{4,3,2,1,0:T(8,128)}, f32[2,2,8,64,64]{4,3,2,1,0:T(8,128)}, f...) custom-call(s32[1]{0:T(128)} %bitcast.core_ref, ...), custom_call_target="tpu_custom_call", output_to_operand_aliasing={{0}: (3, {}), {1}: (4, {}), {2}: (5, {}), {3}: (6, {})} | custom-call | tf_op jit(solution)/shard_map/spread_other/pallas_call | solution.py:707
  (31 shorter events, 0.7 us)
Async XLA Ops:
  42.8 3.5 %collective-permute-start = (bf16[1344,512]{1,0:T(8,128)(2,1)}, bf16[1344,512]{1,0:T(8,128)(2,1)S(1)}, u32[]{:S(2)}, u32[]{:S(2)}) collective-permute-start(bf16[1344,512]{1,0:T(8,128)(2,1)} %get-tuple-element.37), channel_id=1, source_target_pairs={{0,16},{1,17},{2,18},{3,19},{4,20},{5,21},{6,22},{7,23},{8,24},{9,... | collective-permute-start | bytes 4128776 | tf_op jit(solution)/shard_map/ppermute | solution.py:721
  48.1 10.1 %collective-permute-start.1 = (bf16[224,512]{1,0:T(8,128)(2,1)S(1)}, bf16[224,512]{1,0:T(8,128)(2,1)S(1)}, u32[]{:S(2)}, u32[]{:S(2)}) collective-permute-start(bf16[224,512]{1,0:T(8,128)(2,1)S(1)} %get-tuple-element.57), channel_id=1, source_target_pairs={{0,1},{1,0},{2,3},{3,2},{4,5},{5,4},{6,7},{7,6},{8,9},{9,8},{10,11... | collective-permute-start | bytes 688136 | tf_op jit(solution)/shard_map/ppermute | solution.py:721
  52.3 7.4 %collective-permute-start.7 = (bf16[224,512]{1,0:T(8,128)(2,1)S(1)}, bf16[224,512]{1,0:T(8,128)(2,1)S(1)}, u32[]{:S(2)}, u32[]{:S(2)}) collective-permute-start(bf16[224,512]{1,0:T(8,128)(2,1)S(1)} %get-tuple-element.58), channel_id=1, source_target_pairs={{0,4},{1,5},{2,6},{3,7},{4,0},{5,1},{6,2},{7,3},{8,12},{9,13},{10,... | collective-permute-start | bytes 688136 | tf_op jit(solution)/shard_map/ppermute | solution.py:721
  53.9 7.5 %collective-permute-start.4 = (bf16[224,512]{1,0:T(8,128)(2,1)S(1)}, bf16[224,512]{1,0:T(8,128)(2,1)S(1)}, u32[]{:S(2)}, u32[]{:S(2)}) collective-permute-start(bf16[224,512]{1,0:T(8,128)(2,1)S(1)} %get-tuple-element.59), channel_id=1, source_target_pairs={{0,2},{1,3},{2,0},{3,1},{4,6},{5,7},{6,4},{7,5},{8,10},{9,11},{10,... | collective-permute-start | bytes 688136 | tf_op jit(solution)/shard_map/ppermute | solution.py:721
  61.7 4.9 %collective-permute-start.5 = (bf16[112,512]{1,0:T(8,128)(2,1)S(1)}, bf16[112,512]{1,0:T(8,128)(2,1)S(1)}, u32[]{:S(2)}, u32[]{:S(2)}) collective-permute-start(bf16[112,512]{1,0:T(8,128)(2,1)S(1)} %broadcast_select_fusion.8), channel_id=1, source_target_pairs={{0,4},{1,5},{2,6},{3,7},{4,0},{5,1},{6,2},{7,3},{8,12},{9,13},{10,... | collective-permute-start | bytes 344072 | tf_op jit(solution)/shard_map/ppermute | solution.py:721
  62.3 4.9 %collective-permute-start.8 = (bf16[112,512]{1,0:T(8,128)(2,1)S(1)}, bf16[112,512]{1,0:T(8,128)(2,1)S(1)}, u32[]{:S(2)}, u32[]{:S(2)}) collective-permute-start(bf16[112,512]{1,0:T(8,128)(2,1)S(1)} %broadcast_select_fusion.5), channel_id=1, source_target_pairs={{0,1},{1,0},{2,3},{3,2},{4,5},{5,4},{6,7},{7,6},{8,9},{9,8},{10,11... | collective-permute-start | bytes 344072 | tf_op jit(solution)/shard_map/ppermute | solution.py:721
  62.7 6.3 %collective-permute-start.2 = (bf16[112,512]{1,0:T(8,128)(2,1)S(1)}, bf16[112,512]{1,0:T(8,128)(2,1)S(1)}, u32[]{:S(2)}, u32[]{:S(2)}) collective-permute-start(bf16[112,512]{1,0:T(8,128)(2,1)S(1)} %broadcast_select_fusion.11), channel_id=1, source_target_pairs={{0,2},{1,3},{2,0},{3,1},{4,6},{5,7},{6,4},{7,5},{8,10},{9,11},{10,... | collective-permute-start | bytes 344072 | tf_op jit(solution)/shard_map/ppermute | solution.py:721
  66.6 4.7 %collective-permute-start.6 = (bf16[56,512]{1,0:T(8,128)(2,1)S(1)}, bf16[56,512]{1,0:T(8,128)(2,1)S(1)}, u32[]{:S(2)}, u32[]{:S(2)}) collective-permute-start(bf16[56,512]{1,0:T(8,128)(2,1)S(1)} %broadcast_select_fusion.17), channel_id=1, source_target_pairs={{0,1},{1,0},{2,3},{3,2},{4,5},{5,4},{6,7},{7,6},{8,9},{9,8},{10,11... | collective-permute-start | bytes 172040 | tf_op jit(solution)/shard_map/ppermute | solution.py:721
  67.2 4.2 %collective-permute-start.9 = (bf16[56,512]{1,0:T(8,128)(2,1)S(1)}, bf16[56,512]{1,0:T(8,128)(2,1)S(1)}, u32[]{:S(2)}, u32[]{:S(2)}) collective-permute-start(bf16[56,512]{1,0:T(8,128)(2,1)S(1)} %broadcast_select_fusion.14), channel_id=1, source_target_pairs={{0,2},{1,3},{2,0},{3,1},{4,6},{5,7},{6,4},{7,5},{8,10},{9,11},{10,... | collective-permute-start | bytes 172040 | tf_op jit(solution)/shard_map/ppermute | solution.py:721
  69.1 4.4 %collective-permute-start.3 = (bf16[56,512]{1,0:T(8,128)(2,1)S(1)}, bf16[56,512]{1,0:T(8,128)(2,1)S(1)}, u32[]{:S(2)}, u32[]{:S(2)}) collective-permute-start(bf16[56,512]{1,0:T(8,128)(2,1)S(1)} %broadcast_select_fusion.20), channel_id=1, source_target_pairs={{0,4},{1,5},{2,6},{3,7},{4,0},{5,1},{6,2},{7,3},{8,12},{9,13},{10,... | collective-permute-start | bytes 172040 | tf_op jit(solution)/shard_map/ppermute | solution.py:721
  73.5 9.2 %collective-permute-start.10 = (bf16[168,512]{1,0:T(8,128)(2,1)S(1)}, bf16[168,512]{1,0:T(8,128)(2,1)S(1)}, u32[]{:S(2)}, u32[]{:S(2)}) collective-permute-start(bf16[168,512]{1,0:T(8,128)(2,1)S(1)} %pad_maximum_fusion.3), channel_id=1, source_target_pairs={{0,8},{1,9},{2,10},{3,11},{4,12},{5,13},{6,14},{7,15},{8,0},{9,1},... | collective-permute-start | bytes 516104 | tf_op jit(solution)/shard_map/ppermute | solution.py:721
  82.8 4.2 %collective-permute-start.17 = (bf16[56,512]{1,0:T(8,128)(2,1)S(1)}, bf16[56,512]{1,0:T(8,128)(2,1)S(1)}, u32[]{:S(2)}, u32[]{:S(2)}) collective-permute-start(bf16[56,512]{1,0:T(8,128)(2,1)S(1)} %get-tuple-element.76), channel_id=1, source_target_pairs={{0,2},{1,3},{2,0},{3,1},{4,6},{5,7},{6,4},{7,5},{8,10},{9,11},{10,... | collective-permute-start | bytes 172040 | tf_op jit(solution)/shard_map/ppermute | solution.py:721
  83.3 4.7 %collective-permute-start.14 = (bf16[56,512]{1,0:T(8,128)(2,1)S(1)}, bf16[56,512]{1,0:T(8,128)(2,1)S(1)}, u32[]{:S(2)}, u32[]{:S(2)}) collective-permute-start(bf16[56,512]{1,0:T(8,128)(2,1)S(1)} %get-tuple-element.77), channel_id=1, source_target_pairs={{0,1},{1,0},{2,3},{3,2},{4,5},{5,4},{6,7},{7,6},{8,9},{9,8},{10,11... | collective-permute-start | bytes 172040 | tf_op jit(solution)/shard_map/ppermute | solution.py:721
  84.9 4.2 %collective-permute-start.11 = (bf16[56,512]{1,0:T(8,128)(2,1)S(1)}, bf16[56,512]{1,0:T(8,128)(2,1)S(1)}, u32[]{:S(2)}, u32[]{:S(2)}) collective-permute-start(bf16[56,512]{1,0:T(8,128)(2,1)S(1)} %get-tuple-element.78), channel_id=1, source_target_pairs={{0,4},{1,5},{2,6},{3,7},{4,0},{5,1},{6,2},{7,3},{8,12},{9,13},{10,... | collective-permute-start | bytes 172040 | tf_op jit(solution)/shard_map/ppermute | solution.py:721
  89.1 5.9 %collective-permute-start.15 = (bf16[112,512]{1,0:T(8,128)(2,1)S(1)}, bf16[112,512]{1,0:T(8,128)(2,1)S(1)}, u32[]{:S(2)}, u32[]{:S(2)}) collective-permute-start(bf16[112,512]{1,0:T(8,128)(2,1)S(1)} %pad_maximum_fusion.5), channel_id=1, source_target_pairs={{0,4},{1,5},{2,6},{3,7},{4,0},{5,1},{6,2},{7,3},{8,12},{9,13},{10,... | collective-permute-start | bytes 344072 | tf_op jit(solution)/shard_map/ppermute | solution.py:721
  89.7 6.1 %collective-permute-start.12 = (bf16[112,512]{1,0:T(8,128)(2,1)S(1)}, bf16[112,512]{1,0:T(8,128)(2,1)S(1)}, u32[]{:S(2)}, u32[]{:S(2)}) collective-permute-start(bf16[112,512]{1,0:T(8,128)(2,1)S(1)} %pad_maximum_fusion.4), channel_id=1, source_target_pairs={{0,2},{1,3},{2,0},{3,1},{4,6},{5,7},{6,4},{7,5},{8,10},{9,11},{10,... | collective-permute-start | bytes 344072 | tf_op jit(solution)/shard_map/ppermute | solution.py:721
  90.3 6.3 %collective-permute-start.18 = (bf16[112,512]{1,0:T(8,128)(2,1)S(1)}, bf16[112,512]{1,0:T(8,128)(2,1)S(1)}, u32[]{:S(2)}, u32[]{:S(2)}) collective-permute-start(bf16[112,512]{1,0:T(8,128)(2,1)S(1)} %pad_maximum_fusion.6), channel_id=1, source_target_pairs={{0,1},{1,0},{2,3},{3,2},{4,5},{5,4},{6,7},{7,6},{8,9},{9,8},{10,11... | collective-permute-start | bytes 344072 | tf_op jit(solution)/shard_map/ppermute | solution.py:721
  95.1 7.0 %collective-permute-start.16 = (bf16[224,512]{1,0:T(8,128)(2,1)S(1)}, bf16[224,512]{1,0:T(8,128)(2,1)S(1)}, u32[]{:S(2)}, u32[]{:S(2)}) collective-permute-start(bf16[224,512]{1,0:T(8,128)(2,1)S(1)} %pad_maximum_fusion.1), channel_id=1, source_target_pairs={{0,2},{1,3},{2,0},{3,1},{4,6},{5,7},{6,4},{7,5},{8,10},{9,11},{10,... | collective-permute-start | bytes 688136 | tf_op jit(solution)/shard_map/ppermute | solution.py:721
  95.9 6.1 %collective-permute-start.13 = (bf16[224,512]{1,0:T(8,128)(2,1)S(1)}, bf16[224,512]{1,0:T(8,128)(2,1)S(1)}, u32[]{:S(2)}, u32[]{:S(2)}) collective-permute-start(bf16[224,512]{1,0:T(8,128)(2,1)S(1)} %pad_maximum_fusion), channel_id=1, source_target_pairs={{0,1},{1,0},{2,3},{3,2},{4,5},{5,4},{6,7},{7,6},{8,9},{9,8},{10,11... | collective-permute-start | bytes 688136 | tf_op jit(solution)/shard_map/ppermute | solution.py:721
  96.8 6.1 %collective-permute-start.19 = (bf16[224,512]{1,0:T(8,128)(2,1)S(1)}, bf16[224,512]{1,0:T(8,128)(2,1)S(1)}, u32[]{:S(2)}, u32[]{:S(2)}) collective-permute-start(bf16[224,512]{1,0:T(8,128)(2,1)S(1)} %pad_maximum_fusion.2), channel_id=1, source_target_pairs={{0,4},{1,5},{2,6},{3,7},{4,0},{5,1},{6,2},{7,3},{8,12},{9,13},{10,... | collective-permute-start | bytes 688136 | tf_op jit(solution)/shard_map/ppermute | solution.py:721
  103.0 3.2 %collective-permute-start.20 = (bf16[1344,512]{1,0:T(8,128)(2,1)S(1)}, bf16[1344,512]{1,0:T(8,128)(2,1)S(1)}, u32[]{:S(2)}, u32[]{:S(2)}) collective-permute-start(bf16[1344,512]{1,0:T(8,128)(2,1)S(1)} %select_dynamic-update-slice_fusion.mine), channel_id=1, source_target_pairs={{0,16},{1,17},{2,18},{3,19},{4,20},{5,21},{6,22},{7,23},{8,24},{9,... | collective-permute-start | bytes 4128776 | tf_op jit(solution)/shard_map/ppermute | solution.py:721

commit v2 on v1

--- a/solution.py
+++ b/solution.py
@@ -209,7 +209,7 @@
 def kernel(
     grid_ref, keep_ref, core_ref, x_hbm, cot_hbm,
     n1g, n1b, w1_hbm, b1, w2_hbm, b2, n2g, n2b, fc1_hbm, fb1, fc2_hbm, fb2,
-    out_hbm, xg_hbm, mine_hbm, other_hbm,
+    out_hbm, xg_hbm, m0, m1, m2, t0, t1, t2,
     x_ref, cot_ref, w1, w2, fc1, fc2, out_ref, grads_ref, sems,
     at, st, k1, k3, nm, nb, w1g, w2g,
     xh1, rs1, hu, ul, z, o, da, ds, pq, xh2, rs2, v, act, dp,
@@ -571,16 +571,20 @@
         grads_ref[pl.ds(pl.multiple_of((layer ^ core_ref[0]) * PER, PER) + 1280, PER - 1280), :] = t.astype(BF)
 
     vectors(1)
-    mine_copy = copy(8, grads_ref.at[pl.ds(0, PER)], mine_hbm)
-    other_copy = copy(9, grads_ref.at[pl.ds(PER, PER)], other_hbm)
+    sends = [
+        copy(8 + k, grads_ref.at[pl.ds(row, PER // 3)], dst)
+        for k, (row, dst) in enumerate(
+            (((3 * half + c) * (PER // 3), dst) for half, refs in ((1, (t0, t1, t2)), (0, (m0, m1, m2))) for c, dst in enumerate(refs))
+        )
+    ]
     xg_copy = copy(7, xg_ref, xg_hbm)
     vectors(0)
-    other_copy.start()
-    mine_copy.start()
+    for c in sends:
+        c.start()
     xg_copy.start()
     out_copy.wait()
-    other_copy.wait()
-    mine_copy.wait()
+    for c in sends:
+        c.wait()
     xg_copy.wait()
 
 
@@ -600,7 +604,7 @@
         pltpu.VMEM((rows, d), BF), pltpu.VMEM((rows, d), BF),
         pltpu.VMEM(w1r.shape, BF), pltpu.VMEM(w2r.shape, BF), pltpu.VMEM(fc1.shape, BF), pltpu.VMEM(fc2.shape, BF),
         pltpu.VMEM((rows, d), BF), pltpu.VMEM((LAYERS * PER, d), BF),
-        pltpu.SemaphoreType.DMA((10,)),
+        pltpu.SemaphoreType.DMA((14,)),
         pltpu.VMEM((rows, rows), BF), pltpu.VMEM((rows, rows), BF),
         pltpu.VMEM((2, slots, 256), BF), pltpu.VMEM((2, slots, 256), BF),
         pltpu.VMEM((slots, 128), BF), pltpu.VMEM((slots, 128), BF),
@@ -620,11 +624,10 @@
         out_shape=(
             jax.ShapeDtypeStruct((rows, d), BF),
             jax.ShapeDtypeStruct((rows, d), BF),
-            jax.ShapeDtypeStruct((PER, d), BF),
-            jax.ShapeDtypeStruct((PER, d), BF),
-        ),
+        )
+        + (jax.ShapeDtypeStruct((PER // 3, d), BF),) * 6,
         in_specs=[sm, sm, sm, hbm, hbm, vm, vm, hbm, vm, hbm, vm, vm, vm, hbm, vm, hbm, vm],
-        out_specs=(hbm,) * 4,
+        out_specs=(hbm,) * 8,
         scratch_shapes=scratch,
         compiler_params=pltpu.CompilerParams(vmem_limit_bytes=58 * 1024 * 1024),
         name="slab_step",
@@ -634,34 +637,39 @@
 AXES = ("dp", "modes")
 
 
-def spread_layer(layer, src, outs, bufs, sems):
+def spread_layer(layer, parts, outs, bufs, sems):
     fc1, fc2, w1, w2 = bufs
-    fc1[...] = src[0:512, :].astype(F32)
+    p0, p1, p2 = parts
+    n = PER // 3
     copies = [pltpu.make_async_copy(buf, out.at[layer], sems.at[k]) for k, (buf, out) in enumerate(zip(bufs, outs))]
+    fc1[0:n, :] = p0[...].astype(F32)
+    fc1[n:512, :] = p1[0 : 512 - n, :].astype(F32)
     copies[0].start()
-    fc2[...] = src[512:1024, :].astype(F32)
+    fc2[0 : 2 * n - 512, :] = p1[512 - n : n, :].astype(F32)
+    fc2[2 * n - 512 : 512, :] = p2[0 : 1024 - 2 * n, :].astype(F32)
     copies[1].start()
-    for k, (ref, base) in enumerate(((w1, 1024), (w2, 1152))):
+    for k, (ref, base) in enumerate(((w1, 1024 - 2 * n), (w2, 1152 - 2 * n))):
         for part in range(2):
-            block = src[base + part * 64 : base + part * 64 + 64, :].astype(F32)
+            block = p2[base + part * 64 : base + part * 64 + 64, :].astype(F32)
             for j in range(8):
                 ref[part, j] = block[:, j * 64 : j * 64 + 64]
         copies[2 + k].start()
     return copies
 
 
-def spread_mine(core_ref, mine, fc1_out, fc2_out, w1_out, w2_out, fc1, fc2, w1, w2, sems):
-    for c in spread_layer(core_ref[0], mine, (fc1_out, fc2_out, w1_out, w2_out), (fc1, fc2, w1, w2), sems):
+def spread_mine(core_ref, a0, a1, a2, fc1_out, fc2_out, w1_out, w2_out, fc1, fc2, w1, w2, sems):
+    for c in spread_layer(core_ref[0], (a0, a1, a2), (fc1_out, fc2_out, w1_out, w2_out), (fc1, fc2, w1, w2), sems):
         c.wait()
 
 
 def spread_other(
-    core_ref, mine, other, fc1_in, fc2_in, w1_in, w2_in,
+    core_ref, a0, a1, a2, c0, c1, c2, fc1_in, fc2_in, w1_in, w2_in,
     fc1_out, fc2_out, w1_out, w2_out, n1g, n1b, b1, b2, n2g, n2b, fb1, fb2, fc1, fc2, w1, w2, sems,
 ):
-    copies = spread_layer(1 - core_ref[0], other, (fc1_out, fc2_out, w1_out, w2_out), (fc1, fc2, w1, w2), sems)
-    here = mine[1280:1296, :].astype(F32)
-    there = other[1280:1296, :].astype(F32)
+    copies = spread_layer(1 - core_ref[0], (c0, c1, c2), (fc1_out, fc2_out, w1_out, w2_out), (fc1, fc2, w1, w2), sems)
+    row = 1280 - 2 * (PER // 3)
+    here = a2[row : row + 16, :].astype(F32)
+    there = c2[row : row + 16, :].astype(F32)
     for layer in range(LAYERS):
         vec = jnp.where(core_ref[0] == layer, here, there)
         for row, ref in ((0, n1g), (1, n1b), (6, n2g), (7, n2b), (8, fb1), (9, fb2)):
@@ -687,13 +695,13 @@
     return pl.pallas_call(
         spread_mine,
         out_shape=big,
-        in_specs=[pl.BlockSpec(memory_space=pltpu.SMEM), vm],
+        in_specs=[pl.BlockSpec(memory_space=pltpu.SMEM), vm, vm, vm],
         out_specs=(hbm,) * 4,
         scratch_shapes=scratch,
         compiler_params=pltpu.CompilerParams(vmem_limit_bytes=16 * 1024 * 1024),
         cost_estimate=pl.CostEstimate(flops=1 << 20, bytes_accessed=4 << 20, transcendentals=0),
         name="spread_mine",
-    )(core, mine)
+    )(core, *mine)
 
 
 def unpack(core, mine, other, d, big_in=None):
@@ -707,13 +715,13 @@
     fc1, fc2, w1, w2, n1g, n1b, b1, b2, n2g, n2b, fb1, fb2 = pl.pallas_call(
         spread_other,
         out_shape=big + (vec, vec, pair, pair, vec, vec, vec, vec),
-        in_specs=[pl.BlockSpec(memory_space=pltpu.SMEM), vm, vm] + [hbm] * 4,
+        in_specs=[pl.BlockSpec(memory_space=pltpu.SMEM)] + [vm] * 6 + [hbm] * 4,
         out_specs=(hbm,) * 4 + (vm,) * 8,
         scratch_shapes=scratch,
-        input_output_aliases={3: 0, 4: 1, 5: 2, 6: 3},
+        input_output_aliases={7: 0, 8: 1, 9: 2, 10: 3},
         compiler_params=pltpu.CompilerParams(vmem_limit_bytes=16 * 1024 * 1024),
         name="spread_other",
-    )(core, mine, other, *big_in)
+    )(core, *mine, *other, *big_in)
     return n1g, n1b, w1, b1, w2, b2, n2g, n2b, fc1, fb1, fc2, fb2
 
 
@@ -728,11 +736,10 @@
 def all_sum(mine, other, count):
     me = lax.axis_index(AXES)
     top = count // 2
-    mine = add(mine, exchange(other, top, count))
     bits = [1 << k for k in range(top.bit_length() - 1)]
     orders = [[bits[(c + k) % 3] for k in range(3)] for c in range(3)]
-    third = PER // 3
-    parts = [mine[c * third : (c + 1) * third] for c in range(3)]
+    gots = [exchange(t, top, count) for t in other]
+    parts = [add(m, got) for m, got in zip(mine, gots)]
     for k in range(3):
         moved = []
         for c in range(3):
@@ -754,8 +761,7 @@
             low_part = jnp.where(high, gots[c], parts[c])
             high_part = jnp.where(high, parts[c], gots[c])
             parts[c] = jnp.concatenate([low_part, high_part])
-    mine = jnp.concatenate(parts)
-    return mine, exchange(mine, top, count)
+    return parts, [exchange(p, top, count) for p in parts]
 
 
 def solution(mesh):
@@ -763,9 +769,9 @@
 
     def on_device(*args):
         core = lax.axis_index("dp").astype(jnp.int32).reshape(1)
-        out, x_grad, mine, other = local_step(core, *args)
-        mine, other = all_sum(mine, other, count)
-        return (out, x_grad) + tuple(unpack(core, mine, other, mine.shape[1]))
+        out, x_grad, *parts = local_step(core, *args)
+        mine, other = all_sum(parts[:3], parts[3:], count)
+        return (out, x_grad) + tuple(unpack(core, mine, other, out.shape[1]))
 
     rows = P(AXES, None)
     return jax.shard_map(

time: 109 us -> 106 us (0.972)
  waiting for transfers between devices: 30.6 us -> 26.3 us
    ppermute x21 -> x25, waiting for transfers between devices: 30.6 us -> 26.3 us  [exchange(): return lax.ppermute(a, AXES, [(i, i ^ bit) for i in range(count)])]
    ppermute x21 -> x25, starting transfers between devices: 27.6 us -> 28.6 us  [exchange(): return lax.ppermute(a, AXES, [(i, i ^ bit) for i in range(count)])]
    convert_element_type x9 -> x13, other arithmetic: 2.25 us -> 1.88 us  [add(): return (a.astype(F32) + b.astype(F32)).astype(BF)]
  transfers between devices with their start and end apart: 21 -> 25, of which waited for: 15 -> 15; matrix products, arithmetic and copies ran while one was open for 1% -> 2% of each run, Pallas kernels for 2% -> 2%
where the time goes in v2:
time: 106 us; the launch traced here: 105 us
  Pallas kernels  46.7 us (44%)
  starting transfers between devices  28.6 us (27%)
  waiting for transfers between devices  26.3 us (25%)
  other arithmetic  2.65 us (2%)
  between operations  1.17 us (1%)
    pallas_call x1, Pallas kernels, local_step(): pl.pallas_call(kernel, out_shape=(jax.ShapeDtypeStruct((rows, d), BF), ja...  42.4 us
    ppermute x25, starting transfers between devices, exchange(): return lax.ppermute(a, AXES, [(i, i ^ bit) for i in range(count)])  28.6 us
    ppermute x25, waiting for transfers between devices, exchange(): return lax.ppermute(a, AXES, [(i, i ^ bit) for i in range(count)])  26.3 us
    pallas_call x1, Pallas kernels, unpack(): pl.pallas_call(spread_other, out_shape=big + (vec, vec, pair, pair, vec,...  2.47 us
  transfers between devices with their start and end apart: 25, of which 15 were waited for; matrix products, arithmetic and copies ran while one was open for 2% of the time, Pallas kernels for 2%

profile of v2, /device:TPU:0, one launch (start us, length us, event | category | flops | bytes accessed | tf_op | source)
XLA Modules:
  0.0 105.4 jit_solution(14552668678164607445)
XLA Ops:
  0.7 42.4 %slab_step.1 = (bf16[1024,512]{1,0:T(8,128)(2,1)}, bf16[1024,512]{1,0:T(8,128)(2,1)}, bf16[448,512]{1,0:T(8,128)(2,1)}, bf16[448,512]{1,0:T(8,128)(2,1)}, bf16[4...) custom-call(s32[16]{0:T(128)} %grid_ref.1, s32[3]{0:T(128)} %keep_ref.1, ...), custom_call_target="tpu_custom_call" | custom-call | tf_op jit(solution)/shard_map/slab_step/pallas_call | solution.py:622
  43.1 1.8 %collective-permute-start = (bf16[448,512]{1,0:T(8,128)(2,1)}, bf16[448,512]{1,0:T(8,128)(2,1)S(1)}, u32[]{:S(2)}, u32[]{:S(2)}) collective-permute-start(bf16[448,512]{1,0:T(8,128)(2,1)} %get-tuple-element.41), channel_id=1, source_target_pairs={{0,16},{1,17},{2,18},{3,19},{4,20},{5,21},{6,22},{7,23},{8,24},{9,... | collective-permute-start | bytes 1376264 | tf_op jit(solution)/shard_map/ppermute | solution.py:729
  45.0 0.4 collective-permute-start.8
  45.4 1.1 %collective-permute-done = bf16[448,512]{1,0:T(8,128)(2,1)S(1)} collective-permute-done((bf16[448,512]{1,0:T(8,128)(2,1)}, bf16[448,512]{1,0:T(8,128)(2,1)S(1)}, u32[]{:S(2)}, u32[]{:S(2)}) %collective-permute-start) | collective-permute-done | bytes 458784 | tf_op jit(solution)/shard_map/ppermute | solution.py:729
  46.6 1.1 %add_convert_fusion.2 = bf16[448,512]{1,0:T(8,128)(2,1)S(1)} fusion(bf16[448,512]{1,0:T(8,128)(2,1)S(1)} %collective-permute-done, bf16[448,512]{1,0:T(8,128)(2,1)} %get-tuple-element.40), kind=kLoop, calls=%fused_computation.2 | loop fusion | flops 917504 | bytes 1376256 | tf_op jit(solution)/shard_map/convert_element_type | solution.py:733
  47.7 3.4 %collective-permute-start.1 = (bf16[224,512]{1,0:T(8,128)(2,1)S(1)}, bf16[224,512]{1,0:T(8,128)(2,1)S(1)}, u32[]{:S(2)}, u32[]{:S(2)}) collective-permute-start(bf16[224,512]{1,0:T(8,128)(2,1)S(1)} %broadcast_select_fusion.8), channel_id=1, source_target_pairs={{0,1},{1,0},{2,3},{3,2},{4,5},{5,4},{6,7},{7,6},{8,9},{9,8},{10,11... | collective-permute-start | bytes 688136 | tf_op jit(solution)/shard_map/ppermute | solution.py:729
  51.1 0.1 add_convert_fusion.1
  51.3 1.1 %collective-permute-start.5 = (bf16[224,512]{1,0:T(8,128)(2,1)S(1)}, bf16[224,512]{1,0:T(8,128)(2,1)S(1)}, u32[]{:S(2)}, u32[]{:S(2)}) collective-permute-start(bf16[224,512]{1,0:T(8,128)(2,1)S(1)} %broadcast_select_fusion.5), channel_id=1, source_target_pairs={{0,2},{1,3},{2,0},{3,1},{4,6},{5,7},{6,4},{7,5},{8,10},{9,11},{10,... | collective-permute-start | bytes 688136 | tf_op jit(solution)/shard_map/ppermute | solution.py:729
  52.4 0.1 add_convert_fusion
  52.5 1.6 %collective-permute-start.9 = (bf16[224,512]{1,0:T(8,128)(2,1)S(1)}, bf16[224,512]{1,0:T(8,128)(2,1)S(1)}, u32[]{:S(2)}, u32[]{:S(2)}) collective-permute-start(bf16[224,512]{1,0:T(8,128)(2,1)S(1)} %broadcast_select_fusion.2), channel_id=1, source_target_pairs={{0,4},{1,5},{2,6},{3,7},{4,0},{5,1},{6,2},{7,3},{8,12},{9,13},{10,... | collective-permute-start | bytes 688136 | tf_op jit(solution)/shard_map/ppermute | solution.py:729
  54.1 2.9 %collective-permute-done.1 = bf16[224,512]{1,0:T(8,128)(2,1)S(1)} collective-permute-done((bf16[224,512]{1,0:T(8,128)(2,1)S(1)}, bf16[224,512]{1,0:T(8,128)(2,1)S(1)}, u32[]{:S(2)}, u32[]{:S(2)}) %collective-permute-start.1) | collective-permute-done | bytes 229408 | tf_op jit(solution)/shard_map/ppermute | solution.py:729
  57.0 0.1 add_convert_fusion.5
  57.1 1.3 %collective-permute-start.2 = (bf16[112,512]{1,0:T(8,128)(2,1)S(1)}, bf16[112,512]{1,0:T(8,128)(2,1)S(1)}, u32[]{:S(2)}, u32[]{:S(2)}) collective-permute-start(bf16[112,512]{1,0:T(8,128)(2,1)S(1)} %broadcast_select_fusion.17), channel_id=1, source_target_pairs={{0,2},{1,3},{2,0},{3,1},{4,6},{5,7},{6,4},{7,5},{8,10},{9,11},{10,... | collective-permute-start | bytes 344072 | tf_op jit(solution)/shard_map/ppermute | solution.py:729
  58.4 0.3 collective-permute-done.5
  58.7 0.1 add_convert_fusion.4
  58.8 1.9 %collective-permute-start.6 = (bf16[112,512]{1,0:T(8,128)(2,1)S(1)}, bf16[112,512]{1,0:T(8,128)(2,1)S(1)}, u32[]{:S(2)}, u32[]{:S(2)}) collective-permute-start(bf16[112,512]{1,0:T(8,128)(2,1)S(1)} %broadcast_select_fusion.14), channel_id=1, source_target_pairs={{0,4},{1,5},{2,6},{3,7},{4,0},{5,1},{6,2},{7,3},{8,12},{9,13},{10,... | collective-permute-start | bytes 344072 | tf_op jit(solution)/shard_map/ppermute | solution.py:729
  60.7 0.1 add_convert_fusion.3
  60.9 1.2 %collective-permute-start.10 = (bf16[112,512]{1,0:T(8,128)(2,1)S(1)}, bf16[112,512]{1,0:T(8,128)(2,1)S(1)}, u32[]{:S(2)}, u32[]{:S(2)}) collective-permute-start(bf16[112,512]{1,0:T(8,128)(2,1)S(1)} %broadcast_select_fusion.11), channel_id=1, source_target_pairs={{0,1},{1,0},{2,3},{3,2},{4,5},{5,4},{6,7},{7,6},{8,9},{9,8},{10,11... | collective-permute-start | bytes 344072 | tf_op jit(solution)/shard_map/ppermute | solution.py:729
  62.2 1.3 %collective-permute-start.3 = (bf16[56,512]{1,0:T(8,128)(2,1)S(1)}, bf16[56,512]{1,0:T(8,128)(2,1)S(1)}, u32[]{:S(2)}, u32[]{:S(2)}) collective-permute-start(bf16[56,512]{1,0:T(8,128)(2,1)S(1)} %broadcast_select_fusion.26), channel_id=1, source_target_pairs={{0,4},{1,5},{2,6},{3,7},{4,0},{5,1},{6,2},{7,3},{8,12},{9,13},{10,... | collective-permute-start | bytes 172040 | tf_op jit(solution)/shard_map/ppermute | solution.py:729
  63.5 0.3 collective-permute-done.6
  63.9 1.9 %collective-permute-start.7 = (bf16[56,512]{1,0:T(8,128)(2,1)S(1)}, bf16[56,512]{1,0:T(8,128)(2,1)S(1)}, u32[]{:S(2)}, u32[]{:S(2)}) collective-permute-start(bf16[56,512]{1,0:T(8,128)(2,1)S(1)} %broadcast_select_fusion.23), channel_id=1, source_target_pairs={{0,1},{1,0},{2,3},{3,2},{4,5},{5,4},{6,7},{7,6},{8,9},{9,8},{10,11... | collective-permute-start | bytes 172040 | tf_op jit(solution)/shard_map/ppermute | solution.py:729
  65.8 0.5 collective-permute-done.10
  66.4 1.0 collective-permute-start.11
  67.4 0.7 collective-permute-done.7
  68.2 2.5 %collective-permute-done.11 = bf16[56,512]{1,0:T(8,128)(2,1)S(1)} collective-permute-done((bf16[56,512]{1,0:T(8,128)(2,1)S(1)}, bf16[56,512]{1,0:T(8,128)(2,1)S(1)}, u32[]{:S(2)}, u32[]{:S(2)}) %collective-permute-start.11) | collective-permute-done | bytes 57376 | tf_op jit(solution)/shard_map/ppermute | solution.py:729
  70.7 2.7 %collective-permute-start.12 = (bf16[168,512]{1,0:T(8,128)(2,1)S(1)}, bf16[168,512]{1,0:T(8,128)(2,1)S(1)}, u32[]{:S(2)}, u32[]{:S(2)}) collective-permute-start(bf16[168,512]{1,0:T(8,128)(2,1)S(1)} %pad_maximum_fusion.6), channel_id=1, source_target_pairs={{0,8},{1,9},{2,10},{3,11},{4,12},{5,13},{6,14},{7,15},{8,0},{9,1},... | collective-permute-start | bytes 516104 | tf_op jit(solution)/shard_map/ppermute | solution.py:729
  73.3 5.6 %collective-permute-done.12 = bf16[168,512]{1,0:T(8,128)(2,1)S(1)} collective-permute-done((bf16[168,512]{1,0:T(8,128)(2,1)S(1)}, bf16[168,512]{1,0:T(8,128)(2,1)S(1)}, u32[]{:S(2)}, u32[]{:S(2)}) %collective-permute-start.12) | collective-permute-done | bytes 172064 | tf_op jit(solution)/shard_map/ppermute | solution.py:729
  79.1 0.5 collective-permute-start.19
  79.6 0.8 collective-permute-start.16
  80.4 3.2 %collective-permute-done.19 = bf16[56,512]{1,0:T(8,128)(2,1)S(1)} collective-permute-done((bf16[56,512]{1,0:T(8,128)(2,1)S(1)}, bf16[56,512]{1,0:T(8,128)(2,1)S(1)}, u32[]{:S(2)}, u32[]{:S(2)}) %collective-permute-start.19) | collective-permute-done | bytes 57376 | tf_op jit(solution)/shard_map/ppermute | solution.py:729
  83.6 0.4 collective-permute-done.16
  84.0 0.6 collective-permute-done.13
  84.7 1.3 %collective-permute-start.20 = (bf16[112,512]{1,0:T(8,128)(2,1)S(1)}, bf16[112,512]{1,0:T(8,128)(2,1)S(1)}, u32[]{:S(2)}, u32[]{:S(2)}) collective-permute-start(bf16[112,512]{1,0:T(8,128)(2,1)S(1)} %pad_maximum_fusion.9), channel_id=1, source_target_pairs={{0,1},{1,0},{2,3},{3,2},{4,5},{5,4},{6,7},{7,6},{8,9},{9,8},{10,11... | collective-permute-start | bytes 344072 | tf_op jit(solution)/shard_map/ppermute | solution.py:729
  86.0 1.6 %collective-permute-start.14 = (bf16[112,512]{1,0:T(8,128)(2,1)S(1)}, bf16[112,512]{1,0:T(8,128)(2,1)S(1)}, u32[]{:S(2)}, u32[]{:S(2)}) collective-permute-start(bf16[112,512]{1,0:T(8,128)(2,1)S(1)} %pad_maximum_fusion.7), channel_id=1, source_target_pairs={{0,2},{1,3},{2,0},{3,1},{4,6},{5,7},{6,4},{7,5},{8,10},{9,11},{10,... | collective-permute-start | bytes 344072 | tf_op jit(solution)/shard_map/ppermute | solution.py:729
  87.7 2.5 %collective-permute-done.17 = bf16[112,512]{1,0:T(8,128)(2,1)S(1)} collective-permute-done((bf16[112,512]{1,0:T(8,128)(2,1)S(1)}, bf16[112,512]{1,0:T(8,128)(2,1)S(1)}, u32[]{:S(2)}, u32[]{:S(2)}) %collective-permute-start.17) | collective-permute-done | bytes 114720 | tf_op jit(solution)/shard_map/ppermute | solution.py:729
  90.2 0.6 collective-permute-done.20
  90.8 0.1 broadcast_select_fusion.10
  90.9 1.6 %collective-permute-start.21 = (bf16[224,512]{1,0:T(8,128)(2,1)S(1)}, bf16[224,512]{1,0:T(8,128)(2,1)S(1)}, u32[]{:S(2)}, u32[]{:S(2)}) collective-permute-start(bf16[224,512]{1,0:T(8,128)(2,1)S(1)} %pad_maximum_fusion.5), channel_id=1, source_target_pairs={{0,4},{1,5},{2,6},{3,7},{4,0},{5,1},{6,2},{7,3},{8,12},{9,13},{10,... | collective-permute-start | bytes 688136 | tf_op jit(solution)/shard_map/ppermute | solution.py:729
  92.6 1.3 %collective-permute-start.15 = (bf16[224,512]{1,0:T(8,128)(2,1)S(1)}, bf16[224,512]{1,0:T(8,128)(2,1)S(1)}, u32[]{:S(2)}, u32[]{:S(2)}) collective-permute-start(bf16[224,512]{1,0:T(8,128)(2,1)S(1)} %pad_maximum_fusion.3), channel_id=1, source_target_pairs={{0,1},{1,0},{2,3},{3,2},{4,5},{5,4},{6,7},{7,6},{8,9},{9,8},{10,11... | collective-permute-start | bytes 688136 | tf_op jit(solution)/shard_map/ppermute | solution.py:729
  93.9 0.9 collective-permute-start.18
  94.8 2.2 %collective-permute-done.21 = bf16[224,512]{1,0:T(8,128)(2,1)S(1)} collective-permute-done((bf16[224,512]{1,0:T(8,128)(2,1)S(1)}, bf16[224,512]{1,0:T(8,128)(2,1)S(1)}, u32[]{:S(2)}, u32[]{:S(2)}) %collective-permute-start.21) | collective-permute-done | bytes 229408 | tf_op jit(solution)/shard_map/ppermute | solution.py:729
  97.0 0.1 broadcast_select_fusion.1
  97.2 2.8 %collective-permute-done.18 = bf16[224,512]{1,0:T(8,128)(2,1)S(1)} collective-permute-done((bf16[224,512]{1,0:T(8,128)(2,1)S(1)}, bf16[224,512]{1,0:T(8,128)(2,1)S(1)}, u32[]{:S(2)}, u32[]{:S(2)}) %collective-permute-start.18) | collective-permute-done | bytes 229408 | tf_op jit(solution)/shard_map/ppermute | solution.py:729
  100.0 0.1 broadcast_select_fusion.4
  100.2 0.1 broadcast_select_fusion.7
  100.4 0.6 collective-permute-start.22
  100.9 1.8 %spread_mine.1 = (f32[2,512,512]{2,1,0:T(8,128)}, f32[2,512,512]{2,1,0:T(8,128)}, f32[2,2,8,64,64]{4,3,2,1,0:T(8,128)}, f32[2,2,8,64,64]{4,3,2,1,0:T(8,128)}) custom-call(s32[1]{0:T(128)} %bitcast.core_ref, bf16[448,512]{1,0:T(8,128)(2,1)S(1)} %pad_maximum_fusion.a0, bf16[448,512]{1,0:T(8,128)(2,1)S(1)} %pad_maximum_fusion.1.a1, ...), custom_call_target="tpu_custom_call" | custom-call | flops 1048576 | bytes 4194304 | tf_op jit(solution)/shard_map/spread_mine/pallas_call | solution.py:695
  102.8 2.5 %spread_other.1 = (f32[2,512,512]{2,1,0:T(8,128)}, f32[2,512,512]{2,1,0:T(8,128)}, f32[2,2,8,64,64]{4,3,2,1,0:T(8,128)}, f32[2,2,8,64,64]{4,3,2,1,0:T(8,128)}, f...) custom-call(s32[1]{0:T(128)} %bitcast.core_ref, ...), custom_call_target="tpu_custom_call", output_to_operand_aliasing={{0}: (7, {}), {1}: (8, {}), {2}: (9, {}), {3}: (10, {})} | custom-call | tf_op jit(solution)/shard_map/spread_other/pallas_call | solution.py:715
  (48 shorter events, 1.0 us)
Async XLA Ops:
  43.1 8.0 %copy-start.1 = (bf16[448,512]{1,0:T(8,128)(2,1)S(1)}, bf16[448,512]{1,0:T(8,128)(2,1)}, u32[]{:S(2)}) copy-start(bf16[448,512]{1,0:T(8,128)(2,1)} %get-tuple-element.42) | copy-start | bytes 1376260
  43.1 9.3 %copy-start = (bf16[448,512]{1,0:T(8,128)(2,1)S(1)}, bf16[448,512]{1,0:T(8,128)(2,1)}, u32[]{:S(2)}) copy-start(bf16[448,512]{1,0:T(8,128)(2,1)} %get-tuple-element.44) | copy-start | bytes 1376260
  43.1 3.4 %collective-permute-start = (bf16[448,512]{1,0:T(8,128)(2,1)}, bf16[448,512]{1,0:T(8,128)(2,1)S(1)}, u32[]{:S(2)}, u32[]{:S(2)}) collective-permute-start(bf16[448,512]{1,0:T(8,128)(2,1)} %get-tuple-element.41), channel_id=1, source_target_pairs={{0,16},{1,17},{2,18},{3,19},{4,20},{5,21},{6,22},{7,23},{8,24},{9,... | collective-permute-start | bytes 1376264 | tf_op jit(solution)/shard_map/ppermute | solution.py:729
  44.9 6.2 %collective-permute-start.4 = (bf16[448,512]{1,0:T(8,128)(2,1)}, bf16[448,512]{1,0:T(8,128)(2,1)S(1)}, u32[]{:S(2)}, u32[]{:S(2)}) collective-permute-start(bf16[448,512]{1,0:T(8,128)(2,1)} %get-tuple-element.43), channel_id=1, source_target_pairs={{0,16},{1,17},{2,18},{3,19},{4,20},{5,21},{6,22},{7,23},{8,24},{9,... | collective-permute-start | bytes 1376264 | tf_op jit(solution)/shard_map/ppermute | solution.py:729
  45.0 7.4 %collective-permute-start.8 = (bf16[448,512]{1,0:T(8,128)(2,1)}, bf16[448,512]{1,0:T(8,128)(2,1)S(1)}, u32[]{:S(2)}, u32[]{:S(2)}) collective-permute-start(bf16[448,512]{1,0:T(8,128)(2,1)} %get-tuple-element.45), channel_id=1, source_target_pairs={{0,16},{1,17},{2,18},{3,19},{4,20},{5,21},{6,22},{7,23},{8,24},{9,... | collective-permute-start | bytes 1376264 | tf_op jit(solution)/shard_map/ppermute | solution.py:729
  47.7 9.3 %collective-permute-start.1 = (bf16[224,512]{1,0:T(8,128)(2,1)S(1)}, bf16[224,512]{1,0:T(8,128)(2,1)S(1)}, u32[]{:S(2)}, u32[]{:S(2)}) collective-permute-start(bf16[224,512]{1,0:T(8,128)(2,1)S(1)} %broadcast_select_fusion.8), channel_id=1, source_target_pairs={{0,1},{1,0},{2,3},{3,2},{4,5},{5,4},{6,7},{7,6},{8,9},{9,8},{10,11... | collective-permute-start | bytes 688136 | tf_op jit(solution)/shard_map/ppermute | solution.py:729
  51.3 7.4 %collective-permute-start.5 = (bf16[224,512]{1,0:T(8,128)(2,1)S(1)}, bf16[224,512]{1,0:T(8,128)(2,1)S(1)}, u32[]{:S(2)}, u32[]{:S(2)}) collective-permute-start(bf16[224,512]{1,0:T(8,128)(2,1)S(1)} %broadcast_select_fusion.5), channel_id=1, source_target_pairs={{0,2},{1,3},{2,0},{3,1},{4,6},{5,7},{6,4},{7,5},{8,10},{9,11},{10,... | collective-permute-start | bytes 688136 | tf_op jit(solution)/shard_map/ppermute | solution.py:729
  52.5 8.2 %collective-permute-start.9 = (bf16[224,512]{1,0:T(8,128)(2,1)S(1)}, bf16[224,512]{1,0:T(8,128)(2,1)S(1)}, u32[]{:S(2)}, u32[]{:S(2)}) collective-permute-start(bf16[224,512]{1,0:T(8,128)(2,1)S(1)} %broadcast_select_fusion.2), channel_id=1, source_target_pairs={{0,4},{1,5},{2,6},{3,7},{4,0},{5,1},{6,2},{7,3},{8,12},{9,13},{10,... | collective-permute-start | bytes 688136 | tf_op jit(solution)/shard_map/ppermute | solution.py:729
  57.1 5.0 %collective-permute-start.2 = (bf16[112,512]{1,0:T(8,128)(2,1)S(1)}, bf16[112,512]{1,0:T(8,128)(2,1)S(1)}, u32[]{:S(2)}, u32[]{:S(2)}) collective-permute-start(bf16[112,512]{1,0:T(8,128)(2,1)S(1)} %broadcast_select_fusion.17), channel_id=1, source_target_pairs={{0,2},{1,3},{2,0},{3,1},{4,6},{5,7},{6,4},{7,5},{8,10},{9,11},{10,... | collective-permute-start | bytes 344072 | tf_op jit(solution)/shard_map/ppermute | solution.py:729
  58.8 5.0 %collective-permute-start.6 = (bf16[112,512]{1,0:T(8,128)(2,1)S(1)}, bf16[112,512]{1,0:T(8,128)(2,1)S(1)}, u32[]{:S(2)}, u32[]{:S(2)}) collective-permute-start(bf16[112,512]{1,0:T(8,128)(2,1)S(1)} %broadcast_select_fusion.14), channel_id=1, source_target_pairs={{0,4},{1,5},{2,6},{3,7},{4,0},{5,1},{6,2},{7,3},{8,12},{9,13},{10,... | collective-permute-start | bytes 344072 | tf_op jit(solution)/shard_map/ppermute | solution.py:729
  60.9 5.5 %collective-permute-start.10 = (bf16[112,512]{1,0:T(8,128)(2,1)S(1)}, bf16[112,512]{1,0:T(8,128)(2,1)S(1)}, u32[]{:S(2)}, u32[]{:S(2)}) collective-permute-start(bf16[112,512]{1,0:T(8,128)(2,1)S(1)} %broadcast_select_fusion.11), channel_id=1, source_target_pairs={{0,1},{1,0},{2,3},{3,2},{4,5},{5,4},{6,7},{7,6},{8,9},{9,8},{10,11... | collective-permute-start | bytes 344072 | tf_op jit(solution)/shard_map/ppermute | solution.py:729
  62.2 5.2 %collective-permute-start.3 = (bf16[56,512]{1,0:T(8,128)(2,1)S(1)}, bf16[56,512]{1,0:T(8,128)(2,1)S(1)}, u32[]{:S(2)}, u32[]{:S(2)}) collective-permute-start(bf16[56,512]{1,0:T(8,128)(2,1)S(1)} %broadcast_select_fusion.26), channel_id=1, source_target_pairs={{0,4},{1,5},{2,6},{3,7},{4,0},{5,1},{6,2},{7,3},{8,12},{9,13},{10,... | collective-permute-start | bytes 172040 | tf_op jit(solution)/shard_map/ppermute | solution.py:729
  63.9 4.2 %collective-permute-start.7 = (bf16[56,512]{1,0:T(8,128)(2,1)S(1)}, bf16[56,512]{1,0:T(8,128)(2,1)S(1)}, u32[]{:S(2)}, u32[]{:S(2)}) collective-permute-start(bf16[56,512]{1,0:T(8,128)(2,1)S(1)} %broadcast_select_fusion.23), channel_id=1, source_target_pairs={{0,1},{1,0},{2,3},{3,2},{4,5},{5,4},{6,7},{7,6},{8,9},{9,8},{10,11... | collective-permute-start | bytes 172040 | tf_op jit(solution)/shard_map/ppermute | solution.py:729
  66.4 4.2 %collective-permute-start.11 = (bf16[56,512]{1,0:T(8,128)(2,1)S(1)}, bf16[56,512]{1,0:T(8,128)(2,1)S(1)}, u32[]{:S(2)}, u32[]{:S(2)}) collective-permute-start(bf16[56,512]{1,0:T(8,128)(2,1)S(1)} %broadcast_select_fusion.20), channel_id=1, source_target_pairs={{0,2},{1,3},{2,0},{3,1},{4,6},{5,7},{6,4},{7,5},{8,10},{9,11},{10,... | collective-permute-start | bytes 172040 | tf_op jit(solution)/shard_map/ppermute | solution.py:729
  70.7 8.3 %collective-permute-start.12 = (bf16[168,512]{1,0:T(8,128)(2,1)S(1)}, bf16[168,512]{1,0:T(8,128)(2,1)S(1)}, u32[]{:S(2)}, u32[]{:S(2)}) collective-permute-start(bf16[168,512]{1,0:T(8,128)(2,1)S(1)} %pad_maximum_fusion.6), channel_id=1, source_target_pairs={{0,8},{1,9},{2,10},{3,11},{4,12},{5,13},{6,14},{7,15},{8,0},{9,1},... | collective-permute-start | bytes 516104 | tf_op jit(solution)/shard_map/ppermute | solution.py:729
  79.1 4.5 %collective-permute-start.19 = (bf16[56,512]{1,0:T(8,128)(2,1)S(1)}, bf16[56,512]{1,0:T(8,128)(2,1)S(1)}, u32[]{:S(2)}, u32[]{:S(2)}) collective-permute-start(bf16[56,512]{1,0:T(8,128)(2,1)S(1)} %get-tuple-element.84), channel_id=1, source_target_pairs={{0,2},{1,3},{2,0},{3,1},{4,6},{5,7},{6,4},{7,5},{8,10},{9,11},{10,... | collective-permute-start | bytes 172040 | tf_op jit(solution)/shard_map/ppermute | solution.py:729
  79.6 4.4 %collective-permute-start.16 = (bf16[56,512]{1,0:T(8,128)(2,1)S(1)}, bf16[56,512]{1,0:T(8,128)(2,1)S(1)}, u32[]{:S(2)}, u32[]{:S(2)}) collective-permute-start(bf16[56,512]{1,0:T(8,128)(2,1)S(1)} %get-tuple-element.85), channel_id=1, source_target_pairs={{0,1},{1,0},{2,3},{3,2},{4,5},{5,4},{6,7},{7,6},{8,9},{9,8},{10,11... | collective-permute-start | bytes 172040 | tf_op jit(solution)/shard_map/ppermute | solution.py:729
  80.4 4.2 %collective-permute-start.13 = (bf16[56,512]{1,0:T(8,128)(2,1)S(1)}, bf16[56,512]{1,0:T(8,128)(2,1)S(1)}, u32[]{:S(2)}, u32[]{:S(2)}) collective-permute-start(bf16[56,512]{1,0:T(8,128)(2,1)S(1)} %get-tuple-element.86), channel_id=1, source_target_pairs={{0,4},{1,5},{2,6},{3,7},{4,0},{5,1},{6,2},{7,3},{8,12},{9,13},{10,... | collective-permute-start | bytes 172040 | tf_op jit(solution)/shard_map/ppermute | solution.py:729
  84.6 5.5 %collective-permute-start.17 = (bf16[112,512]{1,0:T(8,128)(2,1)S(1)}, bf16[112,512]{1,0:T(8,128)(2,1)S(1)}, u32[]{:S(2)}, u32[]{:S(2)}) collective-permute-start(bf16[112,512]{1,0:T(8,128)(2,1)S(1)} %pad_maximum_fusion.8), channel_id=1, source_target_pairs={{0,4},{1,5},{2,6},{3,7},{4,0},{5,1},{6,2},{7,3},{8,12},{9,13},{10,... | collective-permute-start | bytes 344072 | tf_op jit(solution)/shard_map/ppermute | solution.py:729
  84.7 6.1 %collective-permute-start.20 = (bf16[112,512]{1,0:T(8,128)(2,1)S(1)}, bf16[112,512]{1,0:T(8,128)(2,1)S(1)}, u32[]{:S(2)}, u32[]{:S(2)}) collective-permute-start(bf16[112,512]{1,0:T(8,128)(2,1)S(1)} %pad_maximum_fusion.9), channel_id=1, source_target_pairs={{0,1},{1,0},{2,3},{3,2},{4,5},{5,4},{6,7},{7,6},{8,9},{9,8},{10,11... | collective-permute-start | bytes 344072 | tf_op jit(solution)/shard_map/ppermute | solution.py:729
  86.0 6.5 %collective-permute-start.14 = (bf16[112,512]{1,0:T(8,128)(2,1)S(1)}, bf16[112,512]{1,0:T(8,128)(2,1)S(1)}, u32[]{:S(2)}, u32[]{:S(2)}) collective-permute-start(bf16[112,512]{1,0:T(8,128)(2,1)S(1)} %pad_maximum_fusion.7), channel_id=1, source_target_pairs={{0,2},{1,3},{2,0},{3,1},{4,6},{5,7},{6,4},{7,5},{8,10},{9,11},{10,... | collective-permute-start | bytes 344072 | tf_op jit(solution)/shard_map/ppermute | solution.py:729
  90.9 6.1 %collective-permute-start.21 = (bf16[224,512]{1,0:T(8,128)(2,1)S(1)}, bf16[224,512]{1,0:T(8,128)(2,1)S(1)}, u32[]{:S(2)}, u32[]{:S(2)}) collective-permute-start(bf16[224,512]{1,0:T(8,128)(2,1)S(1)} %pad_maximum_fusion.5), channel_id=1, source_target_pairs={{0,4},{1,5},{2,6},{3,7},{4,0},{5,1},{6,2},{7,3},{8,12},{9,13},{10,... | collective-permute-start | bytes 688136 | tf_op jit(solution)/shard_map/ppermute | solution.py:729
  92.6 7.7 %collective-permute-start.15 = (bf16[224,512]{1,0:T(8,128)(2,1)S(1)}, bf16[224,512]{1,0:T(8,128)(2,1)S(1)}, u32[]{:S(2)}, u32[]{:S(2)}) collective-permute-start(bf16[224,512]{1,0:T(8,128)(2,1)S(1)} %pad_maximum_fusion.3), channel_id=1, source_target_pairs={{0,1},{1,0},{2,3},{3,2},{4,5},{5,4},{6,7},{7,6},{8,9},{9,8},{10,11... | collective-permute-start | bytes 688136 | tf_op jit(solution)/shard_map/ppermute | solution.py:729
  93.9 6.1 %collective-permute-start.18 = (bf16[224,512]{1,0:T(8,128)(2,1)S(1)}, bf16[224,512]{1,0:T(8,128)(2,1)S(1)}, u32[]{:S(2)}, u32[]{:S(2)}) collective-permute-start(bf16[224,512]{1,0:T(8,128)(2,1)S(1)} %pad_maximum_fusion.4), channel_id=1, source_target_pairs={{0,2},{1,3},{2,0},{3,1},{4,6},{5,7},{6,4},{7,5},{8,10},{9,11},{10,... | collective-permute-start | bytes 688136 | tf_op jit(solution)/shard_map/ppermute | solution.py:729
  97.1 5.7 %collective-permute-start.24 = (bf16[448,512]{1,0:T(8,128)(2,1)S(1)}, bf16[448,512]{1,0:T(8,128)(2,1)S(1)}, u32[]{:S(2)}, u32[]{:S(2)}) collective-permute-start(bf16[448,512]{1,0:T(8,128)(2,1)S(1)} %pad_maximum_fusion.2.a2), channel_id=1, source_target_pairs={{0,16},{1,17},{2,18},{3,19},{4,20},{5,21},{6,22},{7,23},{8,24},{9,... | collective-permute-start | bytes 1376264 | tf_op jit(solution)/shard_map/ppermute | solution.py:729
  100.1 2.6 %collective-permute-start.23 = (bf16[448,512]{1,0:T(8,128)(2,1)S(1)}, bf16[448,512]{1,0:T(8,128)(2,1)S(1)}, u32[]{:S(2)}, u32[]{:S(2)}) collective-permute-start(bf16[448,512]{1,0:T(8,128)(2,1)S(1)} %pad_maximum_fusion.1.a1), channel_id=1, source_target_pairs={{0,16},{1,17},{2,18},{3,19},{4,20},{5,21},{6,22},{7,23},{8,24},{9,... | collective-permute-start | bytes 1376264 | tf_op jit(solution)/shard_map/ppermute | solution.py:729
  100.4 2.4 %collective-permute-start.22 = (bf16[448,512]{1,0:T(8,128)(2,1)S(1)}, bf16[448,512]{1,0:T(8,128)(2,1)S(1)}, u32[]{:S(2)}, u32[]{:S(2)}) collective-permute-start(bf16[448,512]{1,0:T(8,128)(2,1)S(1)} %pad_maximum_fusion.a0), channel_id=1, source_target_pairs={{0,16},{1,17},{2,18},{3,19},{4,20},{5,21},{6,22},{7,23},{8,24},{9,... | collective-permute-start | bytes 1376264 | tf_op jit(solution)/shard_map/ppermute | solution.py:729

commit v3 on v2

--- a/solution.py
+++ b/solution.py
@@ -749,11 +749,8 @@
             send = jnp.where(high, parts[c][:n], parts[c][n:])
             moved.append((keep, exchange(send, orders[c][k], count)))
         parts = [add(keep, got) for keep, got in moved]
-    n = parts[0].shape[0]
-    last = jnp.concatenate(parts)
     for bit in bits[3:]:
-        last = add(last, exchange(last, bit, count))
-    parts = [last[c * n : (c + 1) * n] for c in range(3)]
+        parts = [add(p, exchange(p, bit, count)) for p in parts]
     for k in reversed(range(3)):
         gots = [exchange(parts[c], orders[c][k], count) for c in range(3)]
         for c in range(3):

time: 106 us -> 98.2 us (0.926)
  waiting for transfers between devices: 26.3 us -> 12.2 us
  starting transfers between devices: 28.6 us -> 34.9 us
    ppermute x25 -> x27, waiting for transfers between devices: 26.3 us -> 12.2 us  [exchange(): return lax.ppermute(a, AXES, [(i, i ^ bit) for i in range(count)])]
    ppermute x25 -> x27, starting transfers between devices: 28.6 us -> 34.9 us  [exchange(): return lax.ppermute(a, AXES, [(i, i ^ bit) for i in range(count)])]
  transfers between devices with their start and end apart: 25 -> 27, of which waited for: 15 -> 12; matrix products, arithmetic and copies ran while one was open for 2% -> 3% of each run, Pallas kernels for 2% -> 2%
where the time goes in v3:
time: 98.2 us; the launch traced here: 97.7 us
  Pallas kernels  46.7 us (48%)
  starting transfers between devices  34.9 us (36%)
  waiting for transfers between devices  12.2 us (12%)
  other arithmetic  2.64 us (3%)
  between operations  1.18 us (1%)
    pallas_call x1, Pallas kernels, local_step(): pl.pallas_call(kernel, out_shape=(jax.ShapeDtypeStruct((rows, d), BF), ja...  42.4 us
    ppermute x27, starting transfers between devices, exchange(): return lax.ppermute(a, AXES, [(i, i ^ bit) for i in range(count)])  34.9 us
    ppermute x27, waiting for transfers between devices, exchange(): return lax.ppermute(a, AXES, [(i, i ^ bit) for i in range(count)])  12.2 us
    pallas_call x1, Pallas kernels, unpack(): pl.pallas_call(spread_other, out_shape=big + (vec, vec, pair, pair, vec,...  2.47 us
  transfers between devices with their start and end apart: 27, of which 12 were waited for; matrix products, arithmetic and copies ran while one was open for 3% of the time, Pallas kernels for 2%

profile of v3, /device:TPU:0, one launch (start us, length us, event | category | flops | bytes accessed | tf_op | source)
XLA Modules:
  0.0 97.7 jit_solution(3034802222812072278)
XLA Ops:
  0.7 42.4 %slab_step.1 = (bf16[1024,512]{1,0:T(8,128)(2,1)}, bf16[1024,512]{1,0:T(8,128)(2,1)}, bf16[448,512]{1,0:T(8,128)(2,1)}, bf16[448,512]{1,0:T(8,128)(2,1)}, bf16[4...) custom-call(s32[16]{0:T(128)} %grid_ref.1, s32[3]{0:T(128)} %keep_ref.1, ...), custom_call_target="tpu_custom_call" | custom-call | tf_op jit(solution)/shard_map/slab_step/pallas_call | solution.py:622
  43.1 0.5 collective-permute-start
  43.6 0.1 collective-permute-start.8
  43.7 0.4 collective-permute-start.16
  44.2 1.1 %collective-permute-done = bf16[448,512]{1,0:T(8,128)(2,1)S(1)} collective-permute-done((bf16[448,512]{1,0:T(8,128)(2,1)}, bf16[448,512]{1,0:T(8,128)(2,1)S(1)}, u32[]{:S(2)}, u32[]{:S(2)}) %collective-permute-start) | collective-permute-done | bytes 458784 | tf_op jit(solution)/shard_map/ppermute | solution.py:729
  45.3 1.1 %add_convert_fusion.2 = bf16[448,512]{1,0:T(8,128)(2,1)S(1)} fusion(bf16[448,512]{1,0:T(8,128)(2,1)S(1)} %collective-permute-done, bf16[448,512]{1,0:T(8,128)(2,1)} %get-tuple-element.40), kind=kLoop, calls=%fused_computation.2 | loop fusion | flops 917504 | bytes 1376256 | tf_op jit(solution)/shard_map/convert_element_type | solution.py:733
  46.5 4.7 %collective-permute-start.1 = (bf16[224,512]{1,0:T(8,128)(2,1)S(1)}, bf16[224,512]{1,0:T(8,128)(2,1)S(1)}, u32[]{:S(2)}, u32[]{:S(2)}) collective-permute-start(bf16[224,512]{1,0:T(8,128)(2,1)S(1)} %broadcast_select_fusion.8), channel_id=1, source_target_pairs={{0,1},{1,0},{2,3},{3,2},{4,5},{5,4},{6,7},{7,6},{8,9},{9,8},{10,11... | collective-permute-start | bytes 688136 | tf_op jit(solution)/shard_map/ppermute | solution.py:729
  51.1 0.1 add_convert_fusion.1
  51.3 1.6 %collective-permute-start.9 = (bf16[224,512]{1,0:T(8,128)(2,1)S(1)}, bf16[224,512]{1,0:T(8,128)(2,1)S(1)}, u32[]{:S(2)}, u32[]{:S(2)}) collective-permute-start(bf16[224,512]{1,0:T(8,128)(2,1)S(1)} %broadcast_select_fusion.5), channel_id=1, source_target_pairs={{0,2},{1,3},{2,0},{3,1},{4,6},{5,7},{6,4},{7,5},{8,10},{9,11},{10,... | collective-permute-start | bytes 688136 | tf_op jit(solution)/shard_map/ppermute | solution.py:729
  52.9 0.1 add_convert_fusion
  53.0 1.2 %collective-permute-start.17 = (bf16[224,512]{1,0:T(8,128)(2,1)S(1)}, bf16[224,512]{1,0:T(8,128)(2,1)S(1)}, u32[]{:S(2)}, u32[]{:S(2)}) collective-permute-start(bf16[224,512]{1,0:T(8,128)(2,1)S(1)} %broadcast_select_fusion.2), channel_id=1, source_target_pairs={{0,4},{1,5},{2,6},{3,7},{4,0},{5,1},{6,2},{7,3},{8,12},{9,13},{10,... | collective-permute-start | bytes 688136 | tf_op jit(solution)/shard_map/ppermute | solution.py:729
  54.2 2.8 %collective-permute-done.1 = bf16[224,512]{1,0:T(8,128)(2,1)S(1)} collective-permute-done((bf16[224,512]{1,0:T(8,128)(2,1)S(1)}, bf16[224,512]{1,0:T(8,128)(2,1)S(1)}, u32[]{:S(2)}, u32[]{:S(2)}) %collective-permute-start.1) | collective-permute-done | bytes 229408 | tf_op jit(solution)/shard_map/ppermute | solution.py:729
  57.0 0.1 add_convert_fusion.5
  57.1 2.0 %collective-permute-start.2 = (bf16[112,512]{1,0:T(8,128)(2,1)S(1)}, bf16[112,512]{1,0:T(8,128)(2,1)S(1)}, u32[]{:S(2)}, u32[]{:S(2)}) collective-permute-start(bf16[112,512]{1,0:T(8,128)(2,1)S(1)} %broadcast_select_fusion.17), channel_id=1, source_target_pairs={{0,2},{1,3},{2,0},{3,1},{4,6},{5,7},{6,4},{7,5},{8,10},{9,11},{10,... | collective-permute-start | bytes 344072 | tf_op jit(solution)/shard_map/ppermute | solution.py:729
  59.2 0.1 add_convert_fusion.4
  59.3 1.7 %collective-permute-start.10 = (bf16[112,512]{1,0:T(8,128)(2,1)S(1)}, bf16[112,512]{1,0:T(8,128)(2,1)S(1)}, u32[]{:S(2)}, u32[]{:S(2)}) collective-permute-start(bf16[112,512]{1,0:T(8,128)(2,1)S(1)} %broadcast_select_fusion.14), channel_id=1, source_target_pairs={{0,4},{1,5},{2,6},{3,7},{4,0},{5,1},{6,2},{7,3},{8,12},{9,13},{10,... | collective-permute-start | bytes 344072 | tf_op jit(solution)/shard_map/ppermute | solution.py:729
  61.0 0.1 add_convert_fusion.3
  61.1 0.9 collective-permute-start.18
  61.9 0.1 collective-permute-done.2
  62.1 2.1 %collective-permute-start.3 = (bf16[56,512]{1,0:T(8,128)(2,1)S(1)}, bf16[56,512]{1,0:T(8,128)(2,1)S(1)}, u32[]{:S(2)}, u32[]{:S(2)}) collective-permute-start(bf16[56,512]{1,0:T(8,128)(2,1)S(1)} %broadcast_select_fusion.26), channel_id=1, source_target_pairs={{0,4},{1,5},{2,6},{3,7},{4,0},{5,1},{6,2},{7,3},{8,12},{9,13},{10,... | collective-permute-start | bytes 172040 | tf_op jit(solution)/shard_map/ppermute | solution.py:729
  64.2 0.6 collective-permute-done.10
  64.8 1.3 %collective-permute-start.11 = (bf16[56,512]{1,0:T(8,128)(2,1)S(1)}, bf16[56,512]{1,0:T(8,128)(2,1)S(1)}, u32[]{:S(2)}, u32[]{:S(2)}) collective-permute-start(bf16[56,512]{1,0:T(8,128)(2,1)S(1)} %broadcast_select_fusion.23), channel_id=1, source_target_pairs={{0,1},{1,0},{2,3},{3,2},{4,5},{5,4},{6,7},{7,6},{8,9},{9,8},{10,11... | collective-permute-start | bytes 172040 | tf_op jit(solution)/shard_map/ppermute | solution.py:729
  66.1 0.4 collective-permute-done.18
  66.6 0.4 collective-permute-start.19
  67.1 3.3 %collective-permute-start.4 = (bf16[56,512]{1,0:T(8,128)(2,1)S(1)}, bf16[56,512]{1,0:T(8,128)(2,1)S(1)}, u32[]{:S(2)}, u32[]{:S(2)}) collective-permute-start(bf16[56,512]{1,0:T(8,128)(2,1)S(1)} %add_convert_fusion.14), channel_id=1, source_target_pairs={{0,8},{1,9},{2,10},{3,11},{4,12},{5,13},{6,14},{7,15},{8,0},{9,1},... | collective-permute-start | bytes 172040 | tf_op jit(solution)/shard_map/ppermute | solution.py:729
  70.4 0.9 collective-permute-start.12
  71.3 2.2 %collective-permute-start.20 = (bf16[56,512]{1,0:T(8,128)(2,1)S(1)}, bf16[56,512]{1,0:T(8,128)(2,1)S(1)}, u32[]{:S(2)}, u32[]{:S(2)}) collective-permute-start(bf16[56,512]{1,0:T(8,128)(2,1)S(1)} %add_convert_fusion.10), channel_id=1, source_target_pairs={{0,8},{1,9},{2,10},{3,11},{4,12},{5,13},{6,14},{7,15},{8,0},{9,1},... | collective-permute-start | bytes 172040 | tf_op jit(solution)/shard_map/ppermute | solution.py:729
  73.5 1.3 %collective-permute-start.5 = (bf16[56,512]{1,0:T(8,128)(2,1)S(1)}, bf16[56,512]{1,0:T(8,128)(2,1)S(1)}, u32[]{:S(2)}, u32[]{:S(2)}) collective-permute-start(bf16[56,512]{1,0:T(8,128)(2,1)S(1)} %add_convert_fusion.13), channel_id=1, source_target_pairs={{0,4},{1,5},{2,6},{3,7},{4,0},{5,1},{6,2},{7,3},{8,12},{9,13},{10,... | collective-permute-start | bytes 172040 | tf_op jit(solution)/shard_map/ppermute | solution.py:729
  74.9 1.1 %collective-permute-done.12 = bf16[56,512]{1,0:T(8,128)(2,1)S(1)} collective-permute-done((bf16[56,512]{1,0:T(8,128)(2,1)S(1)}, bf16[56,512]{1,0:T(8,128)(2,1)S(1)}, u32[]{:S(2)}, u32[]{:S(2)}) %collective-permute-start.12) | collective-permute-done | bytes 57376 | tf_op jit(solution)/shard_map/ppermute | solution.py:729
  76.0 1.1 %collective-permute-start.13 = (bf16[56,512]{1,0:T(8,128)(2,1)S(1)}, bf16[56,512]{1,0:T(8,128)(2,1)S(1)}, u32[]{:S(2)}, u32[]{:S(2)}) collective-permute-start(bf16[56,512]{1,0:T(8,128)(2,1)S(1)} %add_convert_fusion.11), channel_id=1, source_target_pairs={{0,1},{1,0},{2,3},{3,2},{4,5},{5,4},{6,7},{7,6},{8,9},{9,8},{10,11... | collective-permute-start | bytes 172040 | tf_op jit(solution)/shard_map/ppermute | solution.py:729
  77.2 0.8 collective-permute-start.21
  78.0 2.3 %collective-permute-start.6 = (bf16[112,512]{1,0:T(8,128)(2,1)S(1)}, bf16[112,512]{1,0:T(8,128)(2,1)S(1)}, u32[]{:S(2)}, u32[]{:S(2)}) collective-permute-start(bf16[112,512]{1,0:T(8,128)(2,1)S(1)} %pad_maximum_fusion.6), channel_id=1, source_target_pairs={{0,2},{1,3},{2,0},{3,1},{4,6},{5,7},{6,4},{7,5},{8,10},{9,11},{10,... | collective-permute-start | bytes 344072 | tf_op jit(solution)/shard_map/ppermute | solution.py:729
  80.4 1.0 %collective-permute-done.21 = bf16[56,512]{1,0:T(8,128)(2,1)S(1)} collective-permute-done((bf16[56,512]{1,0:T(8,128)(2,1)S(1)}, bf16[56,512]{1,0:T(8,128)(2,1)S(1)}, u32[]{:S(2)}, u32[]{:S(2)}) %collective-permute-start.21) | collective-permute-done | bytes 57376 | tf_op jit(solution)/shard_map/ppermute | solution.py:729
  81.4 1.2 %collective-permute-start.22 = (bf16[112,512]{1,0:T(8,128)(2,1)S(1)}, bf16[112,512]{1,0:T(8,128)(2,1)S(1)}, u32[]{:S(2)}, u32[]{:S(2)}) collective-permute-start(bf16[112,512]{1,0:T(8,128)(2,1)S(1)} %pad_maximum_fusion.8), channel_id=1, source_target_pairs={{0,1},{1,0},{2,3},{3,2},{4,5},{5,4},{6,7},{7,6},{8,9},{9,8},{10,11... | collective-permute-start | bytes 344072 | tf_op jit(solution)/shard_map/ppermute | solution.py:729
  82.7 0.6 collective-permute-done.6
  83.3 2.3 %collective-permute-start.7 = (bf16[224,512]{1,0:T(8,128)(2,1)S(1)}, bf16[224,512]{1,0:T(8,128)(2,1)S(1)}, u32[]{:S(2)}, u32[]{:S(2)}) collective-permute-start(bf16[224,512]{1,0:T(8,128)(2,1)S(1)} %pad_maximum_fusion.3), channel_id=1, source_target_pairs={{0,1},{1,0},{2,3},{3,2},{4,5},{5,4},{6,7},{7,6},{8,9},{9,8},{10,11... | collective-permute-start | bytes 688136 | tf_op jit(solution)/shard_map/ppermute | solution.py:729
  85.6 0.5 collective-permute-done.14
  86.2 0.5 collective-permute-start.15
  86.7 1.8 %collective-permute-start.23 = (bf16[224,512]{1,0:T(8,128)(2,1)S(1)}, bf16[224,512]{1,0:T(8,128)(2,1)S(1)}, u32[]{:S(2)}, u32[]{:S(2)}) collective-permute-start(bf16[224,512]{1,0:T(8,128)(2,1)S(1)} %pad_maximum_fusion.5), channel_id=1, source_target_pairs={{0,4},{1,5},{2,6},{3,7},{4,0},{5,1},{6,2},{7,3},{8,12},{9,13},{10,... | collective-permute-start | bytes 688136 | tf_op jit(solution)/shard_map/ppermute | solution.py:729
  88.5 1.1 %collective-permute-done.7 = bf16[224,512]{1,0:T(8,128)(2,1)S(1)} collective-permute-done((bf16[224,512]{1,0:T(8,128)(2,1)S(1)}, bf16[224,512]{1,0:T(8,128)(2,1)S(1)}, u32[]{:S(2)}, u32[]{:S(2)}) %collective-permute-start.7) | collective-permute-done | bytes 229408 | tf_op jit(solution)/shard_map/ppermute | solution.py:729
  89.6 0.1 broadcast_select_fusion.7
  89.8 2.4 %collective-permute-done.15 = bf16[224,512]{1,0:T(8,128)(2,1)S(1)} collective-permute-done((bf16[224,512]{1,0:T(8,128)(2,1)S(1)}, bf16[224,512]{1,0:T(8,128)(2,1)S(1)}, u32[]{:S(2)}, u32[]{:S(2)}) %collective-permute-start.15) | collective-permute-done | bytes 229408 | tf_op jit(solution)/shard_map/ppermute | solution.py:729
  92.3 0.1 broadcast_select_fusion.4
  92.5 0.4 collective-permute-done.23
  92.8 0.1 broadcast_select_fusion.1
  92.9 0.2 collective-permute-start.26
  93.1 1.8 %spread_mine.1 = (f32[2,512,512]{2,1,0:T(8,128)}, f32[2,512,512]{2,1,0:T(8,128)}, f32[2,2,8,64,64]{4,3,2,1,0:T(8,128)}, f32[2,2,8,64,64]{4,3,2,1,0:T(8,128)}) custom-call(s32[1]{0:T(128)} %bitcast.core_ref, bf16[448,512]{1,0:T(8,128)(2,1)S(1)} %pad_maximum_fusion.a0, bf16[448,512]{1,0:T(8,128)(2,1)S(1)} %pad_maximum_fusion.1.a1, ...), custom_call_target="tpu_custom_call" | custom-call | flops 1048576 | bytes 4194304 | tf_op jit(solution)/shard_map/spread_mine/pallas_call | solution.py:695
  95.0 2.5 %spread_other.1 = (f32[2,512,512]{2,1,0:T(8,128)}, f32[2,512,512]{2,1,0:T(8,128)}, f32[2,2,8,64,64]{4,3,2,1,0:T(8,128)}, f32[2,2,8,64,64]{4,3,2,1,0:T(8,128)}, f...) custom-call(s32[1]{0:T(128)} %bitcast.core_ref, ...), custom_call_target="tpu_custom_call", output_to_operand_aliasing={{0}: (7, {}), {1}: (8, {}), {2}: (9, {}), {3}: (10, {})} | custom-call | tf_op jit(solution)/shard_map/spread_other/pallas_call | solution.py:715
  (55 shorter events, 1.0 us)
Async XLA Ops:
  43.1 8.0 %copy-start.1 = (bf16[448,512]{1,0:T(8,128)(2,1)S(1)}, bf16[448,512]{1,0:T(8,128)(2,1)}, u32[]{:S(2)}) copy-start(bf16[448,512]{1,0:T(8,128)(2,1)} %get-tuple-element.42) | copy-start | bytes 1376260
  43.1 9.8 %copy-start = (bf16[448,512]{1,0:T(8,128)(2,1)S(1)}, bf16[448,512]{1,0:T(8,128)(2,1)}, u32[]{:S(2)}) copy-start(bf16[448,512]{1,0:T(8,128)(2,1)} %get-tuple-element.44) | copy-start | bytes 1376260
  43.1 2.2 %collective-permute-start = (bf16[448,512]{1,0:T(8,128)(2,1)}, bf16[448,512]{1,0:T(8,128)(2,1)S(1)}, u32[]{:S(2)}, u32[]{:S(2)}) collective-permute-start(bf16[448,512]{1,0:T(8,128)(2,1)} %get-tuple-element.41), channel_id=1, source_target_pairs={{0,16},{1,17},{2,18},{3,19},{4,20},{5,21},{6,22},{7,23},{8,24},{9,... | collective-permute-start | bytes 1376264 | tf_op jit(solution)/shard_map/ppermute | solution.py:729
  43.6 7.5 %collective-permute-start.8 = (bf16[448,512]{1,0:T(8,128)(2,1)}, bf16[448,512]{1,0:T(8,128)(2,1)S(1)}, u32[]{:S(2)}, u32[]{:S(2)}) collective-permute-start(bf16[448,512]{1,0:T(8,128)(2,1)} %get-tuple-element.43), channel_id=1, source_target_pairs={{0,16},{1,17},{2,18},{3,19},{4,20},{5,21},{6,22},{7,23},{8,24},{9,... | collective-permute-start | bytes 1376264 | tf_op jit(solution)/shard_map/ppermute | solution.py:729
  43.7 9.2 %collective-permute-start.16 = (bf16[448,512]{1,0:T(8,128)(2,1)}, bf16[448,512]{1,0:T(8,128)(2,1)S(1)}, u32[]{:S(2)}, u32[]{:S(2)}) collective-permute-start(bf16[448,512]{1,0:T(8,128)(2,1)} %get-tuple-element.45), channel_id=1, source_target_pairs={{0,16},{1,17},{2,18},{3,19},{4,20},{5,21},{6,22},{7,23},{8,24},{9,... | collective-permute-start | bytes 1376264 | tf_op jit(solution)/shard_map/ppermute | solution.py:729
  46.5 10.6 %collective-permute-start.1 = (bf16[224,512]{1,0:T(8,128)(2,1)S(1)}, bf16[224,512]{1,0:T(8,128)(2,1)S(1)}, u32[]{:S(2)}, u32[]{:S(2)}) collective-permute-start(bf16[224,512]{1,0:T(8,128)(2,1)S(1)} %broadcast_select_fusion.8), channel_id=1, source_target_pairs={{0,1},{1,0},{2,3},{3,2},{4,5},{5,4},{6,7},{7,6},{8,9},{9,8},{10,11... | collective-permute-start | bytes 688136 | tf_op jit(solution)/shard_map/ppermute | solution.py:729
  51.3 7.9 %collective-permute-start.9 = (bf16[224,512]{1,0:T(8,128)(2,1)S(1)}, bf16[224,512]{1,0:T(8,128)(2,1)S(1)}, u32[]{:S(2)}, u32[]{:S(2)}) collective-permute-start(bf16[224,512]{1,0:T(8,128)(2,1)S(1)} %broadcast_select_fusion.5), channel_id=1, source_target_pairs={{0,2},{1,3},{2,0},{3,1},{4,6},{5,7},{6,4},{7,5},{8,10},{9,11},{10,... | collective-permute-start | bytes 688136 | tf_op jit(solution)/shard_map/ppermute | solution.py:729
  53.0 7.9 %collective-permute-start.17 = (bf16[224,512]{1,0:T(8,128)(2,1)S(1)}, bf16[224,512]{1,0:T(8,128)(2,1)S(1)}, u32[]{:S(2)}, u32[]{:S(2)}) collective-permute-start(bf16[224,512]{1,0:T(8,128)(2,1)S(1)} %broadcast_select_fusion.2), channel_id=1, source_target_pairs={{0,4},{1,5},{2,6},{3,7},{4,0},{5,1},{6,2},{7,3},{8,12},{9,13},{10,... | collective-permute-start | bytes 688136 | tf_op jit(solution)/shard_map/ppermute | solution.py:729
  57.1 4.9 %collective-permute-start.2 = (bf16[112,512]{1,0:T(8,128)(2,1)S(1)}, bf16[112,512]{1,0:T(8,128)(2,1)S(1)}, u32[]{:S(2)}, u32[]{:S(2)}) collective-permute-start(bf16[112,512]{1,0:T(8,128)(2,1)S(1)} %broadcast_select_fusion.17), channel_id=1, source_target_pairs={{0,2},{1,3},{2,0},{3,1},{4,6},{5,7},{6,4},{7,5},{8,10},{9,11},{10,... | collective-permute-start | bytes 344072 | tf_op jit(solution)/shard_map/ppermute | solution.py:729
  59.3 5.5 %collective-permute-start.10 = (bf16[112,512]{1,0:T(8,128)(2,1)S(1)}, bf16[112,512]{1,0:T(8,128)(2,1)S(1)}, u32[]{:S(2)}, u32[]{:S(2)}) collective-permute-start(bf16[112,512]{1,0:T(8,128)(2,1)S(1)} %broadcast_select_fusion.14), channel_id=1, source_target_pairs={{0,4},{1,5},{2,6},{3,7},{4,0},{5,1},{6,2},{7,3},{8,12},{9,13},{10,... | collective-permute-start | bytes 344072 | tf_op jit(solution)/shard_map/ppermute | solution.py:729
  61.1 5.5 %collective-permute-start.18 = (bf16[112,512]{1,0:T(8,128)(2,1)S(1)}, bf16[112,512]{1,0:T(8,128)(2,1)S(1)}, u32[]{:S(2)}, u32[]{:S(2)}) collective-permute-start(bf16[112,512]{1,0:T(8,128)(2,1)S(1)} %broadcast_select_fusion.11), channel_id=1, source_target_pairs={{0,1},{1,0},{2,3},{3,2},{4,5},{5,4},{6,7},{7,6},{8,9},{9,8},{10,11... | collective-permute-start | bytes 344072 | tf_op jit(solution)/shard_map/ppermute | solution.py:729
  62.1 5.0 %collective-permute-start.3 = (bf16[56,512]{1,0:T(8,128)(2,1)S(1)}, bf16[56,512]{1,0:T(8,128)(2,1)S(1)}, u32[]{:S(2)}, u32[]{:S(2)}) collective-permute-start(bf16[56,512]{1,0:T(8,128)(2,1)S(1)} %broadcast_select_fusion.26), channel_id=1, source_target_pairs={{0,4},{1,5},{2,6},{3,7},{4,0},{5,1},{6,2},{7,3},{8,12},{9,13},{10,... | collective-permute-start | bytes 172040 | tf_op jit(solution)/shard_map/ppermute | solution.py:729
  64.8 5.6 %collective-permute-start.11 = (bf16[56,512]{1,0:T(8,128)(2,1)S(1)}, bf16[56,512]{1,0:T(8,128)(2,1)S(1)}, u32[]{:S(2)}, u32[]{:S(2)}) collective-permute-start(bf16[56,512]{1,0:T(8,128)(2,1)S(1)} %broadcast_select_fusion.23), channel_id=1, source_target_pairs={{0,1},{1,0},{2,3},{3,2},{4,5},{5,4},{6,7},{7,6},{8,9},{9,8},{10,11... | collective-permute-start | bytes 172040 | tf_op jit(solution)/shard_map/ppermute | solution.py:729
  66.6 4.7 %collective-permute-start.19 = (bf16[56,512]{1,0:T(8,128)(2,1)S(1)}, bf16[56,512]{1,0:T(8,128)(2,1)S(1)}, u32[]{:S(2)}, u32[]{:S(2)}) collective-permute-start(bf16[56,512]{1,0:T(8,128)(2,1)S(1)} %broadcast_select_fusion.20), channel_id=1, source_target_pairs={{0,2},{1,3},{2,0},{3,1},{4,6},{5,7},{6,4},{7,5},{8,10},{9,11},{10,... | collective-permute-start | bytes 172040 | tf_op jit(solution)/shard_map/ppermute | solution.py:729
  67.1 6.4 %collective-permute-start.4 = (bf16[56,512]{1,0:T(8,128)(2,1)S(1)}, bf16[56,512]{1,0:T(8,128)(2,1)S(1)}, u32[]{:S(2)}, u32[]{:S(2)}) collective-permute-start(bf16[56,512]{1,0:T(8,128)(2,1)S(1)} %add_convert_fusion.14), channel_id=1, source_target_pairs={{0,8},{1,9},{2,10},{3,11},{4,12},{5,13},{6,14},{7,15},{8,0},{9,1},... | collective-permute-start | bytes 172040 | tf_op jit(solution)/shard_map/ppermute | solution.py:729
  70.4 5.6 %collective-permute-start.12 = (bf16[56,512]{1,0:T(8,128)(2,1)S(1)}, bf16[56,512]{1,0:T(8,128)(2,1)S(1)}, u32[]{:S(2)}, u32[]{:S(2)}) collective-permute-start(bf16[56,512]{1,0:T(8,128)(2,1)S(1)} %add_convert_fusion.12), channel_id=1, source_target_pairs={{0,8},{1,9},{2,10},{3,11},{4,12},{5,13},{6,14},{7,15},{8,0},{9,1},... | collective-permute-start | bytes 172040 | tf_op jit(solution)/shard_map/ppermute | solution.py:729
  71.3 5.8 %collective-permute-start.20 = (bf16[56,512]{1,0:T(8,128)(2,1)S(1)}, bf16[56,512]{1,0:T(8,128)(2,1)S(1)}, u32[]{:S(2)}, u32[]{:S(2)}) collective-permute-start(bf16[56,512]{1,0:T(8,128)(2,1)S(1)} %add_convert_fusion.10), channel_id=1, source_target_pairs={{0,8},{1,9},{2,10},{3,11},{4,12},{5,13},{6,14},{7,15},{8,0},{9,1},... | collective-permute-start | bytes 172040 | tf_op jit(solution)/shard_map/ppermute | solution.py:729
  73.5 4.4 %collective-permute-start.5 = (bf16[56,512]{1,0:T(8,128)(2,1)S(1)}, bf16[56,512]{1,0:T(8,128)(2,1)S(1)}, u32[]{:S(2)}, u32[]{:S(2)}) collective-permute-start(bf16[56,512]{1,0:T(8,128)(2,1)S(1)} %add_convert_fusion.13), channel_id=1, source_target_pairs={{0,4},{1,5},{2,6},{3,7},{4,0},{5,1},{6,2},{7,3},{8,12},{9,13},{10,... | collective-permute-start | bytes 172040 | tf_op jit(solution)/shard_map/ppermute | solution.py:729
  76.0 4.3 %collective-permute-start.13 = (bf16[56,512]{1,0:T(8,128)(2,1)S(1)}, bf16[56,512]{1,0:T(8,128)(2,1)S(1)}, u32[]{:S(2)}, u32[]{:S(2)}) collective-permute-start(bf16[56,512]{1,0:T(8,128)(2,1)S(1)} %add_convert_fusion.11), channel_id=1, source_target_pairs={{0,1},{1,0},{2,3},{3,2},{4,5},{5,4},{6,7},{7,6},{8,9},{9,8},{10,11... | collective-permute-start | bytes 172040 | tf_op jit(solution)/shard_map/ppermute | solution.py:729
  77.2 4.2 %collective-permute-start.21 = (bf16[56,512]{1,0:T(8,128)(2,1)S(1)}, bf16[56,512]{1,0:T(8,128)(2,1)S(1)}, u32[]{:S(2)}, u32[]{:S(2)}) collective-permute-start(bf16[56,512]{1,0:T(8,128)(2,1)S(1)} %add_convert_fusion.9), channel_id=1, source_target_pairs={{0,2},{1,3},{2,0},{3,1},{4,6},{5,7},{6,4},{7,5},{8,10},{9,11},{10,... | collective-permute-start | bytes 172040 | tf_op jit(solution)/shard_map/ppermute | solution.py:729
  78.0 5.3 %collective-permute-start.6 = (bf16[112,512]{1,0:T(8,128)(2,1)S(1)}, bf16[112,512]{1,0:T(8,128)(2,1)S(1)}, u32[]{:S(2)}, u32[]{:S(2)}) collective-permute-start(bf16[112,512]{1,0:T(8,128)(2,1)S(1)} %pad_maximum_fusion.6), channel_id=1, source_target_pairs={{0,2},{1,3},{2,0},{3,1},{4,6},{5,7},{6,4},{7,5},{8,10},{9,11},{10,... | collective-permute-start | bytes 344072 | tf_op jit(solution)/shard_map/ppermute | solution.py:729
  80.3 5.8 %collective-permute-start.14 = (bf16[112,512]{1,0:T(8,128)(2,1)S(1)}, bf16[112,512]{1,0:T(8,128)(2,1)S(1)}, u32[]{:S(2)}, u32[]{:S(2)}) collective-permute-start(bf16[112,512]{1,0:T(8,128)(2,1)S(1)} %pad_maximum_fusion.7), channel_id=1, source_target_pairs={{0,4},{1,5},{2,6},{3,7},{4,0},{5,1},{6,2},{7,3},{8,12},{9,13},{10,... | collective-permute-start | bytes 344072 | tf_op jit(solution)/shard_map/ppermute | solution.py:729
  81.4 5.2 %collective-permute-start.22 = (bf16[112,512]{1,0:T(8,128)(2,1)S(1)}, bf16[112,512]{1,0:T(8,128)(2,1)S(1)}, u32[]{:S(2)}, u32[]{:S(2)}) collective-permute-start(bf16[112,512]{1,0:T(8,128)(2,1)S(1)} %pad_maximum_fusion.8), channel_id=1, source_target_pairs={{0,1},{1,0},{2,3},{3,2},{4,5},{5,4},{6,7},{7,6},{8,9},{9,8},{10,11... | collective-permute-start | bytes 344072 | tf_op jit(solution)/shard_map/ppermute | solution.py:729
  83.3 6.3 %collective-permute-start.7 = (bf16[224,512]{1,0:T(8,128)(2,1)S(1)}, bf16[224,512]{1,0:T(8,128)(2,1)S(1)}, u32[]{:S(2)}, u32[]{:S(2)}) collective-permute-start(bf16[224,512]{1,0:T(8,128)(2,1)S(1)} %pad_maximum_fusion.3), channel_id=1, source_target_pairs={{0,1},{1,0},{2,3},{3,2},{4,5},{5,4},{6,7},{7,6},{8,9},{9,8},{10,11... | collective-permute-start | bytes 688136 | tf_op jit(solution)/shard_map/ppermute | solution.py:729
  86.2 6.1 %collective-permute-start.15 = (bf16[224,512]{1,0:T(8,128)(2,1)S(1)}, bf16[224,512]{1,0:T(8,128)(2,1)S(1)}, u32[]{:S(2)}, u32[]{:S(2)}) collective-permute-start(bf16[224,512]{1,0:T(8,128)(2,1)S(1)} %pad_maximum_fusion.4), channel_id=1, source_target_pairs={{0,2},{1,3},{2,0},{3,1},{4,6},{5,7},{6,4},{7,5},{8,10},{9,11},{10,... | collective-permute-start | bytes 688136 | tf_op jit(solution)/shard_map/ppermute | solution.py:729
  86.7 6.1 %collective-permute-start.23 = (bf16[224,512]{1,0:T(8,128)(2,1)S(1)}, bf16[224,512]{1,0:T(8,128)(2,1)S(1)}, u32[]{:S(2)}, u32[]{:S(2)}) collective-permute-start(bf16[224,512]{1,0:T(8,128)(2,1)S(1)} %pad_maximum_fusion.5), channel_id=1, source_target_pairs={{0,4},{1,5},{2,6},{3,7},{4,0},{5,1},{6,2},{7,3},{8,12},{9,13},{10,... | collective-permute-start | bytes 688136 | tf_op jit(solution)/shard_map/ppermute | solution.py:729
  89.8 5.2 %collective-permute-start.24 = (bf16[448,512]{1,0:T(8,128)(2,1)S(1)}, bf16[448,512]{1,0:T(8,128)(2,1)S(1)}, u32[]{:S(2)}, u32[]{:S(2)}) collective-permute-start(bf16[448,512]{1,0:T(8,128)(2,1)S(1)} %pad_maximum_fusion.a0), channel_id=1, source_target_pairs={{0,16},{1,17},{2,18},{3,19},{4,20},{5,21},{6,22},{7,23},{8,24},{9,... | collective-permute-start | bytes 1376264 | tf_op jit(solution)/shard_map/ppermute | solution.py:729
  92.4 2.6 %collective-permute-start.25 = (bf16[448,512]{1,0:T(8,128)(2,1)S(1)}, bf16[448,512]{1,0:T(8,128)(2,1)S(1)}, u32[]{:S(2)}, u32[]{:S(2)}) collective-permute-start(bf16[448,512]{1,0:T(8,128)(2,1)S(1)} %pad_maximum_fusion.1.a1), channel_id=1, source_target_pairs={{0,16},{1,17},{2,18},{3,19},{4,20},{5,21},{6,22},{7,23},{8,24},{9,... | collective-permute-start | bytes 1376264 | tf_op jit(solution)/shard_map/ppermute | solution.py:729
  92.9 2.1 %collective-permute-start.26 = (bf16[448,512]{1,0:T(8,128)(2,1)S(1)}, bf16[448,512]{1,0:T(8,128)(2,1)S(1)}, u32[]{:S(2)}, u32[]{:S(2)}) collective-permute-start(bf16[448,512]{1,0:T(8,128)(2,1)S(1)} %pad_maximum_fusion.2.a2), channel_id=1, source_target_pairs={{0,16},{1,17},{2,18},{3,19},{4,20},{5,21},{6,22},{7,23},{8,24},{9,... | collective-permute-start | bytes 1376264 | tf_op jit(solution)/shard_map/ppermute | solution.py:729

commit v4 on v3

--- a/solution.py
+++ b/solution.py
@@ -389,7 +389,7 @@
         def gelu_f(i, pre):
             for j in range(0, RT, CF):
                 cd = slice(i * RT + j, i * RT + j + CF)
-                act[layer, cd, :], dp[layer, cd, :] = gelu_split(pre[j : j + CF] + fb1[pl.ds(layer, 1), :])
+                act[layer, cd, :], dp[layer, cd, :] = gelu_pair((pre[j : j + CF] + fb1[pl.ds(layer, 1), :]).astype(BF))
             return nn(act[layer, tile(i), :], fc2[layer])
 
         def leave(i, br):
@@ -557,30 +557,43 @@
             leave(i, y)
             y = nxt
 
+    def vectors(layer):
+        t = jnp.sum(acc[layer], 1)
+        t = jnp.concatenate([t, jnp.zeros((PER - 1290, 512), F32)], 0)
+        grads_ref[pl.ds(pl.multiple_of((layer ^ core_ref[0]) * PER, PER) + 1280, PER - 1280), :] = t.astype(BF)
+
+    sends = [
+        copy(8 + k, grads_ref.at[pl.ds(row, PER // 3)], dst)
+        for k, (row, dst) in enumerate(
+            (((3 * half + c) * (PER // 3), dst) for half, refs in ((1, (t0, t1, t2)), (0, (m0, m1, m2))) for c, dst in enumerate(refs))
+        )
+    ]
+
+    def start_half(half):
+        for h in range(2):
+
+            @pl.when(half == h)
+            def _():
+                for c in sends[3 - 3 * h : 6 - 3 * h]:
+                    c.start()
+
     @partial(lax.fori_loop, 0, LAYERS, init_val=0)
     def _(step, carry):
         layer = LAYERS - 1 - step
         block(lambda: ff_backward(layer))
         block(lambda: mix_backward(layer))
         block(lambda: in_backward(layer))
+
+        @pl.when(step == 0)
+        def _():
+            vectors(1)
+            start_half(1 - core_ref[0])
+
         return carry
 
-    def vectors(layer):
-        t = jnp.sum(acc[layer], 1)
-        t = jnp.concatenate([t, jnp.zeros((PER - 1290, 512), F32)], 0)
-        grads_ref[pl.ds(pl.multiple_of((layer ^ core_ref[0]) * PER, PER) + 1280, PER - 1280), :] = t.astype(BF)
-
-    vectors(1)
-    sends = [
-        copy(8 + k, grads_ref.at[pl.ds(row, PER // 3)], dst)
-        for k, (row, dst) in enumerate(
-            (((3 * half + c) * (PER // 3), dst) for half, refs in ((1, (t0, t1, t2)), (0, (m0, m1, m2))) for c, dst in enumerate(refs))
-        )
-    ]
     xg_copy = copy(7, xg_ref, xg_hbm)
     vectors(0)
-    for c in sends:
-        c.start()
+    start_half(core_ref[0])
     xg_copy.start()
     out_copy.wait()
     for c in sends:

time: 98.2 us -> 96.5 us (0.983)
  starting transfers between devices: 34.9 us -> 29.5 us
  waiting for transfers between devices: 12.2 us -> 15.3 us
  Pallas kernels: 46.7 us -> 47.8 us
    ppermute x27, starting transfers between devices: 34.9 us -> 29.5 us  [exchange(): return lax.ppermute(a, AXES, [(i, i ^ bit) for i in range(count)])]
    ppermute x27, waiting for transfers between devices: 12.2 us -> 15.3 us  [exchange(): return lax.ppermute(a, AXES, [(i, i ^ bit) for i in range(count)])]
    pallas_call x1, Pallas kernels: 42.4 us -> 43.4 us  [local_step(): pl.pallas_call(kernel, out_shape=(jax.ShapeDtypeStruct((rows, d), BF), ja...]
  transfers between devices with their start and end apart: 27 -> 27, of which waited for: 12 -> 14; matrix products, arithmetic and copies ran while one was open for 3% -> 3% of each run, Pallas kernels for 2% -> 2%
where the time goes in v4:
time: 96.5 us; the launch traced here: 96.4 us
  Pallas kernels  47.8 us (50%)
  starting transfers between devices  29.5 us (31%)
  waiting for transfers between devices  15.3 us (16%)
  other arithmetic  2.64 us (3%)
  between operations  1.18 us (1%)
    pallas_call x1, Pallas kernels, local_step(): pl.pallas_call(kernel, out_shape=(jax.ShapeDtypeStruct((rows, d), BF), ja...  43.4 us
    ppermute x27, starting transfers between devices, exchange(): return lax.ppermute(a, AXES, [(i, i ^ bit) for i in range(count)])  29.5 us
    ppermute x27, waiting for transfers between devices, exchange(): return lax.ppermute(a, AXES, [(i, i ^ bit) for i in range(count)])  15.3 us
    pallas_call x1, Pallas kernels, unpack(): pl.pallas_call(spread_other, out_shape=big + (vec, vec, pair, pair, vec,...  2.47 us
  transfers between devices with their start and end apart: 27, of which 14 were waited for; matrix products, arithmetic and copies ran while one was open for 3% of the time, Pallas kernels for 2%

profile of v4, /device:TPU:0, one launch (start us, length us, event | category | flops | bytes accessed | tf_op | source)
XLA Modules:
  0.0 96.4 jit_solution(16263795586602152644)
XLA Ops:
  0.7 43.4 %slab_step.1 = (bf16[1024,512]{1,0:T(8,128)(2,1)}, bf16[1024,512]{1,0:T(8,128)(2,1)}, bf16[448,512]{1,0:T(8,128)(2,1)}, bf16[448,512]{1,0:T(8,128)(2,1)}, bf16[4...) custom-call(s32[16]{0:T(128)} %grid_ref.1, s32[3]{0:T(128)} %keep_ref.1, ...), custom_call_target="tpu_custom_call" | custom-call | tf_op jit(solution)/shard_map/slab_step/pallas_call | solution.py:635
  44.2 0.5 collective-permute-start.8
  44.7 0.1 collective-permute-start.16
  44.8 1.4 %collective-permute-done = bf16[448,512]{1,0:T(8,128)(2,1)S(1)} collective-permute-done((bf16[448,512]{1,0:T(8,128)(2,1)}, bf16[448,512]{1,0:T(8,128)(2,1)S(1)}, u32[]{:S(2)}, u32[]{:S(2)}) %collective-permute-start) | collective-permute-done | bytes 458784 | tf_op jit(solution)/shard_map/ppermute | solution.py:742
  46.2 1.1 %add_convert_fusion.2 = bf16[448,512]{1,0:T(8,128)(2,1)S(1)} fusion(bf16[448,512]{1,0:T(8,128)(2,1)S(1)} %collective-permute-done, bf16[448,512]{1,0:T(8,128)(2,1)} %get-tuple-element.40), kind=kLoop, calls=%fused_computation.2 | loop fusion | flops 917504 | bytes 1376256 | tf_op jit(solution)/shard_map/convert_element_type | solution.py:746
  47.4 1.6 %collective-permute-start.1 = (bf16[224,512]{1,0:T(8,128)(2,1)S(1)}, bf16[224,512]{1,0:T(8,128)(2,1)S(1)}, u32[]{:S(2)}, u32[]{:S(2)}) collective-permute-start(bf16[224,512]{1,0:T(8,128)(2,1)S(1)} %broadcast_select_fusion.8), channel_id=1, source_target_pairs={{0,1},{1,0},{2,3},{3,2},{4,5},{5,4},{6,7},{7,6},{8,9},{9,8},{10,11... | collective-permute-start | bytes 688136 | tf_op jit(solution)/shard_map/ppermute | solution.py:742
  49.0 0.1 add_convert_fusion.1
  49.1 1.6 %collective-permute-start.9 = (bf16[224,512]{1,0:T(8,128)(2,1)S(1)}, bf16[224,512]{1,0:T(8,128)(2,1)S(1)}, u32[]{:S(2)}, u32[]{:S(2)}) collective-permute-start(bf16[224,512]{1,0:T(8,128)(2,1)S(1)} %broadcast_select_fusion.5), channel_id=1, source_target_pairs={{0,2},{1,3},{2,0},{3,1},{4,6},{5,7},{6,4},{7,5},{8,10},{9,11},{10,... | collective-permute-start | bytes 688136 | tf_op jit(solution)/shard_map/ppermute | solution.py:742
  50.7 0.1 add_convert_fusion
  50.9 0.9 collective-permute-start.17
  51.7 3.4 %collective-permute-done.1 = bf16[224,512]{1,0:T(8,128)(2,1)S(1)} collective-permute-done((bf16[224,512]{1,0:T(8,128)(2,1)S(1)}, bf16[224,512]{1,0:T(8,128)(2,1)S(1)}, u32[]{:S(2)}, u32[]{:S(2)}) %collective-permute-start.1) | collective-permute-done | bytes 229408 | tf_op jit(solution)/shard_map/ppermute | solution.py:742
  55.1 0.1 add_convert_fusion.5
  55.2 2.1 %collective-permute-start.2 = (bf16[112,512]{1,0:T(8,128)(2,1)S(1)}, bf16[112,512]{1,0:T(8,128)(2,1)S(1)}, u32[]{:S(2)}, u32[]{:S(2)}) collective-permute-start(bf16[112,512]{1,0:T(8,128)(2,1)S(1)} %broadcast_select_fusion.17), channel_id=1, source_target_pairs={{0,2},{1,3},{2,0},{3,1},{4,6},{5,7},{6,4},{7,5},{8,10},{9,11},{10,... | collective-permute-start | bytes 344072 | tf_op jit(solution)/shard_map/ppermute | solution.py:742
  57.3 0.1 add_convert_fusion.4
  57.4 1.6 %collective-permute-start.10 = (bf16[112,512]{1,0:T(8,128)(2,1)S(1)}, bf16[112,512]{1,0:T(8,128)(2,1)S(1)}, u32[]{:S(2)}, u32[]{:S(2)}) collective-permute-start(bf16[112,512]{1,0:T(8,128)(2,1)S(1)} %broadcast_select_fusion.14), channel_id=1, source_target_pairs={{0,4},{1,5},{2,6},{3,7},{4,0},{5,1},{6,2},{7,3},{8,12},{9,13},{10,... | collective-permute-start | bytes 344072 | tf_op jit(solution)/shard_map/ppermute | solution.py:742
  59.1 0.1 add_convert_fusion.3
  59.2 0.8 collective-permute-start.18
  60.0 0.1 collective-permute-done.2
  60.1 2.6 %collective-permute-start.3 = (bf16[56,512]{1,0:T(8,128)(2,1)S(1)}, bf16[56,512]{1,0:T(8,128)(2,1)S(1)}, u32[]{:S(2)}, u32[]{:S(2)}) collective-permute-start(bf16[56,512]{1,0:T(8,128)(2,1)S(1)} %broadcast_select_fusion.26), channel_id=1, source_target_pairs={{0,4},{1,5},{2,6},{3,7},{4,0},{5,1},{6,2},{7,3},{8,12},{9,13},{10,... | collective-permute-start | bytes 172040 | tf_op jit(solution)/shard_map/ppermute | solution.py:742
  62.9 1.1 %collective-permute-start.11 = (bf16[56,512]{1,0:T(8,128)(2,1)S(1)}, bf16[56,512]{1,0:T(8,128)(2,1)S(1)}, u32[]{:S(2)}, u32[]{:S(2)}) collective-permute-start(bf16[56,512]{1,0:T(8,128)(2,1)S(1)} %broadcast_select_fusion.23), channel_id=1, source_target_pairs={{0,1},{1,0},{2,3},{3,2},{4,5},{5,4},{6,7},{7,6},{8,9},{9,8},{10,11... | collective-permute-start | bytes 172040 | tf_op jit(solution)/shard_map/ppermute | solution.py:742
  63.9 0.7 collective-permute-done.18
  64.7 1.0 %collective-permute-start.19 = (bf16[56,512]{1,0:T(8,128)(2,1)S(1)}, bf16[56,512]{1,0:T(8,128)(2,1)S(1)}, u32[]{:S(2)}, u32[]{:S(2)}) collective-permute-start(bf16[56,512]{1,0:T(8,128)(2,1)S(1)} %broadcast_select_fusion.20), channel_id=1, source_target_pairs={{0,2},{1,3},{2,0},{3,1},{4,6},{5,7},{6,4},{7,5},{8,10},{9,11},{10,... | collective-permute-start | bytes 172040 | tf_op jit(solution)/shard_map/ppermute | solution.py:742
  65.8 2.9 %collective-permute-start.4 = (bf16[56,512]{1,0:T(8,128)(2,1)S(1)}, bf16[56,512]{1,0:T(8,128)(2,1)S(1)}, u32[]{:S(2)}, u32[]{:S(2)}) collective-permute-start(bf16[56,512]{1,0:T(8,128)(2,1)S(1)} %add_convert_fusion.14), channel_id=1, source_target_pairs={{0,8},{1,9},{2,10},{3,11},{4,12},{5,13},{6,14},{7,15},{8,0},{9,1},... | collective-permute-start | bytes 172040 | tf_op jit(solution)/shard_map/ppermute | solution.py:742
  68.8 0.5 collective-permute-start.12
  69.3 2.5 %collective-permute-start.20 = (bf16[56,512]{1,0:T(8,128)(2,1)S(1)}, bf16[56,512]{1,0:T(8,128)(2,1)S(1)}, u32[]{:S(2)}, u32[]{:S(2)}) collective-permute-start(bf16[56,512]{1,0:T(8,128)(2,1)S(1)} %add_convert_fusion.10), channel_id=1, source_target_pairs={{0,8},{1,9},{2,10},{3,11},{4,12},{5,13},{6,14},{7,15},{8,0},{9,1},... | collective-permute-start | bytes 172040 | tf_op jit(solution)/shard_map/ppermute | solution.py:742
  71.8 0.9 collective-permute-done.4
  72.7 0.4 collective-permute-start.5
  73.2 1.2 %collective-permute-done.12 = bf16[56,512]{1,0:T(8,128)(2,1)S(1)} collective-permute-done((bf16[56,512]{1,0:T(8,128)(2,1)S(1)}, bf16[56,512]{1,0:T(8,128)(2,1)S(1)}, u32[]{:S(2)}, u32[]{:S(2)}) %collective-permute-start.12) | collective-permute-done | bytes 57376 | tf_op jit(solution)/shard_map/ppermute | solution.py:742
  74.4 1.2 %collective-permute-start.13 = (bf16[56,512]{1,0:T(8,128)(2,1)S(1)}, bf16[56,512]{1,0:T(8,128)(2,1)S(1)}, u32[]{:S(2)}, u32[]{:S(2)}) collective-permute-start(bf16[56,512]{1,0:T(8,128)(2,1)S(1)} %add_convert_fusion.11), channel_id=1, source_target_pairs={{0,1},{1,0},{2,3},{3,2},{4,5},{5,4},{6,7},{7,6},{8,9},{9,8},{10,11... | collective-permute-start | bytes 172040 | tf_op jit(solution)/shard_map/ppermute | solution.py:742
  75.6 0.8 collective-permute-start.21
  76.3 0.6 collective-permute-done.5
  77.0 1.7 %collective-permute-start.6 = (bf16[112,512]{1,0:T(8,128)(2,1)S(1)}, bf16[112,512]{1,0:T(8,128)(2,1)S(1)}, u32[]{:S(2)}, u32[]{:S(2)}) collective-permute-start(bf16[112,512]{1,0:T(8,128)(2,1)S(1)} %pad_maximum_fusion.6), channel_id=1, source_target_pairs={{0,2},{1,3},{2,0},{3,1},{4,6},{5,7},{6,4},{7,5},{8,10},{9,11},{10,... | collective-permute-start | bytes 344072 | tf_op jit(solution)/shard_map/ppermute | solution.py:742
  78.7 0.6 collective-permute-start.14
  79.3 0.5 collective-permute-done.21
  79.9 1.0 %collective-permute-start.22 = (bf16[112,512]{1,0:T(8,128)(2,1)S(1)}, bf16[112,512]{1,0:T(8,128)(2,1)S(1)}, u32[]{:S(2)}, u32[]{:S(2)}) collective-permute-start(bf16[112,512]{1,0:T(8,128)(2,1)S(1)} %pad_maximum_fusion.8), channel_id=1, source_target_pairs={{0,1},{1,0},{2,3},{3,2},{4,5},{5,4},{6,7},{7,6},{8,9},{9,8},{10,11... | collective-permute-start | bytes 344072 | tf_op jit(solution)/shard_map/ppermute | solution.py:742
  80.8 1.4 %collective-permute-done.6 = bf16[112,512]{1,0:T(8,128)(2,1)S(1)} collective-permute-done((bf16[112,512]{1,0:T(8,128)(2,1)S(1)}, bf16[112,512]{1,0:T(8,128)(2,1)S(1)}, u32[]{:S(2)}, u32[]{:S(2)}) %collective-permute-start.6) | collective-permute-done | bytes 114720 | tf_op jit(solution)/shard_map/ppermute | solution.py:742
  82.3 1.6 %collective-permute-start.7 = (bf16[224,512]{1,0:T(8,128)(2,1)S(1)}, bf16[224,512]{1,0:T(8,128)(2,1)S(1)}, u32[]{:S(2)}, u32[]{:S(2)}) collective-permute-start(bf16[224,512]{1,0:T(8,128)(2,1)S(1)} %pad_maximum_fusion.3), channel_id=1, source_target_pairs={{0,1},{1,0},{2,3},{3,2},{4,5},{5,4},{6,7},{7,6},{8,9},{9,8},{10,11... | collective-permute-start | bytes 688136 | tf_op jit(solution)/shard_map/ppermute | solution.py:742
  83.9 0.5 collective-permute-done.14
  84.5 1.0 %collective-permute-start.15 = (bf16[224,512]{1,0:T(8,128)(2,1)S(1)}, bf16[224,512]{1,0:T(8,128)(2,1)S(1)}, u32[]{:S(2)}, u32[]{:S(2)}) collective-permute-start(bf16[224,512]{1,0:T(8,128)(2,1)S(1)} %pad_maximum_fusion.4), channel_id=1, source_target_pairs={{0,2},{1,3},{2,0},{3,1},{4,6},{5,7},{6,4},{7,5},{8,10},{9,11},{10,... | collective-permute-start | bytes 688136 | tf_op jit(solution)/shard_map/ppermute | solution.py:742
  85.5 1.2 %collective-permute-start.23 = (bf16[224,512]{1,0:T(8,128)(2,1)S(1)}, bf16[224,512]{1,0:T(8,128)(2,1)S(1)}, u32[]{:S(2)}, u32[]{:S(2)}) collective-permute-start(bf16[224,512]{1,0:T(8,128)(2,1)S(1)} %pad_maximum_fusion.5), channel_id=1, source_target_pairs={{0,4},{1,5},{2,6},{3,7},{4,0},{5,1},{6,2},{7,3},{8,12},{9,13},{10,... | collective-permute-start | bytes 688136 | tf_op jit(solution)/shard_map/ppermute | solution.py:742
  86.7 1.6 %collective-permute-done.7 = bf16[224,512]{1,0:T(8,128)(2,1)S(1)} collective-permute-done((bf16[224,512]{1,0:T(8,128)(2,1)S(1)}, bf16[224,512]{1,0:T(8,128)(2,1)S(1)}, u32[]{:S(2)}, u32[]{:S(2)}) %collective-permute-start.7) | collective-permute-done | bytes 229408 | tf_op jit(solution)/shard_map/ppermute | solution.py:742
  88.4 0.1 broadcast_select_fusion.7
  88.6 2.0 %collective-permute-done.15 = bf16[224,512]{1,0:T(8,128)(2,1)S(1)} collective-permute-done((bf16[224,512]{1,0:T(8,128)(2,1)S(1)}, bf16[224,512]{1,0:T(8,128)(2,1)S(1)}, u32[]{:S(2)}, u32[]{:S(2)}) %collective-permute-start.15) | collective-permute-done | bytes 229408 | tf_op jit(solution)/shard_map/ppermute | solution.py:742
  90.6 0.1 broadcast_select_fusion.4
  90.8 0.8 collective-permute-done.23
  91.6 0.1 broadcast_select_fusion.1
  91.8 1.8 %spread_mine.1 = (f32[2,512,512]{2,1,0:T(8,128)}, f32[2,512,512]{2,1,0:T(8,128)}, f32[2,2,8,64,64]{4,3,2,1,0:T(8,128)}, f32[2,2,8,64,64]{4,3,2,1,0:T(8,128)}) custom-call(s32[1]{0:T(128)} %bitcast.core_ref, bf16[448,512]{1,0:T(8,128)(2,1)S(1)} %pad_maximum_fusion.a0, bf16[448,512]{1,0:T(8,128)(2,1)S(1)} %pad_maximum_fusion.1.a1, ...), custom_call_target="tpu_custom_call" | custom-call | flops 1048576 | bytes 4194304 | tf_op jit(solution)/shard_map/spread_mine/pallas_call | solution.py:708
  93.7 2.5 %spread_other.1 = (f32[2,512,512]{2,1,0:T(8,128)}, f32[2,512,512]{2,1,0:T(8,128)}, f32[2,2,8,64,64]{4,3,2,1,0:T(8,128)}, f32[2,2,8,64,64]{4,3,2,1,0:T(8,128)}, f...) custom-call(s32[1]{0:T(128)} %bitcast.core_ref, ...), custom_call_target="tpu_custom_call", output_to_operand_aliasing={{0}: (7, {}), {1}: (8, {}), {2}: (9, {}), {3}: (10, {})} | custom-call | tf_op jit(solution)/shard_map/spread_other/pallas_call | solution.py:728
  (55 shorter events, 1.2 us)
Async XLA Ops:
  44.1 4.9 %copy-start.1 = (bf16[448,512]{1,0:T(8,128)(2,1)S(1)}, bf16[448,512]{1,0:T(8,128)(2,1)}, u32[]{:S(2)}) copy-start(bf16[448,512]{1,0:T(8,128)(2,1)} %get-tuple-element.42) | copy-start | bytes 1376260
  44.1 6.6 %copy-start = (bf16[448,512]{1,0:T(8,128)(2,1)S(1)}, bf16[448,512]{1,0:T(8,128)(2,1)}, u32[]{:S(2)}) copy-start(bf16[448,512]{1,0:T(8,128)(2,1)} %get-tuple-element.44) | copy-start | bytes 1376260
  44.1 2.1 %collective-permute-start = (bf16[448,512]{1,0:T(8,128)(2,1)}, bf16[448,512]{1,0:T(8,128)(2,1)S(1)}, u32[]{:S(2)}, u32[]{:S(2)}) collective-permute-start(bf16[448,512]{1,0:T(8,128)(2,1)} %get-tuple-element.41), channel_id=1, source_target_pairs={{0,16},{1,17},{2,18},{3,19},{4,20},{5,21},{6,22},{7,23},{8,24},{9,... | collective-permute-start | bytes 1376264 | tf_op jit(solution)/shard_map/ppermute | solution.py:742
  44.2 4.8 %collective-permute-start.8 = (bf16[448,512]{1,0:T(8,128)(2,1)}, bf16[448,512]{1,0:T(8,128)(2,1)S(1)}, u32[]{:S(2)}, u32[]{:S(2)}) collective-permute-start(bf16[448,512]{1,0:T(8,128)(2,1)} %get-tuple-element.43), channel_id=1, source_target_pairs={{0,16},{1,17},{2,18},{3,19},{4,20},{5,21},{6,22},{7,23},{8,24},{9,... | collective-permute-start | bytes 1376264 | tf_op jit(solution)/shard_map/ppermute | solution.py:742
  44.7 6.0 %collective-permute-start.16 = (bf16[448,512]{1,0:T(8,128)(2,1)}, bf16[448,512]{1,0:T(8,128)(2,1)S(1)}, u32[]{:S(2)}, u32[]{:S(2)}) collective-permute-start(bf16[448,512]{1,0:T(8,128)(2,1)} %get-tuple-element.45), channel_id=1, source_target_pairs={{0,16},{1,17},{2,18},{3,19},{4,20},{5,21},{6,22},{7,23},{8,24},{9,... | collective-permute-start | bytes 1376264 | tf_op jit(solution)/shard_map/ppermute | solution.py:742
  47.4 7.7 %collective-permute-start.1 = (bf16[224,512]{1,0:T(8,128)(2,1)S(1)}, bf16[224,512]{1,0:T(8,128)(2,1)S(1)}, u32[]{:S(2)}, u32[]{:S(2)}) collective-permute-start(bf16[224,512]{1,0:T(8,128)(2,1)S(1)} %broadcast_select_fusion.8), channel_id=1, source_target_pairs={{0,1},{1,0},{2,3},{3,2},{4,5},{5,4},{6,7},{7,6},{8,9},{9,8},{10,11... | collective-permute-start | bytes 688136 | tf_op jit(solution)/shard_map/ppermute | solution.py:742
  49.1 8.2 %collective-permute-start.9 = (bf16[224,512]{1,0:T(8,128)(2,1)S(1)}, bf16[224,512]{1,0:T(8,128)(2,1)S(1)}, u32[]{:S(2)}, u32[]{:S(2)}) collective-permute-start(bf16[224,512]{1,0:T(8,128)(2,1)S(1)} %broadcast_select_fusion.5), channel_id=1, source_target_pairs={{0,2},{1,3},{2,0},{3,1},{4,6},{5,7},{6,4},{7,5},{8,10},{9,11},{10,... | collective-permute-start | bytes 688136 | tf_op jit(solution)/shard_map/ppermute | solution.py:742
  50.9 8.2 %collective-permute-start.17 = (bf16[224,512]{1,0:T(8,128)(2,1)S(1)}, bf16[224,512]{1,0:T(8,128)(2,1)S(1)}, u32[]{:S(2)}, u32[]{:S(2)}) collective-permute-start(bf16[224,512]{1,0:T(8,128)(2,1)S(1)} %broadcast_select_fusion.2), channel_id=1, source_target_pairs={{0,4},{1,5},{2,6},{3,7},{4,0},{5,1},{6,2},{7,3},{8,12},{9,13},{10,... | collective-permute-start | bytes 688136 | tf_op jit(solution)/shard_map/ppermute | solution.py:742
  55.2 4.9 %collective-permute-start.2 = (bf16[112,512]{1,0:T(8,128)(2,1)S(1)}, bf16[112,512]{1,0:T(8,128)(2,1)S(1)}, u32[]{:S(2)}, u32[]{:S(2)}) collective-permute-start(bf16[112,512]{1,0:T(8,128)(2,1)S(1)} %broadcast_select_fusion.17), channel_id=1, source_target_pairs={{0,2},{1,3},{2,0},{3,1},{4,6},{5,7},{6,4},{7,5},{8,10},{9,11},{10,... | collective-permute-start | bytes 344072 | tf_op jit(solution)/shard_map/ppermute | solution.py:742
  57.4 5.4 %collective-permute-start.10 = (bf16[112,512]{1,0:T(8,128)(2,1)S(1)}, bf16[112,512]{1,0:T(8,128)(2,1)S(1)}, u32[]{:S(2)}, u32[]{:S(2)}) collective-permute-start(bf16[112,512]{1,0:T(8,128)(2,1)S(1)} %broadcast_select_fusion.14), channel_id=1, source_target_pairs={{0,4},{1,5},{2,6},{3,7},{4,0},{5,1},{6,2},{7,3},{8,12},{9,13},{10,... | collective-permute-start | bytes 344072 | tf_op jit(solution)/shard_map/ppermute | solution.py:742
  59.2 5.5 %collective-permute-start.18 = (bf16[112,512]{1,0:T(8,128)(2,1)S(1)}, bf16[112,512]{1,0:T(8,128)(2,1)S(1)}, u32[]{:S(2)}, u32[]{:S(2)}) collective-permute-start(bf16[112,512]{1,0:T(8,128)(2,1)S(1)} %broadcast_select_fusion.11), channel_id=1, source_target_pairs={{0,1},{1,0},{2,3},{3,2},{4,5},{5,4},{6,7},{7,6},{8,9},{9,8},{10,11... | collective-permute-start | bytes 344072 | tf_op jit(solution)/shard_map/ppermute | solution.py:742
  60.1 5.6 %collective-permute-start.3 = (bf16[56,512]{1,0:T(8,128)(2,1)S(1)}, bf16[56,512]{1,0:T(8,128)(2,1)S(1)}, u32[]{:S(2)}, u32[]{:S(2)}) collective-permute-start(bf16[56,512]{1,0:T(8,128)(2,1)S(1)} %broadcast_select_fusion.26), channel_id=1, source_target_pairs={{0,4},{1,5},{2,6},{3,7},{4,0},{5,1},{6,2},{7,3},{8,12},{9,13},{10,... | collective-permute-start | bytes 172040 | tf_op jit(solution)/shard_map/ppermute | solution.py:742
  62.9 5.8 %collective-permute-start.11 = (bf16[56,512]{1,0:T(8,128)(2,1)S(1)}, bf16[56,512]{1,0:T(8,128)(2,1)S(1)}, u32[]{:S(2)}, u32[]{:S(2)}) collective-permute-start(bf16[56,512]{1,0:T(8,128)(2,1)S(1)} %broadcast_select_fusion.23), channel_id=1, source_target_pairs={{0,1},{1,0},{2,3},{3,2},{4,5},{5,4},{6,7},{7,6},{8,9},{9,8},{10,11... | collective-permute-start | bytes 172040 | tf_op jit(solution)/shard_map/ppermute | solution.py:742
  64.7 4.6 %collective-permute-start.19 = (bf16[56,512]{1,0:T(8,128)(2,1)S(1)}, bf16[56,512]{1,0:T(8,128)(2,1)S(1)}, u32[]{:S(2)}, u32[]{:S(2)}) collective-permute-start(bf16[56,512]{1,0:T(8,128)(2,1)S(1)} %broadcast_select_fusion.20), channel_id=1, source_target_pairs={{0,2},{1,3},{2,0},{3,1},{4,6},{5,7},{6,4},{7,5},{8,10},{9,11},{10,... | collective-permute-start | bytes 172040 | tf_op jit(solution)/shard_map/ppermute | solution.py:742
  65.8 6.9 %collective-permute-start.4 = (bf16[56,512]{1,0:T(8,128)(2,1)S(1)}, bf16[56,512]{1,0:T(8,128)(2,1)S(1)}, u32[]{:S(2)}, u32[]{:S(2)}) collective-permute-start(bf16[56,512]{1,0:T(8,128)(2,1)S(1)} %add_convert_fusion.14), channel_id=1, source_target_pairs={{0,8},{1,9},{2,10},{3,11},{4,12},{5,13},{6,14},{7,15},{8,0},{9,1},... | collective-permute-start | bytes 172040 | tf_op jit(solution)/shard_map/ppermute | solution.py:742
  68.8 5.6 %collective-permute-start.12 = (bf16[56,512]{1,0:T(8,128)(2,1)S(1)}, bf16[56,512]{1,0:T(8,128)(2,1)S(1)}, u32[]{:S(2)}, u32[]{:S(2)}) collective-permute-start(bf16[56,512]{1,0:T(8,128)(2,1)S(1)} %add_convert_fusion.12), channel_id=1, source_target_pairs={{0,8},{1,9},{2,10},{3,11},{4,12},{5,13},{6,14},{7,15},{8,0},{9,1},... | collective-permute-start | bytes 172040 | tf_op jit(solution)/shard_map/ppermute | solution.py:742
  69.3 6.3 %collective-permute-start.20 = (bf16[56,512]{1,0:T(8,128)(2,1)S(1)}, bf16[56,512]{1,0:T(8,128)(2,1)S(1)}, u32[]{:S(2)}, u32[]{:S(2)}) collective-permute-start(bf16[56,512]{1,0:T(8,128)(2,1)S(1)} %add_convert_fusion.10), channel_id=1, source_target_pairs={{0,8},{1,9},{2,10},{3,11},{4,12},{5,13},{6,14},{7,15},{8,0},{9,1},... | collective-permute-start | bytes 172040 | tf_op jit(solution)/shard_map/ppermute | solution.py:742
  72.7 4.2 %collective-permute-start.5 = (bf16[56,512]{1,0:T(8,128)(2,1)S(1)}, bf16[56,512]{1,0:T(8,128)(2,1)S(1)}, u32[]{:S(2)}, u32[]{:S(2)}) collective-permute-start(bf16[56,512]{1,0:T(8,128)(2,1)S(1)} %add_convert_fusion.13), channel_id=1, source_target_pairs={{0,4},{1,5},{2,6},{3,7},{4,0},{5,1},{6,2},{7,3},{8,12},{9,13},{10,... | collective-permute-start | bytes 172040 | tf_op jit(solution)/shard_map/ppermute | solution.py:742
  74.4 4.3 %collective-permute-start.13 = (bf16[56,512]{1,0:T(8,128)(2,1)S(1)}, bf16[56,512]{1,0:T(8,128)(2,1)S(1)}, u32[]{:S(2)}, u32[]{:S(2)}) collective-permute-start(bf16[56,512]{1,0:T(8,128)(2,1)S(1)} %add_convert_fusion.11), channel_id=1, source_target_pairs={{0,1},{1,0},{2,3},{3,2},{4,5},{5,4},{6,7},{7,6},{8,9},{9,8},{10,11... | collective-permute-start | bytes 172040 | tf_op jit(solution)/shard_map/ppermute | solution.py:742
  75.6 4.2 %collective-permute-start.21 = (bf16[56,512]{1,0:T(8,128)(2,1)S(1)}, bf16[56,512]{1,0:T(8,128)(2,1)S(1)}, u32[]{:S(2)}, u32[]{:S(2)}) collective-permute-start(bf16[56,512]{1,0:T(8,128)(2,1)S(1)} %add_convert_fusion.9), channel_id=1, source_target_pairs={{0,2},{1,3},{2,0},{3,1},{4,6},{5,7},{6,4},{7,5},{8,10},{9,11},{10,... | collective-permute-start | bytes 172040 | tf_op jit(solution)/shard_map/ppermute | solution.py:742
  77.0 5.2 %collective-permute-start.6 = (bf16[112,512]{1,0:T(8,128)(2,1)S(1)}, bf16[112,512]{1,0:T(8,128)(2,1)S(1)}, u32[]{:S(2)}, u32[]{:S(2)}) collective-permute-start(bf16[112,512]{1,0:T(8,128)(2,1)S(1)} %pad_maximum_fusion.6), channel_id=1, source_target_pairs={{0,2},{1,3},{2,0},{3,1},{4,6},{5,7},{6,4},{7,5},{8,10},{9,11},{10,... | collective-permute-start | bytes 344072 | tf_op jit(solution)/shard_map/ppermute | solution.py:742
  78.7 5.7 %collective-permute-start.14 = (bf16[112,512]{1,0:T(8,128)(2,1)S(1)}, bf16[112,512]{1,0:T(8,128)(2,1)S(1)}, u32[]{:S(2)}, u32[]{:S(2)}) collective-permute-start(bf16[112,512]{1,0:T(8,128)(2,1)S(1)} %pad_maximum_fusion.7), channel_id=1, source_target_pairs={{0,4},{1,5},{2,6},{3,7},{4,0},{5,1},{6,2},{7,3},{8,12},{9,13},{10,... | collective-permute-start | bytes 344072 | tf_op jit(solution)/shard_map/ppermute | solution.py:742
  79.9 5.6 %collective-permute-start.22 = (bf16[112,512]{1,0:T(8,128)(2,1)S(1)}, bf16[112,512]{1,0:T(8,128)(2,1)S(1)}, u32[]{:S(2)}, u32[]{:S(2)}) collective-permute-start(bf16[112,512]{1,0:T(8,128)(2,1)S(1)} %pad_maximum_fusion.8), channel_id=1, source_target_pairs={{0,1},{1,0},{2,3},{3,2},{4,5},{5,4},{6,7},{7,6},{8,9},{9,8},{10,11... | collective-permute-start | bytes 344072 | tf_op jit(solution)/shard_map/ppermute | solution.py:742
  82.3 6.1 %collective-permute-start.7 = (bf16[224,512]{1,0:T(8,128)(2,1)S(1)}, bf16[224,512]{1,0:T(8,128)(2,1)S(1)}, u32[]{:S(2)}, u32[]{:S(2)}) collective-permute-start(bf16[224,512]{1,0:T(8,128)(2,1)S(1)} %pad_maximum_fusion.3), channel_id=1, source_target_pairs={{0,1},{1,0},{2,3},{3,2},{4,5},{5,4},{6,7},{7,6},{8,9},{9,8},{10,11... | collective-permute-start | bytes 688136 | tf_op jit(solution)/shard_map/ppermute | solution.py:742
  84.5 6.1 %collective-permute-start.15 = (bf16[224,512]{1,0:T(8,128)(2,1)S(1)}, bf16[224,512]{1,0:T(8,128)(2,1)S(1)}, u32[]{:S(2)}, u32[]{:S(2)}) collective-permute-start(bf16[224,512]{1,0:T(8,128)(2,1)S(1)} %pad_maximum_fusion.4), channel_id=1, source_target_pairs={{0,2},{1,3},{2,0},{3,1},{4,6},{5,7},{6,4},{7,5},{8,10},{9,11},{10,... | collective-permute-start | bytes 688136 | tf_op jit(solution)/shard_map/ppermute | solution.py:742
  85.5 6.1 %collective-permute-start.23 = (bf16[224,512]{1,0:T(8,128)(2,1)S(1)}, bf16[224,512]{1,0:T(8,128)(2,1)S(1)}, u32[]{:S(2)}, u32[]{:S(2)}) collective-permute-start(bf16[224,512]{1,0:T(8,128)(2,1)S(1)} %pad_maximum_fusion.5), channel_id=1, source_target_pairs={{0,4},{1,5},{2,6},{3,7},{4,0},{5,1},{6,2},{7,3},{8,12},{9,13},{10,... | collective-permute-start | bytes 688136 | tf_op jit(solution)/shard_map/ppermute | solution.py:742
  88.5 5.2 %collective-permute-start.24 = (bf16[448,512]{1,0:T(8,128)(2,1)S(1)}, bf16[448,512]{1,0:T(8,128)(2,1)S(1)}, u32[]{:S(2)}, u32[]{:S(2)}) collective-permute-start(bf16[448,512]{1,0:T(8,128)(2,1)S(1)} %pad_maximum_fusion.a0), channel_id=1, source_target_pairs={{0,16},{1,17},{2,18},{3,19},{4,20},{5,21},{6,22},{7,23},{8,24},{9,... | collective-permute-start | bytes 1376264 | tf_op jit(solution)/shard_map/ppermute | solution.py:742
  90.7 3.0 %collective-permute-start.25 = (bf16[448,512]{1,0:T(8,128)(2,1)S(1)}, bf16[448,512]{1,0:T(8,128)(2,1)S(1)}, u32[]{:S(2)}, u32[]{:S(2)}) collective-permute-start(bf16[448,512]{1,0:T(8,128)(2,1)S(1)} %pad_maximum_fusion.1.a1), channel_id=1, source_target_pairs={{0,16},{1,17},{2,18},{3,19},{4,20},{5,21},{6,22},{7,23},{8,24},{9,... | collective-permute-start | bytes 1376264 | tf_op jit(solution)/shard_map/ppermute | solution.py:742
  91.8 2.0 %collective-permute-start.26 = (bf16[448,512]{1,0:T(8,128)(2,1)S(1)}, bf16[448,512]{1,0:T(8,128)(2,1)S(1)}, u32[]{:S(2)}, u32[]{:S(2)}) collective-permute-start(bf16[448,512]{1,0:T(8,128)(2,1)S(1)} %pad_maximum_fusion.2.a2), channel_id=1, source_target_pairs={{0,16},{1,17},{2,18},{3,19},{4,20},{5,21},{6,22},{7,23},{8,24},{9,... | collective-permute-start | bytes 1376264 | tf_op jit(solution)/shard_map/ppermute | solution.py:742

commit v5 on v4

--- a/solution.py
+++ b/solution.py
@@ -45,7 +45,8 @@
 def gelu_split(x):
     p = 0.5 + 0.5 * jnp.tanh(x * (C0 + C1 * (x * x)))
     y = (x * p).astype(BF)
-    xb, pb, qb = x.astype(BF), p.astype(BF), (1.0 - p).astype(BF)
+    xb, pb = x.astype(BF), p.astype(BF)
+    qb = 1.0 - pb
     return y, pb + y * qb * (2.0 * C0 + (6.0 * C1) * (xb * xb))
 
 

time: 96.5 us -> 96.7 us (level)
  Pallas kernels: 47.8 us -> 46.6 us
  starting transfers between devices: 29.5 us -> 30.6 us
    pallas_call x1, Pallas kernels: 43.4 us -> 42.3 us  [local_step(): pl.pallas_call(kernel, out_shape=(jax.ShapeDtypeStruct((rows, d), BF), ja...]
    ppermute x27, starting transfers between devices: 29.5 us -> 30.6 us  [exchange(): return lax.ppermute(a, AXES, [(i, i ^ bit) for i in range(count)])]
  transfers between devices with their start and end apart: 27 -> 27, of which waited for: 14 -> 12; matrix products, arithmetic and copies ran while one was open for 3% -> 3% of each run, Pallas kernels for 2% -> 2%
where the time goes in v5:
time: 96.7 us; the launch traced here: 96.2 us
  Pallas kernels  46.6 us (48%)
  starting transfers between devices  30.6 us (32%)
  waiting for transfers between devices  15.2 us (16%)
  other arithmetic  2.64 us (3%)
  between operations  1.19 us (1%)
    pallas_call x1, Pallas kernels, local_step(): pl.pallas_call(kernel, out_shape=(jax.ShapeDtypeStruct((rows, d), BF), ja...  42.3 us
    ppermute x27, starting transfers between devices, exchange(): return lax.ppermute(a, AXES, [(i, i ^ bit) for i in range(count)])  30.6 us
    ppermute x27, waiting for transfers between devices, exchange(): return lax.ppermute(a, AXES, [(i, i ^ bit) for i in range(count)])  15.2 us
    pallas_call x1, Pallas kernels, unpack(): pl.pallas_call(spread_other, out_shape=big + (vec, vec, pair, pair, vec,...  2.47 us
  transfers between devices with their start and end apart: 27, of which 12 were waited for; matrix products, arithmetic and copies ran while one was open for 3% of the time, Pallas kernels for 2%

profile of v5, /device:TPU:0, one launch (start us, length us, event | category | flops | bytes accessed | tf_op | source)
XLA Modules:
  0.0 96.2 jit_solution(5045298630701951708)
XLA Ops:
  0.7 42.3 %slab_step.1 = (bf16[1024,512]{1,0:T(8,128)(2,1)}, bf16[1024,512]{1,0:T(8,128)(2,1)}, bf16[448,512]{1,0:T(8,128)(2,1)}, bf16[448,512]{1,0:T(8,128)(2,1)}, bf16[4...) custom-call(s32[16]{0:T(128)} %grid_ref.1, s32[3]{0:T(128)} %keep_ref.1, ...), custom_call_target="tpu_custom_call" | custom-call | tf_op jit(solution)/shard_map/slab_step/pallas_call | solution.py:636
  42.9 1.0 %collective-permute-start = (bf16[448,512]{1,0:T(8,128)(2,1)}, bf16[448,512]{1,0:T(8,128)(2,1)S(1)}, u32[]{:S(2)}, u32[]{:S(2)}) collective-permute-start(bf16[448,512]{1,0:T(8,128)(2,1)} %get-tuple-element.41), channel_id=1, source_target_pairs={{0,16},{1,17},{2,18},{3,19},{4,20},{5,21},{6,22},{7,23},{8,24},{9,... | collective-permute-start | bytes 1376264 | tf_op jit(solution)/shard_map/ppermute | solution.py:743
  43.9 0.1 collective-permute-start.8
  44.0 0.4 collective-permute-start.16
  44.4 1.1 %collective-permute-done = bf16[448,512]{1,0:T(8,128)(2,1)S(1)} collective-permute-done((bf16[448,512]{1,0:T(8,128)(2,1)}, bf16[448,512]{1,0:T(8,128)(2,1)S(1)}, u32[]{:S(2)}, u32[]{:S(2)}) %collective-permute-start) | collective-permute-done | bytes 458784 | tf_op jit(solution)/shard_map/ppermute | solution.py:743
  45.6 1.1 %add_convert_fusion.2 = bf16[448,512]{1,0:T(8,128)(2,1)S(1)} fusion(bf16[448,512]{1,0:T(8,128)(2,1)S(1)} %collective-permute-done, bf16[448,512]{1,0:T(8,128)(2,1)} %get-tuple-element.40), kind=kLoop, calls=%fused_computation.2 | loop fusion | flops 917504 | bytes 1376256 | tf_op jit(solution)/shard_map/convert_element_type | solution.py:747
  46.8 2.4 %collective-permute-start.1 = (bf16[224,512]{1,0:T(8,128)(2,1)S(1)}, bf16[224,512]{1,0:T(8,128)(2,1)S(1)}, u32[]{:S(2)}, u32[]{:S(2)}) collective-permute-start(bf16[224,512]{1,0:T(8,128)(2,1)S(1)} %broadcast_select_fusion.8), channel_id=1, source_target_pairs={{0,1},{1,0},{2,3},{3,2},{4,5},{5,4},{6,7},{7,6},{8,9},{9,8},{10,11... | collective-permute-start | bytes 688136 | tf_op jit(solution)/shard_map/ppermute | solution.py:743
  49.2 0.1 add_convert_fusion.1
  49.3 2.1 %collective-permute-start.9 = (bf16[224,512]{1,0:T(8,128)(2,1)S(1)}, bf16[224,512]{1,0:T(8,128)(2,1)S(1)}, u32[]{:S(2)}, u32[]{:S(2)}) collective-permute-start(bf16[224,512]{1,0:T(8,128)(2,1)S(1)} %broadcast_select_fusion.5), channel_id=1, source_target_pairs={{0,2},{1,3},{2,0},{3,1},{4,6},{5,7},{6,4},{7,5},{8,10},{9,11},{10,... | collective-permute-start | bytes 688136 | tf_op jit(solution)/shard_map/ppermute | solution.py:743
  51.4 0.1 add_convert_fusion
  51.6 0.2 collective-permute-start.17
  51.8 3.5 %collective-permute-done.1 = bf16[224,512]{1,0:T(8,128)(2,1)S(1)} collective-permute-done((bf16[224,512]{1,0:T(8,128)(2,1)S(1)}, bf16[224,512]{1,0:T(8,128)(2,1)S(1)}, u32[]{:S(2)}, u32[]{:S(2)}) %collective-permute-start.1) | collective-permute-done | bytes 229408 | tf_op jit(solution)/shard_map/ppermute | solution.py:743
  55.3 0.1 add_convert_fusion.5
  55.4 1.9 %collective-permute-start.2 = (bf16[112,512]{1,0:T(8,128)(2,1)S(1)}, bf16[112,512]{1,0:T(8,128)(2,1)S(1)}, u32[]{:S(2)}, u32[]{:S(2)}) collective-permute-start(bf16[112,512]{1,0:T(8,128)(2,1)S(1)} %broadcast_select_fusion.17), channel_id=1, source_target_pairs={{0,2},{1,3},{2,0},{3,1},{4,6},{5,7},{6,4},{7,5},{8,10},{9,11},{10,... | collective-permute-start | bytes 344072 | tf_op jit(solution)/shard_map/ppermute | solution.py:743
  57.3 0.1 add_convert_fusion.4
  57.4 1.4 %collective-permute-start.10 = (bf16[112,512]{1,0:T(8,128)(2,1)S(1)}, bf16[112,512]{1,0:T(8,128)(2,1)S(1)}, u32[]{:S(2)}, u32[]{:S(2)}) collective-permute-start(bf16[112,512]{1,0:T(8,128)(2,1)S(1)} %broadcast_select_fusion.14), channel_id=1, source_target_pairs={{0,4},{1,5},{2,6},{3,7},{4,0},{5,1},{6,2},{7,3},{8,12},{9,13},{10,... | collective-permute-start | bytes 344072 | tf_op jit(solution)/shard_map/ppermute | solution.py:743
  58.8 0.1 add_convert_fusion.3
  58.9 0.8 collective-permute-start.18
  59.7 0.6 collective-permute-done.2
  60.4 1.2 %collective-permute-start.3 = (bf16[56,512]{1,0:T(8,128)(2,1)S(1)}, bf16[56,512]{1,0:T(8,128)(2,1)S(1)}, u32[]{:S(2)}, u32[]{:S(2)}) collective-permute-start(bf16[56,512]{1,0:T(8,128)(2,1)S(1)} %broadcast_select_fusion.26), channel_id=1, source_target_pairs={{0,4},{1,5},{2,6},{3,7},{4,0},{5,1},{6,2},{7,3},{8,12},{9,13},{10,... | collective-permute-start | bytes 172040 | tf_op jit(solution)/shard_map/ppermute | solution.py:743
  61.6 1.0 %collective-permute-done.10 = bf16[112,512]{1,0:T(8,128)(2,1)S(1)} collective-permute-done((bf16[112,512]{1,0:T(8,128)(2,1)S(1)}, bf16[112,512]{1,0:T(8,128)(2,1)S(1)}, u32[]{:S(2)}, u32[]{:S(2)}) %collective-permute-start.10) | collective-permute-done | bytes 114720 | tf_op jit(solution)/shard_map/ppermute | solution.py:743
  62.6 2.1 %collective-permute-start.11 = (bf16[56,512]{1,0:T(8,128)(2,1)S(1)}, bf16[56,512]{1,0:T(8,128)(2,1)S(1)}, u32[]{:S(2)}, u32[]{:S(2)}) collective-permute-start(bf16[56,512]{1,0:T(8,128)(2,1)S(1)} %broadcast_select_fusion.23), channel_id=1, source_target_pairs={{0,1},{1,0},{2,3},{3,2},{4,5},{5,4},{6,7},{7,6},{8,9},{9,8},{10,11... | collective-permute-start | bytes 172040 | tf_op jit(solution)/shard_map/ppermute | solution.py:743
  64.8 0.1 collective-permute-start.19
  64.9 3.8 %collective-permute-start.4 = (bf16[56,512]{1,0:T(8,128)(2,1)S(1)}, bf16[56,512]{1,0:T(8,128)(2,1)S(1)}, u32[]{:S(2)}, u32[]{:S(2)}) collective-permute-start(bf16[56,512]{1,0:T(8,128)(2,1)S(1)} %add_convert_fusion.14), channel_id=1, source_target_pairs={{0,8},{1,9},{2,10},{3,11},{4,12},{5,13},{6,14},{7,15},{8,0},{9,1},... | collective-permute-start | bytes 172040 | tf_op jit(solution)/shard_map/ppermute | solution.py:743
  68.8 1.1 %collective-permute-start.12 = (bf16[56,512]{1,0:T(8,128)(2,1)S(1)}, bf16[56,512]{1,0:T(8,128)(2,1)S(1)}, u32[]{:S(2)}, u32[]{:S(2)}) collective-permute-start(bf16[56,512]{1,0:T(8,128)(2,1)S(1)} %add_convert_fusion.12), channel_id=1, source_target_pairs={{0,8},{1,9},{2,10},{3,11},{4,12},{5,13},{6,14},{7,15},{8,0},{9,1},... | collective-permute-start | bytes 172040 | tf_op jit(solution)/shard_map/ppermute | solution.py:743
  70.0 2.3 %collective-permute-start.20 = (bf16[56,512]{1,0:T(8,128)(2,1)S(1)}, bf16[56,512]{1,0:T(8,128)(2,1)S(1)}, u32[]{:S(2)}, u32[]{:S(2)}) collective-permute-start(bf16[56,512]{1,0:T(8,128)(2,1)S(1)} %add_convert_fusion.10), channel_id=1, source_target_pairs={{0,8},{1,9},{2,10},{3,11},{4,12},{5,13},{6,14},{7,15},{8,0},{9,1},... | collective-permute-start | bytes 172040 | tf_op jit(solution)/shard_map/ppermute | solution.py:743
  72.3 1.1 %collective-permute-done.4 = bf16[56,512]{1,0:T(8,128)(2,1)S(1)} collective-permute-done((bf16[56,512]{1,0:T(8,128)(2,1)S(1)}, bf16[56,512]{1,0:T(8,128)(2,1)S(1)}, u32[]{:S(2)}, u32[]{:S(2)}) %collective-permute-start.4) | collective-permute-done | bytes 57376 | tf_op jit(solution)/shard_map/ppermute | solution.py:743
  73.4 1.2 %collective-permute-done.12 = bf16[56,512]{1,0:T(8,128)(2,1)S(1)} collective-permute-done((bf16[56,512]{1,0:T(8,128)(2,1)S(1)}, bf16[56,512]{1,0:T(8,128)(2,1)S(1)}, u32[]{:S(2)}, u32[]{:S(2)}) %collective-permute-start.12) | collective-permute-done | bytes 57376 | tf_op jit(solution)/shard_map/ppermute | solution.py:743
  74.6 1.1 %collective-permute-start.13 = (bf16[56,512]{1,0:T(8,128)(2,1)S(1)}, bf16[56,512]{1,0:T(8,128)(2,1)S(1)}, u32[]{:S(2)}, u32[]{:S(2)}) collective-permute-start(bf16[56,512]{1,0:T(8,128)(2,1)S(1)} %add_convert_fusion.11), channel_id=1, source_target_pairs={{0,1},{1,0},{2,3},{3,2},{4,5},{5,4},{6,7},{7,6},{8,9},{9,8},{10,11... | collective-permute-start | bytes 172040 | tf_op jit(solution)/shard_map/ppermute | solution.py:743
  75.7 1.7 %collective-permute-start.21 = (bf16[56,512]{1,0:T(8,128)(2,1)S(1)}, bf16[56,512]{1,0:T(8,128)(2,1)S(1)}, u32[]{:S(2)}, u32[]{:S(2)}) collective-permute-start(bf16[56,512]{1,0:T(8,128)(2,1)S(1)} %add_convert_fusion.9), channel_id=1, source_target_pairs={{0,2},{1,3},{2,0},{3,1},{4,6},{5,7},{6,4},{7,5},{8,10},{9,11},{10,... | collective-permute-start | bytes 172040 | tf_op jit(solution)/shard_map/ppermute | solution.py:743
  77.4 0.2 collective-permute-done.5
  77.6 1.2 %collective-permute-start.6 = (bf16[112,512]{1,0:T(8,128)(2,1)S(1)}, bf16[112,512]{1,0:T(8,128)(2,1)S(1)}, u32[]{:S(2)}, u32[]{:S(2)}) collective-permute-start(bf16[112,512]{1,0:T(8,128)(2,1)S(1)} %pad_maximum_fusion.6), channel_id=1, source_target_pairs={{0,2},{1,3},{2,0},{3,1},{4,6},{5,7},{6,4},{7,5},{8,10},{9,11},{10,... | collective-permute-start | bytes 344072 | tf_op jit(solution)/shard_map/ppermute | solution.py:743
  78.9 1.0 %collective-permute-start.14 = (bf16[112,512]{1,0:T(8,128)(2,1)S(1)}, bf16[112,512]{1,0:T(8,128)(2,1)S(1)}, u32[]{:S(2)}, u32[]{:S(2)}) collective-permute-start(bf16[112,512]{1,0:T(8,128)(2,1)S(1)} %pad_maximum_fusion.7), channel_id=1, source_target_pairs={{0,4},{1,5},{2,6},{3,7},{4,0},{5,1},{6,2},{7,3},{8,12},{9,13},{10,... | collective-permute-start | bytes 344072 | tf_op jit(solution)/shard_map/ppermute | solution.py:743
  80.0 1.1 %collective-permute-start.22 = (bf16[112,512]{1,0:T(8,128)(2,1)S(1)}, bf16[112,512]{1,0:T(8,128)(2,1)S(1)}, u32[]{:S(2)}, u32[]{:S(2)}) collective-permute-start(bf16[112,512]{1,0:T(8,128)(2,1)S(1)} %pad_maximum_fusion.8), channel_id=1, source_target_pairs={{0,1},{1,0},{2,3},{3,2},{4,5},{5,4},{6,7},{7,6},{8,9},{9,8},{10,11... | collective-permute-start | bytes 344072 | tf_op jit(solution)/shard_map/ppermute | solution.py:743
  81.1 2.2 %collective-permute-done.6 = bf16[112,512]{1,0:T(8,128)(2,1)S(1)} collective-permute-done((bf16[112,512]{1,0:T(8,128)(2,1)S(1)}, bf16[112,512]{1,0:T(8,128)(2,1)S(1)}, u32[]{:S(2)}, u32[]{:S(2)}) %collective-permute-start.6) | collective-permute-done | bytes 114720 | tf_op jit(solution)/shard_map/ppermute | solution.py:743
  83.4 0.5 collective-permute-start.7
  83.9 0.7 collective-permute-done.14
  84.7 0.3 collective-permute-start.15
  85.1 2.3 %collective-permute-start.23 = (bf16[224,512]{1,0:T(8,128)(2,1)S(1)}, bf16[224,512]{1,0:T(8,128)(2,1)S(1)}, u32[]{:S(2)}, u32[]{:S(2)}) collective-permute-start(bf16[224,512]{1,0:T(8,128)(2,1)S(1)} %pad_maximum_fusion.5), channel_id=1, source_target_pairs={{0,4},{1,5},{2,6},{3,7},{4,0},{5,1},{6,2},{7,3},{8,12},{9,13},{10,... | collective-permute-start | bytes 688136 | tf_op jit(solution)/shard_map/ppermute | solution.py:743
  87.3 2.2 %collective-permute-done.7 = bf16[224,512]{1,0:T(8,128)(2,1)S(1)} collective-permute-done((bf16[224,512]{1,0:T(8,128)(2,1)S(1)}, bf16[224,512]{1,0:T(8,128)(2,1)S(1)}, u32[]{:S(2)}, u32[]{:S(2)}) %collective-permute-start.7) | collective-permute-done | bytes 229408 | tf_op jit(solution)/shard_map/ppermute | solution.py:743
  89.5 0.1 broadcast_select_fusion.7
  89.7 1.0 %collective-permute-done.15 = bf16[224,512]{1,0:T(8,128)(2,1)S(1)} collective-permute-done((bf16[224,512]{1,0:T(8,128)(2,1)S(1)}, bf16[224,512]{1,0:T(8,128)(2,1)S(1)}, u32[]{:S(2)}, u32[]{:S(2)}) %collective-permute-start.15) | collective-permute-done | bytes 229408 | tf_op jit(solution)/shard_map/ppermute | solution.py:743
  90.8 0.1 broadcast_select_fusion.4
  91.0 0.4 collective-permute-done.23
  91.3 0.1 broadcast_select_fusion.1
  91.5 0.2 collective-permute-start.26
  91.7 1.8 %spread_mine.1 = (f32[2,512,512]{2,1,0:T(8,128)}, f32[2,512,512]{2,1,0:T(8,128)}, f32[2,2,8,64,64]{4,3,2,1,0:T(8,128)}, f32[2,2,8,64,64]{4,3,2,1,0:T(8,128)}) custom-call(s32[1]{0:T(128)} %bitcast.core_ref, bf16[448,512]{1,0:T(8,128)(2,1)S(1)} %pad_maximum_fusion.a0, bf16[448,512]{1,0:T(8,128)(2,1)S(1)} %pad_maximum_fusion.1.a1, ...), custom_call_target="tpu_custom_call" | custom-call | flops 1048576 | bytes 4194304 | tf_op jit(solution)/shard_map/spread_mine/pallas_call | solution.py:709
  93.5 2.5 %spread_other.1 = (f32[2,512,512]{2,1,0:T(8,128)}, f32[2,512,512]{2,1,0:T(8,128)}, f32[2,2,8,64,64]{4,3,2,1,0:T(8,128)}, f32[2,2,8,64,64]{4,3,2,1,0:T(8,128)}, f...) custom-call(s32[1]{0:T(128)} %bitcast.core_ref, ...), custom_call_target="tpu_custom_call", output_to_operand_aliasing={{0}: (7, {}), {1}: (8, {}), {2}: (9, {}), {3}: (10, {})} | custom-call | tf_op jit(solution)/shard_map/spread_other/pallas_call | solution.py:729
  (55 shorter events, 1.1 us)
Async XLA Ops:
  42.9 6.2 %copy-start.1 = (bf16[448,512]{1,0:T(8,128)(2,1)S(1)}, bf16[448,512]{1,0:T(8,128)(2,1)}, u32[]{:S(2)}) copy-start(bf16[448,512]{1,0:T(8,128)(2,1)} %get-tuple-element.42) | copy-start | bytes 1376260
  42.9 8.5 %copy-start = (bf16[448,512]{1,0:T(8,128)(2,1)S(1)}, bf16[448,512]{1,0:T(8,128)(2,1)}, u32[]{:S(2)}) copy-start(bf16[448,512]{1,0:T(8,128)(2,1)} %get-tuple-element.44) | copy-start | bytes 1376260
  42.9 2.6 %collective-permute-start = (bf16[448,512]{1,0:T(8,128)(2,1)}, bf16[448,512]{1,0:T(8,128)(2,1)S(1)}, u32[]{:S(2)}, u32[]{:S(2)}) collective-permute-start(bf16[448,512]{1,0:T(8,128)(2,1)} %get-tuple-element.41), channel_id=1, source_target_pairs={{0,16},{1,17},{2,18},{3,19},{4,20},{5,21},{6,22},{7,23},{8,24},{9,... | collective-permute-start | bytes 1376264 | tf_op jit(solution)/shard_map/ppermute | solution.py:743
  43.9 5.2 %collective-permute-start.8 = (bf16[448,512]{1,0:T(8,128)(2,1)}, bf16[448,512]{1,0:T(8,128)(2,1)S(1)}, u32[]{:S(2)}, u32[]{:S(2)}) collective-permute-start(bf16[448,512]{1,0:T(8,128)(2,1)} %get-tuple-element.43), channel_id=1, source_target_pairs={{0,16},{1,17},{2,18},{3,19},{4,20},{5,21},{6,22},{7,23},{8,24},{9,... | collective-permute-start | bytes 1376264 | tf_op jit(solution)/shard_map/ppermute | solution.py:743
  44.0 7.4 %collective-permute-start.16 = (bf16[448,512]{1,0:T(8,128)(2,1)}, bf16[448,512]{1,0:T(8,128)(2,1)S(1)}, u32[]{:S(2)}, u32[]{:S(2)}) collective-permute-start(bf16[448,512]{1,0:T(8,128)(2,1)} %get-tuple-element.45), channel_id=1, source_target_pairs={{0,16},{1,17},{2,18},{3,19},{4,20},{5,21},{6,22},{7,23},{8,24},{9,... | collective-permute-start | bytes 1376264 | tf_op jit(solution)/shard_map/ppermute | solution.py:743
  46.8 8.5 %collective-permute-start.1 = (bf16[224,512]{1,0:T(8,128)(2,1)S(1)}, bf16[224,512]{1,0:T(8,128)(2,1)S(1)}, u32[]{:S(2)}, u32[]{:S(2)}) collective-permute-start(bf16[224,512]{1,0:T(8,128)(2,1)S(1)} %broadcast_select_fusion.8), channel_id=1, source_target_pairs={{0,1},{1,0},{2,3},{3,2},{4,5},{5,4},{6,7},{7,6},{8,9},{9,8},{10,11... | collective-permute-start | bytes 688136 | tf_op jit(solution)/shard_map/ppermute | solution.py:743
  49.3 8.0 %collective-permute-start.9 = (bf16[224,512]{1,0:T(8,128)(2,1)S(1)}, bf16[224,512]{1,0:T(8,128)(2,1)S(1)}, u32[]{:S(2)}, u32[]{:S(2)}) collective-permute-start(bf16[224,512]{1,0:T(8,128)(2,1)S(1)} %broadcast_select_fusion.5), channel_id=1, source_target_pairs={{0,2},{1,3},{2,0},{3,1},{4,6},{5,7},{6,4},{7,5},{8,10},{9,11},{10,... | collective-permute-start | bytes 688136 | tf_op jit(solution)/shard_map/ppermute | solution.py:743
  51.6 7.2 %collective-permute-start.17 = (bf16[224,512]{1,0:T(8,128)(2,1)S(1)}, bf16[224,512]{1,0:T(8,128)(2,1)S(1)}, u32[]{:S(2)}, u32[]{:S(2)}) collective-permute-start(bf16[224,512]{1,0:T(8,128)(2,1)S(1)} %broadcast_select_fusion.2), channel_id=1, source_target_pairs={{0,4},{1,5},{2,6},{3,7},{4,0},{5,1},{6,2},{7,3},{8,12},{9,13},{10,... | collective-permute-start | bytes 688136 | tf_op jit(solution)/shard_map/ppermute | solution.py:743
  55.4 4.9 %collective-permute-start.2 = (bf16[112,512]{1,0:T(8,128)(2,1)S(1)}, bf16[112,512]{1,0:T(8,128)(2,1)S(1)}, u32[]{:S(2)}, u32[]{:S(2)}) collective-permute-start(bf16[112,512]{1,0:T(8,128)(2,1)S(1)} %broadcast_select_fusion.17), channel_id=1, source_target_pairs={{0,2},{1,3},{2,0},{3,1},{4,6},{5,7},{6,4},{7,5},{8,10},{9,11},{10,... | collective-permute-start | bytes 344072 | tf_op jit(solution)/shard_map/ppermute | solution.py:743
  57.4 5.2 %collective-permute-start.10 = (bf16[112,512]{1,0:T(8,128)(2,1)S(1)}, bf16[112,512]{1,0:T(8,128)(2,1)S(1)}, u32[]{:S(2)}, u32[]{:S(2)}) collective-permute-start(bf16[112,512]{1,0:T(8,128)(2,1)S(1)} %broadcast_select_fusion.14), channel_id=1, source_target_pairs={{0,4},{1,5},{2,6},{3,7},{4,0},{5,1},{6,2},{7,3},{8,12},{9,13},{10,... | collective-permute-start | bytes 344072 | tf_op jit(solution)/shard_map/ppermute | solution.py:743
  58.9 5.8 %collective-permute-start.18 = (bf16[112,512]{1,0:T(8,128)(2,1)S(1)}, bf16[112,512]{1,0:T(8,128)(2,1)S(1)}, u32[]{:S(2)}, u32[]{:S(2)}) collective-permute-start(bf16[112,512]{1,0:T(8,128)(2,1)S(1)} %broadcast_select_fusion.11), channel_id=1, source_target_pairs={{0,1},{1,0},{2,3},{3,2},{4,5},{5,4},{6,7},{7,6},{8,9},{9,8},{10,11... | collective-permute-start | bytes 344072 | tf_op jit(solution)/shard_map/ppermute | solution.py:743
  60.4 4.5 %collective-permute-start.3 = (bf16[56,512]{1,0:T(8,128)(2,1)S(1)}, bf16[56,512]{1,0:T(8,128)(2,1)S(1)}, u32[]{:S(2)}, u32[]{:S(2)}) collective-permute-start(bf16[56,512]{1,0:T(8,128)(2,1)S(1)} %broadcast_select_fusion.26), channel_id=1, source_target_pairs={{0,4},{1,5},{2,6},{3,7},{4,0},{5,1},{6,2},{7,3},{8,12},{9,13},{10,... | collective-permute-start | bytes 172040 | tf_op jit(solution)/shard_map/ppermute | solution.py:743
  62.6 6.2 %collective-permute-start.11 = (bf16[56,512]{1,0:T(8,128)(2,1)S(1)}, bf16[56,512]{1,0:T(8,128)(2,1)S(1)}, u32[]{:S(2)}, u32[]{:S(2)}) collective-permute-start(bf16[56,512]{1,0:T(8,128)(2,1)S(1)} %broadcast_select_fusion.23), channel_id=1, source_target_pairs={{0,1},{1,0},{2,3},{3,2},{4,5},{5,4},{6,7},{7,6},{8,9},{9,8},{10,11... | collective-permute-start | bytes 172040 | tf_op jit(solution)/shard_map/ppermute | solution.py:743
  64.8 5.1 %collective-permute-start.19 = (bf16[56,512]{1,0:T(8,128)(2,1)S(1)}, bf16[56,512]{1,0:T(8,128)(2,1)S(1)}, u32[]{:S(2)}, u32[]{:S(2)}) collective-permute-start(bf16[56,512]{1,0:T(8,128)(2,1)S(1)} %broadcast_select_fusion.20), channel_id=1, source_target_pairs={{0,2},{1,3},{2,0},{3,1},{4,6},{5,7},{6,4},{7,5},{8,10},{9,11},{10,... | collective-permute-start | bytes 172040 | tf_op jit(solution)/shard_map/ppermute | solution.py:743
  64.9 8.4 %collective-permute-start.4 = (bf16[56,512]{1,0:T(8,128)(2,1)S(1)}, bf16[56,512]{1,0:T(8,128)(2,1)S(1)}, u32[]{:S(2)}, u32[]{:S(2)}) collective-permute-start(bf16[56,512]{1,0:T(8,128)(2,1)S(1)} %add_convert_fusion.14), channel_id=1, source_target_pairs={{0,8},{1,9},{2,10},{3,11},{4,12},{5,13},{6,14},{7,15},{8,0},{9,1},... | collective-permute-start | bytes 172040 | tf_op jit(solution)/shard_map/ppermute | solution.py:743
  68.8 5.8 %collective-permute-start.12 = (bf16[56,512]{1,0:T(8,128)(2,1)S(1)}, bf16[56,512]{1,0:T(8,128)(2,1)S(1)}, u32[]{:S(2)}, u32[]{:S(2)}) collective-permute-start(bf16[56,512]{1,0:T(8,128)(2,1)S(1)} %add_convert_fusion.12), channel_id=1, source_target_pairs={{0,8},{1,9},{2,10},{3,11},{4,12},{5,13},{6,14},{7,15},{8,0},{9,1},... | collective-permute-start | bytes 172040 | tf_op jit(solution)/shard_map/ppermute | solution.py:743
  70.0 5.7 %collective-permute-start.20 = (bf16[56,512]{1,0:T(8,128)(2,1)S(1)}, bf16[56,512]{1,0:T(8,128)(2,1)S(1)}, u32[]{:S(2)}, u32[]{:S(2)}) collective-permute-start(bf16[56,512]{1,0:T(8,128)(2,1)S(1)} %add_convert_fusion.10), channel_id=1, source_target_pairs={{0,8},{1,9},{2,10},{3,11},{4,12},{5,13},{6,14},{7,15},{8,0},{9,1},... | collective-permute-start | bytes 172040 | tf_op jit(solution)/shard_map/ppermute | solution.py:743
  73.4 4.2 %collective-permute-start.5 = (bf16[56,512]{1,0:T(8,128)(2,1)S(1)}, bf16[56,512]{1,0:T(8,128)(2,1)S(1)}, u32[]{:S(2)}, u32[]{:S(2)}) collective-permute-start(bf16[56,512]{1,0:T(8,128)(2,1)S(1)} %add_convert_fusion.13), channel_id=1, source_target_pairs={{0,4},{1,5},{2,6},{3,7},{4,0},{5,1},{6,2},{7,3},{8,12},{9,13},{10,... | collective-permute-start | bytes 172040 | tf_op jit(solution)/shard_map/ppermute | solution.py:743
  74.6 4.3 %collective-permute-start.13 = (bf16[56,512]{1,0:T(8,128)(2,1)S(1)}, bf16[56,512]{1,0:T(8,128)(2,1)S(1)}, u32[]{:S(2)}, u32[]{:S(2)}) collective-permute-start(bf16[56,512]{1,0:T(8,128)(2,1)S(1)} %add_convert_fusion.11), channel_id=1, source_target_pairs={{0,1},{1,0},{2,3},{3,2},{4,5},{5,4},{6,7},{7,6},{8,9},{9,8},{10,11... | collective-permute-start | bytes 172040 | tf_op jit(solution)/shard_map/ppermute | solution.py:743
  75.7 4.2 %collective-permute-start.21 = (bf16[56,512]{1,0:T(8,128)(2,1)S(1)}, bf16[56,512]{1,0:T(8,128)(2,1)S(1)}, u32[]{:S(2)}, u32[]{:S(2)}) collective-permute-start(bf16[56,512]{1,0:T(8,128)(2,1)S(1)} %add_convert_fusion.9), channel_id=1, source_target_pairs={{0,2},{1,3},{2,0},{3,1},{4,6},{5,7},{6,4},{7,5},{8,10},{9,11},{10,... | collective-permute-start | bytes 172040 | tf_op jit(solution)/shard_map/ppermute | solution.py:743
  77.6 5.7 %collective-permute-start.6 = (bf16[112,512]{1,0:T(8,128)(2,1)S(1)}, bf16[112,512]{1,0:T(8,128)(2,1)S(1)}, u32[]{:S(2)}, u32[]{:S(2)}) collective-permute-start(bf16[112,512]{1,0:T(8,128)(2,1)S(1)} %pad_maximum_fusion.6), channel_id=1, source_target_pairs={{0,2},{1,3},{2,0},{3,1},{4,6},{5,7},{6,4},{7,5},{8,10},{9,11},{10,... | collective-permute-start | bytes 344072 | tf_op jit(solution)/shard_map/ppermute | solution.py:743
  78.9 5.7 %collective-permute-start.14 = (bf16[112,512]{1,0:T(8,128)(2,1)S(1)}, bf16[112,512]{1,0:T(8,128)(2,1)S(1)}, u32[]{:S(2)}, u32[]{:S(2)}) collective-permute-start(bf16[112,512]{1,0:T(8,128)(2,1)S(1)} %pad_maximum_fusion.7), channel_id=1, source_target_pairs={{0,4},{1,5},{2,6},{3,7},{4,0},{5,1},{6,2},{7,3},{8,12},{9,13},{10,... | collective-permute-start | bytes 344072 | tf_op jit(solution)/shard_map/ppermute | solution.py:743
  80.0 5.0 %collective-permute-start.22 = (bf16[112,512]{1,0:T(8,128)(2,1)S(1)}, bf16[112,512]{1,0:T(8,128)(2,1)S(1)}, u32[]{:S(2)}, u32[]{:S(2)}) collective-permute-start(bf16[112,512]{1,0:T(8,128)(2,1)S(1)} %pad_maximum_fusion.8), channel_id=1, source_target_pairs={{0,1},{1,0},{2,3},{3,2},{4,5},{5,4},{6,7},{7,6},{8,9},{9,8},{10,11... | collective-permute-start | bytes 344072 | tf_op jit(solution)/shard_map/ppermute | solution.py:743
  83.4 6.1 %collective-permute-start.7 = (bf16[224,512]{1,0:T(8,128)(2,1)S(1)}, bf16[224,512]{1,0:T(8,128)(2,1)S(1)}, u32[]{:S(2)}, u32[]{:S(2)}) collective-permute-start(bf16[224,512]{1,0:T(8,128)(2,1)S(1)} %pad_maximum_fusion.3), channel_id=1, source_target_pairs={{0,1},{1,0},{2,3},{3,2},{4,5},{5,4},{6,7},{7,6},{8,9},{9,8},{10,11... | collective-permute-start | bytes 688136 | tf_op jit(solution)/shard_map/ppermute | solution.py:743
  84.7 6.1 %collective-permute-start.15 = (bf16[224,512]{1,0:T(8,128)(2,1)S(1)}, bf16[224,512]{1,0:T(8,128)(2,1)S(1)}, u32[]{:S(2)}, u32[]{:S(2)}) collective-permute-start(bf16[224,512]{1,0:T(8,128)(2,1)S(1)} %pad_maximum_fusion.4), channel_id=1, source_target_pairs={{0,2},{1,3},{2,0},{3,1},{4,6},{5,7},{6,4},{7,5},{8,10},{9,11},{10,... | collective-permute-start | bytes 688136 | tf_op jit(solution)/shard_map/ppermute | solution.py:743
  85.1 6.3 %collective-permute-start.23 = (bf16[224,512]{1,0:T(8,128)(2,1)S(1)}, bf16[224,512]{1,0:T(8,128)(2,1)S(1)}, u32[]{:S(2)}, u32[]{:S(2)}) collective-permute-start(bf16[224,512]{1,0:T(8,128)(2,1)S(1)} %pad_maximum_fusion.5), channel_id=1, source_target_pairs={{0,4},{1,5},{2,6},{3,7},{4,0},{5,1},{6,2},{7,3},{8,12},{9,13},{10,... | collective-permute-start | bytes 688136 | tf_op jit(solution)/shard_map/ppermute | solution.py:743
  89.6 3.9 %collective-permute-start.24 = (bf16[448,512]{1,0:T(8,128)(2,1)S(1)}, bf16[448,512]{1,0:T(8,128)(2,1)S(1)}, u32[]{:S(2)}, u32[]{:S(2)}) collective-permute-start(bf16[448,512]{1,0:T(8,128)(2,1)S(1)} %pad_maximum_fusion.a0), channel_id=1, source_target_pairs={{0,16},{1,17},{2,18},{3,19},{4,20},{5,21},{6,22},{7,23},{8,24},{9,... | collective-permute-start | bytes 1376264 | tf_op jit(solution)/shard_map/ppermute | solution.py:743
  90.9 2.6 %collective-permute-start.25 = (bf16[448,512]{1,0:T(8,128)(2,1)S(1)}, bf16[448,512]{1,0:T(8,128)(2,1)S(1)}, u32[]{:S(2)}, u32[]{:S(2)}) collective-permute-start(bf16[448,512]{1,0:T(8,128)(2,1)S(1)} %pad_maximum_fusion.1.a1), channel_id=1, source_target_pairs={{0,16},{1,17},{2,18},{3,19},{4,20},{5,21},{6,22},{7,23},{8,24},{9,... | collective-permute-start | bytes 1376264 | tf_op jit(solution)/shard_map/ppermute | solution.py:743
  91.5 2.1 %collective-permute-start.26 = (bf16[448,512]{1,0:T(8,128)(2,1)S(1)}, bf16[448,512]{1,0:T(8,128)(2,1)S(1)}, u32[]{:S(2)}, u32[]{:S(2)}) collective-permute-start(bf16[448,512]{1,0:T(8,128)(2,1)S(1)} %pad_maximum_fusion.2.a2), channel_id=1, source_target_pairs={{0,16},{1,17},{2,18},{3,19},{4,20},{5,21},{6,22},{7,23},{8,24},{9,... | collective-permute-start | bytes 1376264 | tf_op jit(solution)/shard_map/ppermute | solution.py:743
